TPU v7x, 32 devices: a whole 2x2x4 slice. The times are simulated.
32 devices in a mesh: seq: 8 (over z, y), head: 4 (over x, core).
Axes of the slice: x: 2, y: 2, z: 4, core: 2. Of those that a mesh axis runs over, the one named last changes fastest.
Arguments:
- rotated_query_rows: bfloat16 [4096, 4096], P(('seq', 'head')), may hold values from -8 to 8
- rotated_key_rows: bfloat16 [4096, 2048], P(('seq', 'head')), may hold values from -8 to 8
- value_matrix: bfloat16 [4096, 2048], P(('seq', 'head')), may hold values from -6 to 6
- output_gradient: bfloat16 [4096, 4096], P(('seq', 'head')), may hold values from -6 to 6
- doc_lengths: int32 [8], replicated, may hold values from 1 to 2048, 4096 in all
Outputs:
- attended: bfloat16 [4096, 4096], P(('seq', 'head'))
- query_grad: bfloat16 [4096, 4096], P(('seq', 'head'))
- key_gradient: bfloat16 [4096, 2048], P(('seq', 'head'))
- value_gradient: bfloat16 [4096, 2048], P(('seq', 'head'))
Inputs may be any that keep to these rules, and one draw needn't show every extreme that they name: `doc_lengths`: the lengths of the 8 documents packed in order; they sum to 4096 and the longest has 2048 tokens.
All inputs are finite; a program needn't handle non-finite values.
Results may differ from a plain program's by a relative error of at most 0.02.
Values may be sent and summed in bfloat16 or wider, within the bound.
No kernel may reach another device: no remote copies, remote signals or barrier semaphores. Data moves between devices by JAX's collectives and lax.ppermute only.
A program may use at most 128 MiB of HBM per device.

v0:
```python
import functools

import jax
import jax.numpy as jnp
from jax import lax
from jax.experimental import pallas as pl
from jax.experimental.pallas import tpu as pltpu
from jax.sharding import Mesh
from jax.sharding import PartitionSpec as P

HEAD_WIDTH = 256
WINDOW_LENGTH = 1024
MEMBERS = 8
HALF = MEMBERS // 2
DISTANCES = (7, 6, 5, 4, 3, 2, 1, 0)
BACK_DISTANCES = (7, 6, 5, 4, 0, 1, 2, 3)

TILE = 256
TILES = WINDOW_LENGTH // TILE
SPAN = TILES + 1
KEYS = SPAN * TILE
ROWS = WINDOW_LENGTH // MEMBERS
CHUNKS = TILE // ROWS
COLUMNS = 2 * TILE
SCORE_SCALE = HEAD_WIDTH ** (-0.5)
LOG2_E = 1.4426950408889634

IN_HBM = pl.BlockSpec(memory_space=pltpu.HBM)
SCALARS = pl.BlockSpec(memory_space=pltpu.SMEM)
SMALL_LIMIT = pltpu.CompilerParams(vmem_limit_bytes=4 * 1024 * 1024)
WHOLE_LIMIT = pltpu.CompilerParams(vmem_limit_bytes=64 * 1024 * 1024)
LIMIT = pltpu.CompilerParams(vmem_limit_bytes=62 * 1024 * 1024)


def dot(left, right, contract):
    return lax.dot_general(
        left, right, ((contract[:1], contract[1:]), ((), ())), preferred_element_type=jnp.float32
    )


def copies_of(pairs, semaphores):
    return [
        pltpu.make_async_copy(source, target, semaphores.at[item])
        for item, (source, target) in enumerate(pairs)
    ]


def columns_of(ref, head, width):
    return ref.at[:, pl.ds(pl.multiple_of(head * width, width), width)]


def staged(arriving, leaving):
    for copies in arriving:
        for copy in copies:
            copy.start()
    for copies, onward in zip(arriving, leaving):
        for copy in copies:
            copy.wait()
        for copy in onward:
            copy.start()
    for onward in leaving:
        for copy in onward:
            copy.wait()


def pack_kernel(distances, left_ref, right_ref, *refs):
    pieces, (buffer, arrived, sent) = refs[:HALF], refs[HALF:]
    member = lax.axis_index("member")
    width = left_ref.shape[1] // MEMBERS
    arriving, leaving = [], []
    for item, distance in enumerate(distances):
        head = member ^ distance
        pairs = [
            (columns_of(left_ref, head, width), buffer.at[item, :, pl.ds(0, width)]),
            (columns_of(right_ref, head, width), buffer.at[item, :, pl.ds(width, width)]),
        ]
        arriving.append(copies_of(pairs, arrived.at[item]))
        leaving.append([pltpu.make_async_copy(buffer.at[item], pieces[item], sent.at[item])])
    staged(arriving, leaving)


def pack(left, right, distances):
    rows, columns = left.shape
    shape = (rows, 2 * columns // MEMBERS)
    return pl.pallas_call(
        functools.partial(pack_kernel, distances),
        in_specs=[IN_HBM] * 2,
        out_specs=[IN_HBM] * HALF,
        out_shape=[jax.ShapeDtypeStruct(shape, left.dtype)] * HALF,
        scratch_shapes=[
            pltpu.VMEM((HALF, *shape), left.dtype),
            pltpu.SemaphoreType.DMA((HALF, 2)),
            pltpu.SemaphoreType.DMA((HALF,)),
        ],
        compiler_params=WHOLE_LIMIT,
        cost_estimate=pl.CostEstimate(
            flops=0, bytes_accessed=4 * rows * columns, transcendentals=0
        ),
    )(left, right)


def unpack_kernel(*refs):
    pieces, (left_ref, right_ref, sent) = refs[:MEMBERS], refs[MEMBERS:]
    member = lax.axis_index("member")
    width = left_ref.shape[1] // MEMBERS
    copies = []
    for item, distance in enumerate(BACK_DISTANCES):
        head = member ^ distance
        pairs = [
            (pieces[item].at[:, pl.ds(0, width)], columns_of(left_ref, head, width)),
            (pieces[item].at[:, pl.ds(width, width)], columns_of(right_ref, head, width)),
        ]
        copies += copies_of(pairs, sent.at[item])
    for copy in copies:
        copy.start()
    for copy in copies:
        copy.wait()


def unpack(pieces):
    rows, columns = pieces[0].shape
    whole = jax.ShapeDtypeStruct((rows, MEMBERS * columns // 2), pieces[0].dtype)
    return pl.pallas_call(
        unpack_kernel,
        in_specs=[pl.BlockSpec(memory_space=pltpu.VMEM)] * MEMBERS,
        out_specs=[IN_HBM] * 2,
        out_shape=[whole] * 2,
        scratch_shapes=[pltpu.SemaphoreType.DMA((MEMBERS, 2))],
        compiler_params=SMALL_LIMIT,
        cost_estimate=pl.CostEstimate(
            flops=0, bytes_accessed=4 * MEMBERS * rows * columns, transcendentals=0
        ),
    )(*pieces)


def attention_kernel(lengths_ref, rows_ref, *refs):
    own_halves, earlier_halves, out_ref, refs = refs[:2], refs[2:4], refs[4], refs[5:]
    own_grads, earlier_grads, refs = refs[:2], refs[2:4], refs[4:]
    kv, kv_turned, sums, weights, grad_weights, refs = *refs[:5], refs[5:]
    scores = refs
    step = pl.program_id(0)
    width = HEAD_WIDTH
    member = lax.axis_index("member")

    def turn(tile):
        part = kv[pl.ds(tile * CHUNKS, CHUNKS)].reshape(TILE, 2 * width)
        kv_turned[:, pl.ds(pl.multiple_of(tile * TILE, TILE), TILE)] = part.T

    @pl.when(step == 0)
    def _():
        for item, distance in enumerate(DISTANCES):
            half, part, chunk = item // HALF, item % HALF, member ^ distance
            kv[chunk] = earlier_halves[half][part]
            kv[MEMBERS + chunk] = own_halves[half][part]
        sums[:MEMBERS] = jnp.zeros((MEMBERS, ROWS, 2 * width), jnp.float32)
        for tile in range(TILES):
            turn(tile)

    turn(TILES + step)

    def key_tile(item, first):
        tile = pl.ds((step + item) * CHUNKS, CHUNKS)
        return kv[tile, :, first : first + width].reshape(TILE, width)

    def turned_window(first):
        place = pl.ds(pl.multiple_of(step * TILE, TILE), KEYS)
        return kv_turned[first : first + width, place]

    def add(item, first, part):
        tile = pl.ds((step + item) * CHUNKS, CHUNKS)
        part = part.reshape(CHUNKS, ROWS, width)
        if item < TILES:
            part = sums[tile, :, first : first + width] + part
        sums[tile, :, first : first + width] = part

    queries = [rows_ref[:, head * width : (head + 1) * width] for head in range(2)]
    cotangents = [rows_ref[:, (2 + head) * width : (3 + head) * width] for head in range(2)]
    queries_turned = [part.T for part in queries]
    cotangents_turned = [part.T for part in cotangents]
    columns = [slice(head * TILE, (head + 1) * TILE) for head in range(2)]
    tiles = [slice(item * TILE, (item + 1) * TILE) for item in range(SPAN)]

    first_row = lax.axis_index("stretch") * WINDOW_LENGTH + step * TILE
    row = lax.broadcasted_iota(jnp.int32, (1, TILE), 1)
    oldest = row - (WINDOW_LENGTH - 1)

    def passed(item, carried):
        begin, oldest = carried
        near = begin - first_row
        oldest = jnp.where(near <= row, jnp.maximum(oldest, near), oldest)
        return begin + lengths_ref[item], oldest

    _, oldest = lax.fori_loop(0, lengths_ref.shape[0], passed, (jnp.int32(0), oldest))
    key_row = lax.broadcasted_iota(jnp.int32, (TILE, TILE), 0)

    tops = [jnp.full((1, TILE), -jnp.inf, jnp.float32)] * 2
    totals = [jnp.zeros((1, TILE), jnp.float32)] * 2

    def score(head, item):
        part = dot(key_tile(item, 0), queries_turned[head], (1, 0))
        seen = key_row >= oldest - (item - TILES) * TILE
        if item == TILES:
            seen = seen & (key_row <= row)
        part = jnp.where(seen, part, -jnp.inf)
        tops[head] = jnp.maximum(tops[head], jnp.max(part, axis=0, keepdims=True))
        scores[head][item] = part

    def weigh(head, item):
        part = jnp.exp2((scores[head][item] - tops[head]) * (SCORE_SCALE * LOG2_E))
        totals[head] = totals[head] + jnp.sum(part, axis=0, keepdims=True)
        weights[tiles[item], columns[head]] = part.astype(jnp.bfloat16)

    def put(head, first, part):
        place = slice((first + head) * width, (first + head + 1) * width)
        out_ref[:, place] = part.astype(jnp.bfloat16).T

    def attend(head, share):
        attended = dot(turned_window(width), weights[:, columns[head]], (1, 0))
        attended = (attended * share).astype(jnp.bfloat16)
        put(head, 0, attended)
        products = attended.astype(jnp.float32) * cotangents_turned[head].astype(jnp.float32)
        return jnp.sum(products, axis=0, keepdims=True)

    def weigh_grad(head, item, row_delta):
        grad = dot(key_tile(item, width), cotangents_turned[head], (1, 0)) - row_delta
        part = weights[tiles[item], columns[head]].astype(jnp.float32)
        part = (part * grad).astype(jnp.bfloat16)
        grad_weights[tiles[item], columns[head]] = part

    def make_query_grad(head, share):
        query_grad = dot(turned_window(0), grad_weights[:, columns[head]], (1, 0))
        put(head, 2, query_grad * (share * SCORE_SCALE))

    def scaled(parts, shares):
        scaled_parts = []
        for part, share in zip(parts, shares):
            down = jnp.broadcast_to(share, (8, TILE)).T[:, :1]
            scaled_parts.append((part.astype(jnp.float32) * down).astype(jnp.bfloat16))
        return jnp.concatenate(scaled_parts, axis=0)

    for item in range(SPAN):
        score(0, item)
    for item in range(SPAN):
        score(1, item)
        weigh(0, item)
    shares = [1.0 / totals[0]]
    deltas = [attend(0, shares[0])]
    for item in range(SPAN):
        weigh(1, item)
    shares.append(1.0 / totals[1])
    deltas.append(attend(1, shares[1]))
    cotangents_scaled = scaled(cotangents, shares)
    queries_scaled = scaled(queries, shares)
    for item in range(SPAN):
        weigh_grad(0, item, deltas[0])
        weigh_grad(1, item, deltas[1])
        add(item, width, dot(weights[tiles[item]], cotangents_scaled, (1, 0)))
        add(item, 0, dot(grad_weights[tiles[item]], queries_scaled, (1, 0)))
    make_query_grad(0, shares[0])
    make_query_grad(1, shares[1])

    @pl.when(step == TILES - 1)
    def _():
        for item, distance in enumerate(BACK_DISTANCES):
            half, part, chunk = item // HALF, item % HALF, member ^ distance
            for halves, place in ((earlier_grads, chunk), (own_grads, MEMBERS + chunk)):
                target = halves[half]
                target[part, :, :width] = (sums[place, :, :width] * SCORE_SCALE).astype(
                    jnp.bfloat16
                )
                target[part, :, width:] = sums[place, :, width:].astype(jnp.bfloat16)


def attention(doc_lengths, rows, own, earlier):
    width = HEAD_WIDTH
    products = 6 * 2 * WINDOW_LENGTH * 2 * KEYS * width
    half = jax.ShapeDtypeStruct((HALF, ROWS, 2 * width), jnp.bfloat16)
    rows_block = pl.BlockSpec((TILE, 4 * width), lambda i: (i, 0))
    half_block = pl.BlockSpec(half.shape, lambda i: (0, 0, 0))
    outputs = pl.pallas_call(
        attention_kernel,
        grid=(TILES,),
        in_specs=[SCALARS, rows_block] + [half_block] * 4,
        out_specs=[rows_block] + [half_block] * 4,
        out_shape=[jax.ShapeDtypeStruct(rows.shape, jnp.bfloat16)] + [half] * 4,
        scratch_shapes=[
            pltpu.VMEM((2 * MEMBERS, ROWS, 2 * width), jnp.bfloat16),
            pltpu.VMEM((2 * width, 2 * WINDOW_LENGTH), jnp.bfloat16),
            pltpu.VMEM((2 * MEMBERS, ROWS, 2 * width), jnp.float32),
            pltpu.VMEM((KEYS, COLUMNS), jnp.bfloat16),
            pltpu.VMEM((KEYS, COLUMNS), jnp.bfloat16),
        ]
        + [pltpu.VMEM((SPAN, TILE, TILE), jnp.float32)] * 2,
        compiler_params=LIMIT,
        cost_estimate=pl.CostEstimate(
            flops=2 * products, bytes_accessed=WINDOW_LENGTH * width * 30, transcendentals=0
        ),
    )(doc_lengths, rows, *own, *earlier)
    return outputs[0], outputs[1:3], outputs[3:]


def by_head(block):
    return block.reshape(ROWS, MEMBERS, block.shape[1] // MEMBERS).transpose(1, 0, 2)


def by_token(blocks):
    return blocks.transpose(1, 0, 2).reshape(ROWS, MEMBERS * blocks.shape[2])


def exchanged(blocks):
    return lax.all_to_all(blocks, "member", split_axis=0, concat_axis=0, tiled=True)


def swapped(pieces, distances):
    moved = []
    for piece, distance in zip(pieces, distances):
        route = [(i, i ^ distance) for i in range(MEMBERS)]
        moved.append(lax.ppermute(piece, "member", route) if distance else piece)
    return moved


def onward(block, direction):
    lower = [(i, i + 1) for i in range(lax.axis_size("stretch") - 1)]
    route = lower if direction > 0 else [(j, i) for i, j in lower]
    return lax.ppermute(block, "stretch", route)


def shards(rotated_query_rows, rotated_key_rows, value_matrix, output_gradient, doc_lengths):
    heavy, light = DISTANCES[:HALF], DISTANCES[HALF:]
    pieces = pack(rotated_key_rows, value_matrix, heavy)
    pieces, rotated_key_rows, value_matrix = lax.optimization_barrier(
        (pieces, rotated_key_rows, value_matrix)
    )
    pieces = swapped(pieces, heavy)
    pieces += swapped(pack(rotated_key_rows, value_matrix, light), light)
    rows = jnp.concatenate([by_head(rotated_query_rows), by_head(output_gradient)], axis=2)
    pieces, rows = lax.optimization_barrier((pieces, rows))
    own = [jnp.stack(pieces[:HALF]), jnp.stack(pieces[HALF:])]
    earlier = [onward(half, 1) for half in own]
    rows = exchanged(rows).reshape(WINDOW_LENGTH, 4 * HEAD_WIDTH)
    results, own_grads, earlier_grads = attention(doc_lengths, rows, own, earlier)
    later = [onward(half, -1) for half in earlier_grads]
    results = exchanged(results.reshape(MEMBERS, ROWS, 4 * HEAD_WIDTH))
    attended = by_token(results[:, :, : 2 * HEAD_WIDTH])
    query_grad = by_token(results[:, :, 2 * HEAD_WIDTH :])
    sums = [
        (own_grads[half].astype(jnp.float32) + later[half].astype(jnp.float32)).astype(
            jnp.bfloat16
        )
        for half in range(2)
    ]
    pieces = [sums[item // HALF][item % HALF] for item in range(MEMBERS)]
    pieces = swapped(pieces, BACK_DISTANCES)
    attended, query_grad, pieces = lax.optimization_barrier((attended, query_grad, pieces))
    return (attended, query_grad, *unpack(pieces))


def solution(mesh):
    grouped = Mesh(mesh.devices.reshape(-1, MEMBERS), ("stretch", "member"))
    spread = P(("stretch", "member"), None)
    return jax.shard_map(
        shards,
        mesh=grouped,
        in_specs=(spread, spread, spread, spread, P()),
        out_specs=(spread, spread, spread, spread),
        check_vma=False,
    )
```

profile of v0, /device:TPU:0, one launch (start us, length us, event | category | flops | bytes accessed | tf_op | source)
XLA Modules:
  0.0 113.5 jit_solution(16548120330110969072)
XLA Ops:
  0.6 1.8 %shard_map.84 = (bf16[128,512]{1,0:T(8,128)(2,1)}, bf16[128,512]{1,0:T(8,128)(2,1)}, bf16[128,512]{1,0:T(8,128)(2,1)}, bf16[128,512]{1,0:T(8,128)(2,1)}) custom-call(bf16[128,2048]{1,0:T(8,128)(2,1)} %left_ref.2, bf16[128,2048]{1,0:T(8,128)(2,1)} %right_ref.2), custom_call_target="tpu_custom_call" | custom-call | bytes 1048576 | tf_op jit(solution)/shard_map/pallas_call | solution.py:85
  2.5 3.4 %collective-permute-start = (bf16[128,512]{1,0:T(8,128)(2,1)}, bf16[128,512]{1,0:T(8,128)(2,1)}, u32[]{:S(2)}, u32[]{:S(2)}) collective-permute-start(bf16[128,512]{1,0:T(8,128)(2,1)} %get-tuple-element.48), channel_id=1, source_target_pairs={{0,7},{1,6},{2,5},{3,4},{4,3},{5,2},{6,1},{7,0},{8,15},{9,14},{10,... | collective-permute-start | bytes 393224 | tf_op jit(solution)/shard_map/ppermute | solution.py:318
  6.5 1.4 %collective-permute-start.2 = (bf16[128,512]{1,0:T(8,128)(2,1)}, bf16[128,512]{1,0:T(8,128)(2,1)}, u32[]{:S(2)}, u32[]{:S(2)}) collective-permute-start(bf16[128,512]{1,0:T(8,128)(2,1)} %get-tuple-element.50), channel_id=1, source_target_pairs={{0,5},{1,4},{2,7},{3,6},{4,1},{5,0},{6,3},{7,2},{8,13},{9,12},{10,... | collective-permute-start | bytes 393224 | tf_op jit(solution)/shard_map/ppermute | solution.py:318
  8.2 1.8 %shard_map.85 = (bf16[128,512]{1,0:T(8,128)(2,1)}, bf16[128,512]{1,0:T(8,128)(2,1)}, bf16[128,512]{1,0:T(8,128)(2,1)}, bf16[128,512]{1,0:T(8,128)(2,1)}) custom-call(bf16[128,2048]{1,0:T(8,128)(2,1)} %left_ref.2, bf16[128,2048]{1,0:T(8,128)(2,1)} %right_ref.2), custom_call_target="tpu_custom_call" | custom-call | bytes 1048576 | tf_op jit(solution)/shard_map/pallas_call | solution.py:85
  10.0 1.2 %collective-permute-start.4 = (bf16[128,512]{1,0:T(8,128)(2,1)}, bf16[128,512]{1,0:T(8,128)(2,1)S(1)}, u32[]{:S(2)}, u32[]{:S(2)}) collective-permute-start(bf16[128,512]{1,0:T(8,128)(2,1)} %get-tuple-element.54), channel_id=1, source_target_pairs={{0,3},{1,2},{2,1},{3,0},{4,7},{5,6},{6,5},{7,4},{8,11},{9,10},{10,... | collective-permute-start | bytes 393224 | tf_op jit(solution)/shard_map/ppermute | solution.py:318
  11.2 1.8 %bitcast_bitcast_fusion = (bf16[8,128,512]{2,1,0:T(8,128)(2,1)S(1)}, bf16[8,128,512]{2,1,0:T(8,128)(2,1)S(1)}) fusion(bf16[16,8,8,512]{3,2,1,0:T(8,128)(2,1)} %bitcast.47, bf16[16,8,8,512]{3,2,1,0:T(8,128)(2,1)} %bitcast.48), kind=kLoop, calls=%fused_computation.1 | loop fusion | bytes 4194304 | tf_op jit(solution)/shard_map/transpose | solution.py:303
  13.9 1.6 %pad_maximum_fusion = bf16[8,128,1024]{2,1,0:T(8,128)(2,1)} fusion(bf16[8,128,512]{2,1,0:T(8,128)(2,1)S(1)} %get-tuple-element.94, bf16[8,128,512]{2,1,0:T(8,128)(2,1)S(1)} %get-tuple-element.95), kind=kLoop, calls=%fused_computation | loop fusion | flops 4194304 | bytes 4194304 | tf_op jit(solution)/shard_map/concatenate | solution.py:336
  15.8 2.8 %collective-permute-done.3 = bf16[128,512]{1,0:T(8,128)(2,1)} collective-permute-done((bf16[128,512]{1,0:T(8,128)(2,1)}, bf16[128,512]{1,0:T(8,128)(2,1)}, u32[]{:S(2)}, u32[]{:S(2)}) %collective-permute-start.3) | collective-permute-done | bytes 131104 | tf_op jit(solution)/shard_map/ppermute | solution.py:318
  19.4 4.5 %all-to-all-start = ((bf16[8,128,1024]{2,1,0:T(8,128)(2,1)}), bf16[8,128,1024]{2,1,0:T(8,128)(2,1)}, u32[]{:S(2)}, u32[]{:S(2)}) async-start(bf16[8,128,1024]{2,1,0:T(8,128)(2,1)} %pad_maximum_fusion), calls=%async_computation | async-start | bytes 4194304 | tf_op jit(solution)/shard_map/all_to_all | solution.py:311
  24.0 3.6 %collective-permute-start.8 = (bf16[4,128,512]{2,1,0:T(8,128)(2,1)S(1)}, bf16[4,128,512]{2,1,0:T(8,128)(2,1)S(1)}, u32[]{:S(2)}, u32[]{:S(2)}) collective-permute-start(bf16[4,128,512]{2,1,0:T(8,128)(2,1)S(1)} %pad_maximum_fusion.2.refs_1_), channel_id=1, source_target_pairs={{0,8},{8,16},{16,24},{1,9},{9,17},{17,25},{2,10},{10,18},{18,26},{... | collective-permute-start | bytes 1572872 | tf_op jit(solution)/shard_map/ppermute | solution.py:325
  27.6 1.2 %pad_maximum_fusion.1.refs_0_ = bf16[4,128,512]{2,1,0:T(8,128)(2,1)S(1)} fusion(bf16[1,128,512]{2,1,0:T(8,128)(2,1)} %bitcast.6, bf16[1,128,512]{2,1,0:T(8,128)(2,1)} %bitcast.5, bf16[1,128,512]{2,1,0:T(8,128)(2,1)} %bitcast.4, bf16[1,128,512]{2,1,0:T(8,128)(2,1)} %bitcast.3), kind=kLoop, calls=%fused_computation.7 | loop fusion | flops 786432 | bytes 1048576 | tf_op jit(solution)/shard_map/stack | solution.py:338
  28.8 4.3 %collective-permute-start.7 = (bf16[4,128,512]{2,1,0:T(8,128)(2,1)S(1)}, bf16[4,128,512]{2,1,0:T(8,128)(2,1)}, u32[]{:S(2)}, u32[]{:S(2)}) collective-permute-start(bf16[4,128,512]{2,1,0:T(8,128)(2,1)S(1)} %pad_maximum_fusion.1.refs_0_), channel_id=1, source_target_pairs={{0,8},{8,16},{16,24},{1,9},{9,17},{17,25},{2,10},{10,18},{18,26},{... | collective-permute-start | bytes 1572872 | tf_op jit(solution)/shard_map/ppermute | solution.py:325
  33.0 6.8 %collective-permute-done.8.refs_3_ = bf16[4,128,512]{2,1,0:T(8,128)(2,1)S(1)} collective-permute-done((bf16[4,128,512]{2,1,0:T(8,128)(2,1)S(1)}, bf16[4,128,512]{2,1,0:T(8,128)(2,1)S(1)}, u32[]{:S(2)}, u32[]{:S(2)}) %collective-permute-start.8) | collective-permute-done | bytes 524320 | tf_op jit(solution)/shard_map/ppermute | solution.py:325
  39.8 10.7 %collective-permute-done.7.refs_2_ = bf16[4,128,512]{2,1,0:T(8,128)(2,1)} collective-permute-done((bf16[4,128,512]{2,1,0:T(8,128)(2,1)S(1)}, bf16[4,128,512]{2,1,0:T(8,128)(2,1)}, u32[]{:S(2)}, u32[]{:S(2)}) %collective-permute-start.7) | collective-permute-done | bytes 524320 | tf_op jit(solution)/shard_map/ppermute | solution.py:325
  50.6 17.7 %shard_map.86 = (bf16[1024,1024]{1,0:T(8,128)(2,1)}, bf16[4,128,512]{2,1,0:T(8,128)(2,1)}, bf16[4,128,512]{2,1,0:T(8,128)(2,1)}, bf16[4,128,512]{2,1,0:T(8,128)(2,1)}, bf16[4,128,512]{2,1,0:T(8,128)(2,1)}) custom-call(s32[8]{0:T(128)} %lengths_ref.1, bf16[1024,1024]{1,0:T(8,128)(2,1)} %bitcast.2.rows_ref, bf16[4,128,512]{2,1,0:T(8,128)(2,1)} %copy-done.3, ...), custom_call_target="tpu_custom_call" | custom-call | flops 16106127360 | bytes 7864320 | tf_op jit(solution)/shard_map/pallas_call | solution.py:280
  68.3 3.9 %all-to-all-start.1 = ((bf16[8,128,1024]{2,1,0:T(8,128)(2,1)}), bf16[8,128,1024]{2,1,0:T(8,128)(2,1)S(1)}, u32[]{:S(2)}, u32[]{:S(2)}) async-start(bf16[8,128,1024]{2,1,0:T(8,128)(2,1)} %bitcast.44), calls=%async_computation.1 | async-start | bytes 4194304 | tf_op jit(solution)/shard_map/all_to_all | solution.py:311
  72.3 1.4 %collective-permute-start.9 = (bf16[4,128,512]{2,1,0:T(8,128)(2,1)S(1)}, bf16[4,128,512]{2,1,0:T(8,128)(2,1)S(1)}, u32[]{:S(2)}, u32[]{:S(2)}) collective-permute-start(bf16[4,128,512]{2,1,0:T(8,128)(2,1)S(1)} %copy-done.6), channel_id=1, source_target_pairs={{8,0},{16,8},{24,16},{9,1},{17,9},{25,17},{10,2},{18,10},{26,18},{... | collective-permute-start | bytes 1572872 | tf_op jit(solution)/shard_map/ppermute | solution.py:325
  73.7 1.3 %collective-permute-start.14 = (bf16[4,128,512]{2,1,0:T(8,128)(2,1)}, bf16[4,128,512]{2,1,0:T(8,128)(2,1)S(1)}, u32[]{:S(2)}, u32[]{:S(2)}) collective-permute-start(bf16[4,128,512]{2,1,0:T(8,128)(2,1)} %get-tuple-element.71), channel_id=1, source_target_pairs={{8,0},{16,8},{24,16},{9,1},{17,9},{25,17},{10,2},{18,10},{26,18},{... | collective-permute-start | bytes 1572872 | tf_op jit(solution)/shard_map/ppermute | solution.py:325
  75.0 14.7 %collective-permute-done.9 = bf16[4,128,512]{2,1,0:T(8,128)(2,1)S(1)} collective-permute-done((bf16[4,128,512]{2,1,0:T(8,128)(2,1)S(1)}, bf16[4,128,512]{2,1,0:T(8,128)(2,1)S(1)}, u32[]{:S(2)}, u32[]{:S(2)}) %collective-permute-start.9) | collective-permute-done | bytes 524320 | tf_op jit(solution)/shard_map/ppermute | solution.py:325
  89.9 2.0 %collective-permute-start.13 = (bf16[128,512]{1,0:T(8,128)(2,1)S(1)}, bf16[128,512]{1,0:T(8,128)(2,1)S(1)}, u32[]{:S(2)}, u32[]{:S(2)}) collective-permute-start(bf16[128,512]{1,0:T(8,128)(2,1)S(1)} %get-tuple-element.90), channel_id=1, source_target_pairs={{0,4},{1,5},{2,6},{3,7},{4,0},{5,1},{6,2},{7,3},{8,12},{9,13},{10,... | collective-permute-start | bytes 393224 | tf_op jit(solution)/shard_map/ppermute | solution.py:318
  91.9 1.5 %collective-permute-start.11 = (bf16[128,512]{1,0:T(8,128)(2,1)S(1)}, bf16[128,512]{1,0:T(8,128)(2,1)S(1)}, u32[]{:S(2)}, u32[]{:S(2)}) collective-permute-start(bf16[128,512]{1,0:T(8,128)(2,1)S(1)} %get-tuple-element.92), channel_id=1, source_target_pairs={{0,6},{1,7},{2,4},{3,5},{4,2},{5,3},{6,0},{7,1},{8,14},{9,15},{10,... | collective-permute-start | bytes 393224 | tf_op jit(solution)/shard_map/ppermute | solution.py:318
  93.3 1.2 %collective-permute-start.10 = (bf16[128,512]{1,0:T(8,128)(2,1)S(1)}, bf16[128,512]{1,0:T(8,128)(2,1)S(1)}, u32[]{:S(2)}, u32[]{:S(2)}) collective-permute-start(bf16[128,512]{1,0:T(8,128)(2,1)S(1)} %get-tuple-element.93), channel_id=1, source_target_pairs={{0,7},{1,6},{2,5},{3,4},{4,3},{5,2},{6,1},{7,0},{8,15},{9,14},{10,... | collective-permute-start | bytes 393224 | tf_op jit(solution)/shard_map/ppermute | solution.py:318
  94.5 6.2 %collective-permute-done.14 = bf16[4,128,512]{2,1,0:T(8,128)(2,1)S(1)} collective-permute-done((bf16[4,128,512]{2,1,0:T(8,128)(2,1)}, bf16[4,128,512]{2,1,0:T(8,128)(2,1)S(1)}, u32[]{:S(2)}, u32[]{:S(2)}) %collective-permute-start.14) | collective-permute-done | bytes 524320 | tf_op jit(solution)/shard_map/ppermute | solution.py:325
  102.5 4.7 %collective-permute-done.13.refs_3_ = bf16[128,512]{1,0:T(8,128)(2,1)S(1)} collective-permute-done((bf16[128,512]{1,0:T(8,128)(2,1)S(1)}, bf16[128,512]{1,0:T(8,128)(2,1)S(1)}, u32[]{:S(2)}, u32[]{:S(2)}) %collective-permute-start.13) | collective-permute-done | bytes 131104 | tf_op jit(solution)/shard_map/ppermute | solution.py:318
  (49 shorter events, 11.3 us)
Async XLA Ops:
  2.5 10.5 %collective-permute-start = (bf16[128,512]{1,0:T(8,128)(2,1)}, bf16[128,512]{1,0:T(8,128)(2,1)}, u32[]{:S(2)}, u32[]{:S(2)}) collective-permute-start(bf16[128,512]{1,0:T(8,128)(2,1)} %get-tuple-element.48), channel_id=1, source_target_pairs={{0,7},{1,6},{2,5},{3,4},{4,3},{5,2},{6,1},{7,0},{8,15},{9,14},{10,... | collective-permute-start | bytes 393224 | tf_op jit(solution)/shard_map/ppermute | solution.py:318
  5.9 7.9 %collective-permute-start.1 = (bf16[128,512]{1,0:T(8,128)(2,1)}, bf16[128,512]{1,0:T(8,128)(2,1)}, u32[]{:S(2)}, u32[]{:S(2)}) collective-permute-start(bf16[128,512]{1,0:T(8,128)(2,1)} %get-tuple-element.49), channel_id=1, source_target_pairs={{0,6},{1,7},{2,4},{3,5},{4,2},{5,3},{6,0},{7,1},{8,14},{9,15},{10,... | collective-permute-start | bytes 393224 | tf_op jit(solution)/shard_map/ppermute | solution.py:318
  6.5 9.3 %collective-permute-start.2 = (bf16[128,512]{1,0:T(8,128)(2,1)}, bf16[128,512]{1,0:T(8,128)(2,1)}, u32[]{:S(2)}, u32[]{:S(2)}) collective-permute-start(bf16[128,512]{1,0:T(8,128)(2,1)} %get-tuple-element.50), channel_id=1, source_target_pairs={{0,5},{1,4},{2,7},{3,6},{4,1},{5,0},{6,3},{7,2},{8,13},{9,12},{10,... | collective-permute-start | bytes 393224 | tf_op jit(solution)/shard_map/ppermute | solution.py:318
  7.9 10.8 %collective-permute-start.3 = (bf16[128,512]{1,0:T(8,128)(2,1)}, bf16[128,512]{1,0:T(8,128)(2,1)}, u32[]{:S(2)}, u32[]{:S(2)}) collective-permute-start(bf16[128,512]{1,0:T(8,128)(2,1)} %get-tuple-element.51), channel_id=1, source_target_pairs={{0,4},{1,5},{2,6},{3,7},{4,0},{5,1},{6,2},{7,3},{8,12},{9,13},{10,... | collective-permute-start | bytes 393224 | tf_op jit(solution)/shard_map/ppermute | solution.py:318
  10.0 8.7 %collective-permute-start.4 = (bf16[128,512]{1,0:T(8,128)(2,1)}, bf16[128,512]{1,0:T(8,128)(2,1)S(1)}, u32[]{:S(2)}, u32[]{:S(2)}) collective-permute-start(bf16[128,512]{1,0:T(8,128)(2,1)} %get-tuple-element.54), channel_id=1, source_target_pairs={{0,3},{1,2},{2,1},{3,0},{4,7},{5,6},{6,5},{7,4},{8,11},{9,10},{10,... | collective-permute-start | bytes 393224 | tf_op jit(solution)/shard_map/ppermute | solution.py:318
  13.0 6.4 %collective-permute-start.5 = (bf16[128,512]{1,0:T(8,128)(2,1)S(1)}, bf16[128,512]{1,0:T(8,128)(2,1)S(1)}, u32[]{:S(2)}, u32[]{:S(2)}) collective-permute-start(bf16[128,512]{1,0:T(8,128)(2,1)S(1)} %copy-done.8), channel_id=1, source_target_pairs={{0,2},{1,3},{2,0},{3,1},{4,6},{5,7},{6,4},{7,5},{8,10},{9,11},{10,... | collective-permute-start | bytes 393224 | tf_op jit(solution)/shard_map/ppermute | solution.py:318
  13.8 5.6 %collective-permute-start.6 = (bf16[128,512]{1,0:T(8,128)(2,1)S(1)}, bf16[128,512]{1,0:T(8,128)(2,1)S(1)}, u32[]{:S(2)}, u32[]{:S(2)}) collective-permute-start(bf16[128,512]{1,0:T(8,128)(2,1)S(1)} %copy-done.7), channel_id=1, source_target_pairs={{0,1},{1,0},{2,3},{3,2},{4,5},{5,4},{6,7},{7,6},{8,9},{9,8},{10,11... | collective-permute-start | bytes 393224 | tf_op jit(solution)/shard_map/ppermute | solution.py:318
  19.4 31.1 %all-to-all-start = ((bf16[8,128,1024]{2,1,0:T(8,128)(2,1)}), bf16[8,128,1024]{2,1,0:T(8,128)(2,1)}, u32[]{:S(2)}, u32[]{:S(2)}) async-start(bf16[8,128,1024]{2,1,0:T(8,128)(2,1)} %pad_maximum_fusion), calls=%async_computation | async-start | bytes 4194304 | tf_op jit(solution)/shard_map/all_to_all | solution.py:311
  24.0 26.6 %copy-start.2 = (bf16[4,128,512]{2,1,0:T(8,128)(2,1)}, bf16[4,128,512]{2,1,0:T(8,128)(2,1)S(1)}, u32[]{:S(2)}) copy-start(bf16[4,128,512]{2,1,0:T(8,128)(2,1)S(1)} %pad_maximum_fusion.2.refs_1_) | copy-start | bytes 1572868
  24.0 15.8 %collective-permute-start.8 = (bf16[4,128,512]{2,1,0:T(8,128)(2,1)S(1)}, bf16[4,128,512]{2,1,0:T(8,128)(2,1)S(1)}, u32[]{:S(2)}, u32[]{:S(2)}) collective-permute-start(bf16[4,128,512]{2,1,0:T(8,128)(2,1)S(1)} %pad_maximum_fusion.2.refs_1_), channel_id=1, source_target_pairs={{0,8},{8,16},{16,24},{1,9},{9,17},{17,25},{2,10},{10,18},{18,26},{... | collective-permute-start | bytes 1572872 | tf_op jit(solution)/shard_map/ppermute | solution.py:325
  28.8 21.8 %copy-start.3 = (bf16[4,128,512]{2,1,0:T(8,128)(2,1)}, bf16[4,128,512]{2,1,0:T(8,128)(2,1)S(1)}, u32[]{:S(2)}) copy-start(bf16[4,128,512]{2,1,0:T(8,128)(2,1)S(1)} %pad_maximum_fusion.1.refs_0_) | copy-start | bytes 1572868
  28.8 21.7 %collective-permute-start.7 = (bf16[4,128,512]{2,1,0:T(8,128)(2,1)S(1)}, bf16[4,128,512]{2,1,0:T(8,128)(2,1)}, u32[]{:S(2)}, u32[]{:S(2)}) collective-permute-start(bf16[4,128,512]{2,1,0:T(8,128)(2,1)S(1)} %pad_maximum_fusion.1.refs_0_), channel_id=1, source_target_pairs={{0,8},{8,16},{16,24},{1,9},{9,17},{17,25},{2,10},{10,18},{18,26},{... | collective-permute-start | bytes 1572872 | tf_op jit(solution)/shard_map/ppermute | solution.py:325
  68.3 21.3 %copy-start.1 = (bf16[4,128,512]{2,1,0:T(8,128)(2,1)S(1)}, bf16[4,128,512]{2,1,0:T(8,128)(2,1)}, u32[]{:S(2)}) copy-start(bf16[4,128,512]{2,1,0:T(8,128)(2,1)} %get-tuple-element.68) | copy-start | bytes 1572868
  68.3 40.7 %all-to-all-start.1 = ((bf16[8,128,1024]{2,1,0:T(8,128)(2,1)}), bf16[8,128,1024]{2,1,0:T(8,128)(2,1)S(1)}, u32[]{:S(2)}, u32[]{:S(2)}) async-start(bf16[8,128,1024]{2,1,0:T(8,128)(2,1)} %bitcast.44), calls=%async_computation.1 | async-start | bytes 4194304 | tf_op jit(solution)/shard_map/all_to_all | solution.py:311
  72.3 28.5 %copy-start = (bf16[4,128,512]{2,1,0:T(8,128)(2,1)S(1)}, bf16[4,128,512]{2,1,0:T(8,128)(2,1)}, u32[]{:S(2)}) copy-start(bf16[4,128,512]{2,1,0:T(8,128)(2,1)} %get-tuple-element.70) | copy-start | bytes 1572868
  72.3 17.4 %collective-permute-start.9 = (bf16[4,128,512]{2,1,0:T(8,128)(2,1)S(1)}, bf16[4,128,512]{2,1,0:T(8,128)(2,1)S(1)}, u32[]{:S(2)}, u32[]{:S(2)}) collective-permute-start(bf16[4,128,512]{2,1,0:T(8,128)(2,1)S(1)} %copy-done.6), channel_id=1, source_target_pairs={{8,0},{16,8},{24,16},{9,1},{17,9},{25,17},{10,2},{18,10},{26,18},{... | collective-permute-start | bytes 1572872 | tf_op jit(solution)/shard_map/ppermute | solution.py:325
  73.7 27.0 %collective-permute-start.14 = (bf16[4,128,512]{2,1,0:T(8,128)(2,1)}, bf16[4,128,512]{2,1,0:T(8,128)(2,1)S(1)}, u32[]{:S(2)}, u32[]{:S(2)}) collective-permute-start(bf16[4,128,512]{2,1,0:T(8,128)(2,1)} %get-tuple-element.71), channel_id=1, source_target_pairs={{8,0},{16,8},{24,16},{9,1},{17,9},{25,17},{10,2},{18,10},{26,18},{... | collective-permute-start | bytes 1572872 | tf_op jit(solution)/shard_map/ppermute | solution.py:325
  89.9 17.4 %collective-permute-start.13 = (bf16[128,512]{1,0:T(8,128)(2,1)S(1)}, bf16[128,512]{1,0:T(8,128)(2,1)S(1)}, u32[]{:S(2)}, u32[]{:S(2)}) collective-permute-start(bf16[128,512]{1,0:T(8,128)(2,1)S(1)} %get-tuple-element.90), channel_id=1, source_target_pairs={{0,4},{1,5},{2,6},{3,7},{4,0},{5,1},{6,2},{7,3},{8,12},{9,13},{10,... | collective-permute-start | bytes 393224 | tf_op jit(solution)/shard_map/ppermute | solution.py:318
  91.9 16.5 %collective-permute-start.12 = (bf16[128,512]{1,0:T(8,128)(2,1)S(1)}, bf16[128,512]{1,0:T(8,128)(2,1)S(1)}, u32[]{:S(2)}, u32[]{:S(2)}) collective-permute-start(bf16[128,512]{1,0:T(8,128)(2,1)S(1)} %get-tuple-element.91), channel_id=1, source_target_pairs={{0,5},{1,4},{2,7},{3,6},{4,1},{5,0},{6,3},{7,2},{8,13},{9,12},{10,... | collective-permute-start | bytes 393224 | tf_op jit(solution)/shard_map/ppermute | solution.py:318
  91.9 19.6 %collective-permute-start.11 = (bf16[128,512]{1,0:T(8,128)(2,1)S(1)}, bf16[128,512]{1,0:T(8,128)(2,1)S(1)}, u32[]{:S(2)}, u32[]{:S(2)}) collective-permute-start(bf16[128,512]{1,0:T(8,128)(2,1)S(1)} %get-tuple-element.92), channel_id=1, source_target_pairs={{0,6},{1,7},{2,4},{3,5},{4,2},{5,3},{6,0},{7,1},{8,14},{9,15},{10,... | collective-permute-start | bytes 393224 | tf_op jit(solution)/shard_map/ppermute | solution.py:318
  93.3 18.1 %collective-permute-start.10 = (bf16[128,512]{1,0:T(8,128)(2,1)S(1)}, bf16[128,512]{1,0:T(8,128)(2,1)S(1)}, u32[]{:S(2)}, u32[]{:S(2)}) collective-permute-start(bf16[128,512]{1,0:T(8,128)(2,1)S(1)} %get-tuple-element.93), channel_id=1, source_target_pairs={{0,7},{1,6},{2,5},{3,4},{4,3},{5,2},{6,1},{7,0},{8,15},{9,14},{10,... | collective-permute-start | bytes 393224 | tf_op jit(solution)/shard_map/ppermute | solution.py:318
  101.6 9.8 %collective-permute-start.17 = (bf16[128,512]{1,0:T(8,128)(2,1)}, bf16[128,512]{1,0:T(8,128)(2,1)S(1)}, u32[]{:S(2)}, u32[]{:S(2)}) collective-permute-start(bf16[128,512]{1,0:T(8,128)(2,1)} %get-tuple-element.86), channel_id=1, source_target_pairs={{0,3},{1,2},{2,1},{3,0},{4,7},{5,6},{6,5},{7,4},{8,11},{9,10},{10,... | collective-permute-start | bytes 393224 | tf_op jit(solution)/shard_map/ppermute | solution.py:318
  107.2 5.2 %collective-permute-start.16 = (bf16[128,512]{1,0:T(8,128)(2,1)}, bf16[128,512]{1,0:T(8,128)(2,1)S(1)}, u32[]{:S(2)}, u32[]{:S(2)}) collective-permute-start(bf16[128,512]{1,0:T(8,128)(2,1)} %get-tuple-element.87), channel_id=1, source_target_pairs={{0,2},{1,3},{2,0},{3,1},{4,6},{5,7},{6,4},{7,5},{8,10},{9,11},{10,... | collective-permute-start | bytes 393224 | tf_op jit(solution)/shard_map/ppermute | solution.py:318
  108.3 4.1 %collective-permute-start.15 = (bf16[128,512]{1,0:T(8,128)(2,1)S(1)}, bf16[128,512]{1,0:T(8,128)(2,1)S(1)}, u32[]{:S(2)}, u32[]{:S(2)}) collective-permute-start(bf16[128,512]{1,0:T(8,128)(2,1)S(1)} %get-tuple-element.88), channel_id=1, source_target_pairs={{0,1},{1,0},{2,3},{3,2},{4,5},{5,4},{6,7},{7,6},{8,9},{9,8},{10,11... | collective-permute-start | bytes 393224 | tf_op jit(solution)/shard_map/ppermute | solution.py:318
  (5 other events, 23.6 us)
where the time goes:
time: 114 us; the launch traced here: 113 us
  waiting for transfers between devices  48.4 us (42%)
  starting transfers between devices  33.6 us (29%)
  Pallas kernels  22.5 us (20%)
  local copies, waits for them, and re-layouts  5.01 us (4%)
  other arithmetic  3.1 us (3%)
    ppermute x4, waiting for transfers between devices, onward(): return lax.ppermute(block, 'stretch', route)  38.3 us
    pallas_call x1, Pallas kernels, attention(): pl.pallas_call(attention_kernel, grid=(TILES,), in_specs=[SCALARS, rows_b...  17.7 us
    ppermute x14, starting transfers between devices, swapped(): moved.append(lax.ppermute(piece, 'member', route) if distance else piece)  14.7 us
    ppermute x4, starting transfers between devices, onward(): return lax.ppermute(block, 'stretch', route)  10.5 us
    ppermute x14, waiting for transfers between devices, swapped(): moved.append(lax.ppermute(piece, 'member', route) if distance else piece)  10.1 us
    all_to_all x2, starting transfers between devices, exchanged(): lax.all_to_all(blocks, 'member', split_axis=0, concat_axis=0, tiled=True)  8.4 us
    pallas_call x2, Pallas kernels, pack(): pl.pallas_call(functools.partial(pack_kernel, distances), in_specs=[IN_HB...  3.67 us
  transfers between devices with their start and end apart: 20, of which 11 were waited for; matrix products, arithmetic and copies ran while one was open for 7% of the time, Pallas kernels for 2%

commit v1 on v0

--- a/solution.py
+++ b/solution.py
@@ -12,7 +12,7 @@
 WINDOW_LENGTH = 1024
 MEMBERS = 8
 HALF = MEMBERS // 2
-DISTANCES = (7, 6, 5, 4, 3, 2, 1, 0)
+GROUPS = ((7, 6, 5, 4), (3, 2), (1, 0))
 BACK_DISTANCES = (7, 6, 5, 4, 0, 1, 2, 3)
 
 TILE = 256
@@ -134,7 +134,7 @@
 
 
 def attention_kernel(lengths_ref, rows_ref, *refs):
-    own_halves, earlier_halves, out_ref, refs = refs[:2], refs[2:4], refs[4], refs[5:]
+    own_parts, earlier_parts, out_ref, refs = refs[:3], refs[3:6], refs[6], refs[7:]
     own_grads, earlier_grads, refs = refs[:2], refs[2:4], refs[4:]
     kv, kv_turned, sums, weights, grad_weights, refs = *refs[:5], refs[5:]
     scores = refs
@@ -148,10 +148,11 @@
 
     @pl.when(step == 0)
     def _():
-        for item, distance in enumerate(DISTANCES):
-            half, part, chunk = item // HALF, item % HALF, member ^ distance
-            kv[chunk] = earlier_halves[half][part]
-            kv[MEMBERS + chunk] = own_halves[half][part]
+        for group, distances in enumerate(GROUPS):
+            for part, distance in enumerate(distances):
+                chunk = member ^ distance
+                kv[chunk] = earlier_parts[group][part]
+                kv[MEMBERS + chunk] = own_parts[group][part]
         sums[:MEMBERS] = jnp.zeros((MEMBERS, ROWS, 2 * width), jnp.float32)
         for tile in range(TILES):
             turn(tile)
@@ -277,10 +278,13 @@
     half = jax.ShapeDtypeStruct((HALF, ROWS, 2 * width), jnp.bfloat16)
     rows_block = pl.BlockSpec((TILE, 4 * width), lambda i: (i, 0))
     half_block = pl.BlockSpec(half.shape, lambda i: (0, 0, 0))
+    group_blocks = [
+        pl.BlockSpec((len(group), ROWS, 2 * width), lambda i: (0, 0, 0)) for group in GROUPS
+    ]
     outputs = pl.pallas_call(
         attention_kernel,
         grid=(TILES,),
-        in_specs=[SCALARS, rows_block] + [half_block] * 4,
+        in_specs=[SCALARS, rows_block] + group_blocks * 2,
         out_specs=[rows_block] + [half_block] * 4,
         out_shape=[jax.ShapeDtypeStruct(rows.shape, jnp.bfloat16)] + [half] * 4,
         scratch_shapes=[
@@ -326,17 +330,20 @@
 
 
 def shards(rotated_query_rows, rotated_key_rows, value_matrix, output_gradient, doc_lengths):
-    heavy, light = DISTANCES[:HALF], DISTANCES[HALF:]
+    heavy, light = GROUPS[0], GROUPS[1] + GROUPS[2]
     pieces = pack(rotated_key_rows, value_matrix, heavy)
     pieces, rotated_key_rows, value_matrix = lax.optimization_barrier(
         (pieces, rotated_key_rows, value_matrix)
     )
     pieces = swapped(pieces, heavy)
     pieces += swapped(pack(rotated_key_rows, value_matrix, light), light)
+    near = jnp.stack(pieces[6:])
+    earlier_near = onward(near, 1)
     rows = jnp.concatenate([by_head(rotated_query_rows), by_head(output_gradient)], axis=2)
-    pieces, rows = lax.optimization_barrier((pieces, rows))
-    own = [jnp.stack(pieces[:HALF]), jnp.stack(pieces[HALF:])]
-    earlier = [onward(half, 1) for half in own]
+    pieces, earlier_near, rows = lax.optimization_barrier((pieces[:6], earlier_near, rows))
+    own = [jnp.stack(pieces[:4]), jnp.stack(pieces[4:])]
+    earlier = [onward(part, 1) for part in own] + [earlier_near]
+    own.append(near)
     rows = exchanged(rows).reshape(WINDOW_LENGTH, 4 * HEAD_WIDTH)
     results, own_grads, earlier_grads = attention(doc_lengths, rows, own, earlier)
     later = [onward(half, -1) for half in earlier_grads]

time: 114 us -> 119 us (1.044)
  waiting for transfers between devices: 48.4 us -> 51.8 us
  starting transfers between devices: 33.6 us -> 35.8 us
    all_to_all x2, waiting for transfers between devices: 0.11 us -> 5.76 us  [exchanged(): lax.all_to_all(blocks, 'member', split_axis=0, concat_axis=0, tiled=True)]
    ppermute x4 -> x5, waiting for transfers between devices: 38.3 us -> 33.6 us  [onward(): return lax.ppermute(block, 'stretch', route)]
    ppermute x4 -> x5, starting transfers between devices: 10.5 us -> 13.2 us  [onward(): return lax.ppermute(block, 'stretch', route)]
    ppermute x14, waiting for transfers between devices: 10.1 us -> 12.4 us  [swapped(): moved.append(lax.ppermute(piece, 'member', route) if distance else piece)]
  transfers between devices with their start and end apart: 20 -> 21, of which waited for: 11 -> 10; matrix products, arithmetic and copies ran while one was open for 7% -> 7% of each run, Pallas kernels for 2% -> 0%
where the time goes in v1:
time: 119 us
  waiting for transfers between devices  51.8 us (44%)
  starting transfers between devices  35.8 us (30%)
  Pallas kernels  22.5 us (19%)
  local copies, waits for them, and re-layouts  5.02 us (4%)
  other arithmetic  2.9 us (2%)
    ppermute x5, waiting for transfers between devices, onward(): return lax.ppermute(block, 'stretch', route)  33.6 us
    pallas_call x1, Pallas kernels, attention(): pl.pallas_call(attention_kernel, grid=(TILES,), in_specs=[SCALARS, rows_b...  17.7 us
    ppermute x14, starting transfers between devices, swapped(): moved.append(lax.ppermute(piece, 'member', route) if distance else piece)  14.5 us
    ppermute x5, starting transfers between devices, onward(): return lax.ppermute(block, 'stretch', route)  13.2 us
    ppermute x14, waiting for transfers between devices, swapped(): moved.append(lax.ppermute(piece, 'member', route) if distance else piece)  12.4 us
    all_to_all x2, starting transfers between devices, exchanged(): lax.all_to_all(blocks, 'member', split_axis=0, concat_axis=0, tiled=True)  8.1 us
    all_to_all x2, waiting for transfers between devices, exchanged(): lax.all_to_all(blocks, 'member', split_axis=0, concat_axis=0, tiled=True)  5.76 us
    pallas_call x2, Pallas kernels, pack(): pl.pallas_call(functools.partial(pack_kernel, distances), in_specs=[IN_HB...  3.66 us
  transfers between devices with their start and end apart: 21, of which 10 were waited for; matrix products, arithmetic and copies ran while one was open for 7% of the time, Pallas kernels for 0%

profile of v1, /device:TPU:0, one launch (start us, length us, event | category | flops | bytes accessed | tf_op | source)
XLA Modules:
  0.0 118.9 jit_solution(7526863348763218057)
XLA Ops:
  0.6 1.8 %shard_map.84 = (bf16[128,512]{1,0:T(8,128)(2,1)}, bf16[128,512]{1,0:T(8,128)(2,1)}, bf16[128,512]{1,0:T(8,128)(2,1)}, bf16[128,512]{1,0:T(8,128)(2,1)}) custom-call(bf16[128,2048]{1,0:T(8,128)(2,1)} %left_ref.2, bf16[128,2048]{1,0:T(8,128)(2,1)} %right_ref.2), custom_call_target="tpu_custom_call" | custom-call | bytes 1048576 | tf_op jit(solution)/shard_map/pallas_call | solution.py:85
  2.5 1.8 %shard_map.85 = (bf16[128,512]{1,0:T(8,128)(2,1)}, bf16[128,512]{1,0:T(8,128)(2,1)}, bf16[128,512]{1,0:T(8,128)(2,1)}, bf16[128,512]{1,0:T(8,128)(2,1)}) custom-call(bf16[128,2048]{1,0:T(8,128)(2,1)} %left_ref.2, bf16[128,2048]{1,0:T(8,128)(2,1)} %right_ref.2), custom_call_target="tpu_custom_call" | custom-call | bytes 1048576 | tf_op jit(solution)/shard_map/pallas_call | solution.py:85
  4.8 3.6 %collective-permute-start = (bf16[128,512]{1,0:T(8,128)(2,1)}, bf16[128,512]{1,0:T(8,128)(2,1)S(1)}, u32[]{:S(2)}, u32[]{:S(2)}) collective-permute-start(bf16[128,512]{1,0:T(8,128)(2,1)} %get-tuple-element.47), channel_id=1, source_target_pairs={{0,7},{1,6},{2,5},{3,4},{4,3},{5,2},{6,1},{7,0},{8,15},{9,14},{10,... | collective-permute-start | bytes 393224 | tf_op jit(solution)/shard_map/ppermute | solution.py:322
  8.4 1.3 %collective-permute-start.2 = (bf16[128,512]{1,0:T(8,128)(2,1)}, bf16[128,512]{1,0:T(8,128)(2,1)S(1)}, u32[]{:S(2)}, u32[]{:S(2)}) collective-permute-start(bf16[128,512]{1,0:T(8,128)(2,1)} %get-tuple-element.49), channel_id=1, source_target_pairs={{0,5},{1,4},{2,7},{3,6},{4,1},{5,0},{6,3},{7,2},{8,13},{9,12},{10,... | collective-permute-start | bytes 393224 | tf_op jit(solution)/shard_map/ppermute | solution.py:322
  11.4 3.5 %collective-permute-start.7 = (bf16[2,128,512]{2,1,0:T(8,128)(2,1)S(1)}, bf16[2,128,512]{2,1,0:T(8,128)(2,1)S(1)}, u32[]{:S(2)}, u32[]{:S(2)}) collective-permute-start(bf16[2,128,512]{2,1,0:T(8,128)(2,1)S(1)} %pad_maximum_fusion.2.refs_2_), channel_id=1, source_target_pairs={{0,8},{8,16},{16,24},{1,9},{9,17},{17,25},{2,10},{10,18},{18,26},{... | collective-permute-start | bytes 786440 | tf_op jit(solution)/shard_map/ppermute | solution.py:329
  14.9 1.8 %bitcast_bitcast_fusion = (bf16[8,128,512]{2,1,0:T(8,128)(2,1)S(1)}, bf16[8,128,512]{2,1,0:T(8,128)(2,1)S(1)}) fusion(bf16[16,8,8,512]{3,2,1,0:T(8,128)(2,1)} %bitcast.47, bf16[16,8,8,512]{3,2,1,0:T(8,128)(2,1)} %bitcast.48), kind=kLoop, calls=%fused_computation.1 | loop fusion | bytes 4194304 | tf_op jit(solution)/shard_map/transpose | solution.py:307
  18.5 1.6 %pad_maximum_fusion = bf16[8,128,1024]{2,1,0:T(8,128)(2,1)} fusion(bf16[8,128,512]{2,1,0:T(8,128)(2,1)S(1)} %get-tuple-element.92, bf16[8,128,512]{2,1,0:T(8,128)(2,1)S(1)} %get-tuple-element.93), kind=kLoop, calls=%fused_computation | loop fusion | flops 4194304 | bytes 4194304 | tf_op jit(solution)/shard_map/concatenate | solution.py:342
  21.1 1.3 %collective-permute-done.4 = bf16[128,512]{1,0:T(8,128)(2,1)S(1)} collective-permute-done((bf16[128,512]{1,0:T(8,128)(2,1)S(1)}, bf16[128,512]{1,0:T(8,128)(2,1)S(1)}, u32[]{:S(2)}, u32[]{:S(2)}) %collective-permute-start.4) | collective-permute-done | bytes 131104 | tf_op jit(solution)/shard_map/ppermute | solution.py:322
  22.4 3.0 %collective-permute-done.5 = bf16[128,512]{1,0:T(8,128)(2,1)S(1)} collective-permute-done((bf16[128,512]{1,0:T(8,128)(2,1)S(1)}, bf16[128,512]{1,0:T(8,128)(2,1)S(1)}, u32[]{:S(2)}, u32[]{:S(2)}) %collective-permute-start.5) | collective-permute-done | bytes 131104 | tf_op jit(solution)/shard_map/ppermute | solution.py:322
  25.4 4.4 %all-to-all-start = ((bf16[8,128,1024]{2,1,0:T(8,128)(2,1)}), bf16[8,128,1024]{2,1,0:T(8,128)(2,1)}, u32[]{:S(2)}, u32[]{:S(2)}) async-start(bf16[8,128,1024]{2,1,0:T(8,128)(2,1)} %pad_maximum_fusion), calls=%async_computation | async-start | bytes 4194304 | tf_op jit(solution)/shard_map/all_to_all | solution.py:315
  29.9 3.5 %collective-permute-start.8 = (bf16[4,128,512]{2,1,0:T(8,128)(2,1)S(1)}, bf16[4,128,512]{2,1,0:T(8,128)(2,1)S(1)}, u32[]{:S(2)}, u32[]{:S(2)}) collective-permute-start(bf16[4,128,512]{2,1,0:T(8,128)(2,1)S(1)} %pad_maximum_fusion.1.refs_0_), channel_id=1, source_target_pairs={{0,8},{8,16},{16,24},{1,9},{9,17},{17,25},{2,10},{10,18},{18,26},{... | collective-permute-start | bytes 1572872 | tf_op jit(solution)/shard_map/ppermute | solution.py:329
  33.4 3.5 %collective-permute-start.9 = (bf16[2,128,512]{2,1,0:T(8,128)(2,1)S(1)}, bf16[2,128,512]{2,1,0:T(8,128)(2,1)S(1)}, u32[]{:S(2)}, u32[]{:S(2)}) collective-permute-start(bf16[2,128,512]{2,1,0:T(8,128)(2,1)S(1)} %pad_maximum_fusion.3.refs_1_), channel_id=1, source_target_pairs={{0,8},{8,16},{16,24},{1,9},{9,17},{17,25},{2,10},{10,18},{18,26},{... | collective-permute-start | bytes 786440 | tf_op jit(solution)/shard_map/ppermute | solution.py:329
  36.9 13.7 %collective-permute-done.9.refs_4_ = bf16[2,128,512]{2,1,0:T(8,128)(2,1)S(1)} collective-permute-done((bf16[2,128,512]{2,1,0:T(8,128)(2,1)S(1)}, bf16[2,128,512]{2,1,0:T(8,128)(2,1)S(1)}, u32[]{:S(2)}, u32[]{:S(2)}) %collective-permute-start.9) | collective-permute-done | bytes 262176 | tf_op jit(solution)/shard_map/ppermute | solution.py:329
  50.7 5.8 %all-to-all-done = bf16[8,128,1024]{2,1,0:T(8,128)(2,1)} async-done(((bf16[8,128,1024]{2,1,0:T(8,128)(2,1)}), bf16[8,128,1024]{2,1,0:T(8,128)(2,1)}, u32[]{:S(2)}, u32[]{:S(2)}) %all-to-all-start) | async-done | bytes 2097184 | tf_op jit(solution)/shard_map/all_to_all | solution.py:315
  56.4 17.7 %shard_map.86 = (bf16[1024,1024]{1,0:T(8,128)(2,1)}, bf16[4,128,512]{2,1,0:T(8,128)(2,1)}, bf16[4,128,512]{2,1,0:T(8,128)(2,1)}, bf16[4,128,512]{2,1,0:T(8,128)(2,1)}, bf16[4,128,512]{2,1,0:T(8,128)(2,1)}) custom-call(s32[8]{0:T(128)} %lengths_ref.1, bf16[1024,1024]{1,0:T(8,128)(2,1)} %bitcast.4.rows_ref, bf16[4,128,512]{2,1,0:T(8,128)(2,1)} %copy-done.2, ...), custom_call_target="tpu_custom_call" | custom-call | flops 16106127360 | bytes 7864320 | tf_op jit(solution)/shard_map/pallas_call | solution.py:284
  74.2 3.7 %all-to-all-start.1 = ((bf16[8,128,1024]{2,1,0:T(8,128)(2,1)}), bf16[8,128,1024]{2,1,0:T(8,128)(2,1)S(1)}, u32[]{:S(2)}, u32[]{:S(2)}) async-start(bf16[8,128,1024]{2,1,0:T(8,128)(2,1)} %bitcast.44), calls=%async_computation.1 | async-start | bytes 4194304 | tf_op jit(solution)/shard_map/all_to_all | solution.py:315
  78.0 1.4 %collective-permute-start.10 = (bf16[4,128,512]{2,1,0:T(8,128)(2,1)S(1)}, bf16[4,128,512]{2,1,0:T(8,128)(2,1)S(1)}, u32[]{:S(2)}, u32[]{:S(2)}) collective-permute-start(bf16[4,128,512]{2,1,0:T(8,128)(2,1)S(1)} %copy-done.6), channel_id=1, source_target_pairs={{8,0},{16,8},{24,16},{9,1},{17,9},{25,17},{10,2},{18,10},{26,18},{... | collective-permute-start | bytes 1572872 | tf_op jit(solution)/shard_map/ppermute | solution.py:329
  79.4 1.3 %collective-permute-start.15 = (bf16[4,128,512]{2,1,0:T(8,128)(2,1)}, bf16[4,128,512]{2,1,0:T(8,128)(2,1)S(1)}, u32[]{:S(2)}, u32[]{:S(2)}) collective-permute-start(bf16[4,128,512]{2,1,0:T(8,128)(2,1)} %get-tuple-element.69), channel_id=1, source_target_pairs={{8,0},{16,8},{24,16},{9,1},{17,9},{25,17},{10,2},{18,10},{26,18},{... | collective-permute-start | bytes 1572872 | tf_op jit(solution)/shard_map/ppermute | solution.py:329
  80.7 14.1 %collective-permute-done.10 = bf16[4,128,512]{2,1,0:T(8,128)(2,1)S(1)} collective-permute-done((bf16[4,128,512]{2,1,0:T(8,128)(2,1)S(1)}, bf16[4,128,512]{2,1,0:T(8,128)(2,1)S(1)}, u32[]{:S(2)}, u32[]{:S(2)}) %collective-permute-start.10) | collective-permute-done | bytes 524320 | tf_op jit(solution)/shard_map/ppermute | solution.py:329
  94.9 2.0 %collective-permute-start.14 = (bf16[128,512]{1,0:T(8,128)(2,1)S(1)}, bf16[128,512]{1,0:T(8,128)(2,1)S(1)}, u32[]{:S(2)}, u32[]{:S(2)}) collective-permute-start(bf16[128,512]{1,0:T(8,128)(2,1)S(1)} %get-tuple-element.88), channel_id=1, source_target_pairs={{0,4},{1,5},{2,6},{3,7},{4,0},{5,1},{6,2},{7,3},{8,12},{9,13},{10,... | collective-permute-start | bytes 393224 | tf_op jit(solution)/shard_map/ppermute | solution.py:322
  96.9 1.4 %collective-permute-start.12 = (bf16[128,512]{1,0:T(8,128)(2,1)S(1)}, bf16[128,512]{1,0:T(8,128)(2,1)S(1)}, u32[]{:S(2)}, u32[]{:S(2)}) collective-permute-start(bf16[128,512]{1,0:T(8,128)(2,1)S(1)} %get-tuple-element.90), channel_id=1, source_target_pairs={{0,6},{1,7},{2,4},{3,5},{4,2},{5,3},{6,0},{7,1},{8,14},{9,15},{10,... | collective-permute-start | bytes 393224 | tf_op jit(solution)/shard_map/ppermute | solution.py:322
  98.4 1.2 %collective-permute-start.11 = (bf16[128,512]{1,0:T(8,128)(2,1)S(1)}, bf16[128,512]{1,0:T(8,128)(2,1)S(1)}, u32[]{:S(2)}, u32[]{:S(2)}) collective-permute-start(bf16[128,512]{1,0:T(8,128)(2,1)S(1)} %get-tuple-element.91), channel_id=1, source_target_pairs={{0,7},{1,6},{2,5},{3,4},{4,3},{5,2},{6,1},{7,0},{8,15},{9,14},{10,... | collective-permute-start | bytes 393224 | tf_op jit(solution)/shard_map/ppermute | solution.py:322
  99.6 5.8 %collective-permute-done.15 = bf16[4,128,512]{2,1,0:T(8,128)(2,1)S(1)} collective-permute-done((bf16[4,128,512]{2,1,0:T(8,128)(2,1)}, bf16[4,128,512]{2,1,0:T(8,128)(2,1)S(1)}, u32[]{:S(2)}, u32[]{:S(2)}) %collective-permute-start.15) | collective-permute-done | bytes 524320 | tf_op jit(solution)/shard_map/ppermute | solution.py:329
  106.9 5.7 %collective-permute-done.14.refs_3_ = bf16[128,512]{1,0:T(8,128)(2,1)S(1)} collective-permute-done((bf16[128,512]{1,0:T(8,128)(2,1)S(1)}, bf16[128,512]{1,0:T(8,128)(2,1)S(1)}, u32[]{:S(2)}, u32[]{:S(2)}) %collective-permute-start.14) | collective-permute-done | bytes 131104 | tf_op jit(solution)/shard_map/ppermute | solution.py:322
  (56 shorter events, 12.9 us)
Async XLA Ops:
  4.3 6.1 %collective-permute-start.6 = (bf16[128,512]{1,0:T(8,128)(2,1)}, bf16[128,512]{1,0:T(8,128)(2,1)S(1)}, u32[]{:S(2)}, u32[]{:S(2)}) collective-permute-start(bf16[128,512]{1,0:T(8,128)(2,1)} %get-tuple-element.55), channel_id=1, source_target_pairs={{0,1},{1,0},{2,3},{3,2},{4,5},{5,4},{6,7},{7,6},{8,9},{9,8},{10,11... | collective-permute-start | bytes 393224 | tf_op jit(solution)/shard_map/ppermute | solution.py:322
  4.8 11.9 %collective-permute-start = (bf16[128,512]{1,0:T(8,128)(2,1)}, bf16[128,512]{1,0:T(8,128)(2,1)S(1)}, u32[]{:S(2)}, u32[]{:S(2)}) collective-permute-start(bf16[128,512]{1,0:T(8,128)(2,1)} %get-tuple-element.47), channel_id=1, source_target_pairs={{0,7},{1,6},{2,5},{3,4},{4,3},{5,2},{6,1},{7,0},{8,15},{9,14},{10,... | collective-permute-start | bytes 393224 | tf_op jit(solution)/shard_map/ppermute | solution.py:322
  8.4 9.5 %collective-permute-start.1 = (bf16[128,512]{1,0:T(8,128)(2,1)}, bf16[128,512]{1,0:T(8,128)(2,1)S(1)}, u32[]{:S(2)}, u32[]{:S(2)}) collective-permute-start(bf16[128,512]{1,0:T(8,128)(2,1)} %get-tuple-element.48), channel_id=1, source_target_pairs={{0,6},{1,7},{2,4},{3,5},{4,2},{5,3},{6,0},{7,1},{8,14},{9,15},{10,... | collective-permute-start | bytes 393224 | tf_op jit(solution)/shard_map/ppermute | solution.py:322
  8.4 11.6 %collective-permute-start.2 = (bf16[128,512]{1,0:T(8,128)(2,1)}, bf16[128,512]{1,0:T(8,128)(2,1)S(1)}, u32[]{:S(2)}, u32[]{:S(2)}) collective-permute-start(bf16[128,512]{1,0:T(8,128)(2,1)} %get-tuple-element.49), channel_id=1, source_target_pairs={{0,5},{1,4},{2,7},{3,6},{4,1},{5,0},{6,3},{7,2},{8,13},{9,12},{10,... | collective-permute-start | bytes 393224 | tf_op jit(solution)/shard_map/ppermute | solution.py:322
  9.8 11.3 %collective-permute-start.3 = (bf16[128,512]{1,0:T(8,128)(2,1)}, bf16[128,512]{1,0:T(8,128)(2,1)S(1)}, u32[]{:S(2)}, u32[]{:S(2)}) collective-permute-start(bf16[128,512]{1,0:T(8,128)(2,1)} %get-tuple-element.50), channel_id=1, source_target_pairs={{0,4},{1,5},{2,6},{3,7},{4,0},{5,1},{6,2},{7,3},{8,12},{9,13},{10,... | collective-permute-start | bytes 393224 | tf_op jit(solution)/shard_map/ppermute | solution.py:322
  11.4 14.0 %collective-permute-start.7 = (bf16[2,128,512]{2,1,0:T(8,128)(2,1)S(1)}, bf16[2,128,512]{2,1,0:T(8,128)(2,1)S(1)}, u32[]{:S(2)}, u32[]{:S(2)}) collective-permute-start(bf16[2,128,512]{2,1,0:T(8,128)(2,1)S(1)} %pad_maximum_fusion.2.refs_2_), channel_id=1, source_target_pairs={{0,8},{8,16},{16,24},{1,9},{9,17},{17,25},{2,10},{10,18},{18,26},{... | collective-permute-start | bytes 786440 | tf_op jit(solution)/shard_map/ppermute | solution.py:329
  16.7 5.7 %collective-permute-start.4 = (bf16[128,512]{1,0:T(8,128)(2,1)S(1)}, bf16[128,512]{1,0:T(8,128)(2,1)S(1)}, u32[]{:S(2)}, u32[]{:S(2)}) collective-permute-start(bf16[128,512]{1,0:T(8,128)(2,1)S(1)} %copy-done.10), channel_id=1, source_target_pairs={{0,3},{1,2},{2,1},{3,0},{4,7},{5,6},{6,5},{7,4},{8,11},{9,10},{10,... | collective-permute-start | bytes 393224 | tf_op jit(solution)/shard_map/ppermute | solution.py:322
  17.9 7.5 %collective-permute-start.5 = (bf16[128,512]{1,0:T(8,128)(2,1)S(1)}, bf16[128,512]{1,0:T(8,128)(2,1)S(1)}, u32[]{:S(2)}, u32[]{:S(2)}) collective-permute-start(bf16[128,512]{1,0:T(8,128)(2,1)S(1)} %copy-done.9), channel_id=1, source_target_pairs={{0,2},{1,3},{2,0},{3,1},{4,6},{5,7},{6,4},{7,5},{8,10},{9,11},{10,... | collective-permute-start | bytes 393224 | tf_op jit(solution)/shard_map/ppermute | solution.py:322
  25.4 31.0 %all-to-all-start = ((bf16[8,128,1024]{2,1,0:T(8,128)(2,1)}), bf16[8,128,1024]{2,1,0:T(8,128)(2,1)}, u32[]{:S(2)}, u32[]{:S(2)}) async-start(bf16[8,128,1024]{2,1,0:T(8,128)(2,1)} %pad_maximum_fusion), calls=%async_computation | async-start | bytes 4194304 | tf_op jit(solution)/shard_map/all_to_all | solution.py:315
  29.8 26.6 %copy-start.2 = (bf16[4,128,512]{2,1,0:T(8,128)(2,1)}, bf16[4,128,512]{2,1,0:T(8,128)(2,1)S(1)}, u32[]{:S(2)}) copy-start(bf16[4,128,512]{2,1,0:T(8,128)(2,1)S(1)} %pad_maximum_fusion.1.refs_0_) | copy-start | bytes 1572868
  29.9 20.8 %collective-permute-start.8 = (bf16[4,128,512]{2,1,0:T(8,128)(2,1)S(1)}, bf16[4,128,512]{2,1,0:T(8,128)(2,1)S(1)}, u32[]{:S(2)}, u32[]{:S(2)}) collective-permute-start(bf16[4,128,512]{2,1,0:T(8,128)(2,1)S(1)} %pad_maximum_fusion.1.refs_0_), channel_id=1, source_target_pairs={{0,8},{8,16},{16,24},{1,9},{9,17},{17,25},{2,10},{10,18},{18,26},{... | collective-permute-start | bytes 1572872 | tf_op jit(solution)/shard_map/ppermute | solution.py:329
  33.4 23.0 %copy-start.4 = (bf16[2,128,512]{2,1,0:T(8,128)(2,1)}, bf16[2,128,512]{2,1,0:T(8,128)(2,1)S(1)}, u32[]{:S(2)}) copy-start(bf16[2,128,512]{2,1,0:T(8,128)(2,1)S(1)} %pad_maximum_fusion.3.refs_1_) | copy-start | bytes 786436
  33.4 17.2 %collective-permute-start.9 = (bf16[2,128,512]{2,1,0:T(8,128)(2,1)S(1)}, bf16[2,128,512]{2,1,0:T(8,128)(2,1)S(1)}, u32[]{:S(2)}, u32[]{:S(2)}) collective-permute-start(bf16[2,128,512]{2,1,0:T(8,128)(2,1)S(1)} %pad_maximum_fusion.3.refs_1_), channel_id=1, source_target_pairs={{0,8},{8,16},{16,24},{1,9},{9,17},{17,25},{2,10},{10,18},{18,26},{... | collective-permute-start | bytes 786440 | tf_op jit(solution)/shard_map/ppermute | solution.py:329
  74.2 40.4 %all-to-all-start.1 = ((bf16[8,128,1024]{2,1,0:T(8,128)(2,1)}), bf16[8,128,1024]{2,1,0:T(8,128)(2,1)S(1)}, u32[]{:S(2)}, u32[]{:S(2)}) async-start(bf16[8,128,1024]{2,1,0:T(8,128)(2,1)} %bitcast.44), calls=%async_computation.1 | async-start | bytes 4194304 | tf_op jit(solution)/shard_map/all_to_all | solution.py:315
  77.9 27.5 %copy-start = (bf16[4,128,512]{2,1,0:T(8,128)(2,1)S(1)}, bf16[4,128,512]{2,1,0:T(8,128)(2,1)}, u32[]{:S(2)}) copy-start(bf16[4,128,512]{2,1,0:T(8,128)(2,1)} %get-tuple-element.68) | copy-start | bytes 1572868
  78.0 16.8 %collective-permute-start.10 = (bf16[4,128,512]{2,1,0:T(8,128)(2,1)S(1)}, bf16[4,128,512]{2,1,0:T(8,128)(2,1)S(1)}, u32[]{:S(2)}, u32[]{:S(2)}) collective-permute-start(bf16[4,128,512]{2,1,0:T(8,128)(2,1)S(1)} %copy-done.6), channel_id=1, source_target_pairs={{8,0},{16,8},{24,16},{9,1},{17,9},{25,17},{10,2},{18,10},{26,18},{... | collective-permute-start | bytes 1572872 | tf_op jit(solution)/shard_map/ppermute | solution.py:329
  79.4 26.0 %collective-permute-start.15 = (bf16[4,128,512]{2,1,0:T(8,128)(2,1)}, bf16[4,128,512]{2,1,0:T(8,128)(2,1)S(1)}, u32[]{:S(2)}, u32[]{:S(2)}) collective-permute-start(bf16[4,128,512]{2,1,0:T(8,128)(2,1)} %get-tuple-element.69), channel_id=1, source_target_pairs={{8,0},{16,8},{24,16},{9,1},{17,9},{25,17},{10,2},{18,10},{26,18},{... | collective-permute-start | bytes 1572872 | tf_op jit(solution)/shard_map/ppermute | solution.py:329
  94.9 17.7 %collective-permute-start.14 = (bf16[128,512]{1,0:T(8,128)(2,1)S(1)}, bf16[128,512]{1,0:T(8,128)(2,1)S(1)}, u32[]{:S(2)}, u32[]{:S(2)}) collective-permute-start(bf16[128,512]{1,0:T(8,128)(2,1)S(1)} %get-tuple-element.88), channel_id=1, source_target_pairs={{0,4},{1,5},{2,6},{3,7},{4,0},{5,1},{6,2},{7,3},{8,12},{9,13},{10,... | collective-permute-start | bytes 393224 | tf_op jit(solution)/shard_map/ppermute | solution.py:322
  96.9 17.2 %collective-permute-start.13 = (bf16[128,512]{1,0:T(8,128)(2,1)S(1)}, bf16[128,512]{1,0:T(8,128)(2,1)S(1)}, u32[]{:S(2)}, u32[]{:S(2)}) collective-permute-start(bf16[128,512]{1,0:T(8,128)(2,1)S(1)} %get-tuple-element.89), channel_id=1, source_target_pairs={{0,5},{1,4},{2,7},{3,6},{4,1},{5,0},{6,3},{7,2},{8,13},{9,12},{10,... | collective-permute-start | bytes 393224 | tf_op jit(solution)/shard_map/ppermute | solution.py:322
  96.9 20.1 %collective-permute-start.12 = (bf16[128,512]{1,0:T(8,128)(2,1)S(1)}, bf16[128,512]{1,0:T(8,128)(2,1)S(1)}, u32[]{:S(2)}, u32[]{:S(2)}) collective-permute-start(bf16[128,512]{1,0:T(8,128)(2,1)S(1)} %get-tuple-element.90), channel_id=1, source_target_pairs={{0,6},{1,7},{2,4},{3,5},{4,2},{5,3},{6,0},{7,1},{8,14},{9,15},{10,... | collective-permute-start | bytes 393224 | tf_op jit(solution)/shard_map/ppermute | solution.py:322
  98.4 18.7 %collective-permute-start.11 = (bf16[128,512]{1,0:T(8,128)(2,1)S(1)}, bf16[128,512]{1,0:T(8,128)(2,1)S(1)}, u32[]{:S(2)}, u32[]{:S(2)}) collective-permute-start(bf16[128,512]{1,0:T(8,128)(2,1)S(1)} %get-tuple-element.91), channel_id=1, source_target_pairs={{0,7},{1,6},{2,5},{3,4},{4,3},{5,2},{6,1},{7,0},{8,15},{9,14},{10,... | collective-permute-start | bytes 393224 | tf_op jit(solution)/shard_map/ppermute | solution.py:322
  106.3 10.7 %collective-permute-start.18 = (bf16[128,512]{1,0:T(8,128)(2,1)}, bf16[128,512]{1,0:T(8,128)(2,1)S(1)}, u32[]{:S(2)}, u32[]{:S(2)}) collective-permute-start(bf16[128,512]{1,0:T(8,128)(2,1)} %get-tuple-element.84), channel_id=1, source_target_pairs={{0,3},{1,2},{2,1},{3,0},{4,7},{5,6},{6,5},{7,4},{8,11},{9,10},{10,... | collective-permute-start | bytes 393224 | tf_op jit(solution)/shard_map/ppermute | solution.py:322
  112.6 5.2 %collective-permute-start.17 = (bf16[128,512]{1,0:T(8,128)(2,1)}, bf16[128,512]{1,0:T(8,128)(2,1)S(1)}, u32[]{:S(2)}, u32[]{:S(2)}) collective-permute-start(bf16[128,512]{1,0:T(8,128)(2,1)} %get-tuple-element.85), channel_id=1, source_target_pairs={{0,2},{1,3},{2,0},{3,1},{4,6},{5,7},{6,4},{7,5},{8,10},{9,11},{10,... | collective-permute-start | bytes 393224 | tf_op jit(solution)/shard_map/ppermute | solution.py:322
  114.2 3.6 %collective-permute-start.16 = (bf16[128,512]{1,0:T(8,128)(2,1)S(1)}, bf16[128,512]{1,0:T(8,128)(2,1)S(1)}, u32[]{:S(2)}, u32[]{:S(2)}) collective-permute-start(bf16[128,512]{1,0:T(8,128)(2,1)S(1)} %get-tuple-element.86), channel_id=1, source_target_pairs={{0,1},{1,0},{2,3},{3,2},{4,5},{5,4},{6,7},{7,6},{8,9},{9,8},{10,11... | collective-permute-start | bytes 393224 | tf_op jit(solution)/shard_map/ppermute | solution.py:322
  (8 other events, 50.4 us)

commit v2 on v0

--- a/solution.py
+++ b/solution.py
@@ -196,11 +196,17 @@
     tops = [jnp.full((1, TILE), -jnp.inf, jnp.float32)] * 2
     totals = [jnp.zeros((1, TILE), jnp.float32)] * 2
 
+    causal = key_row <= row
+    edge_oldest = jnp.where(causal, oldest, oldest + WINDOW_LENGTH)
+
     def score(head, item):
         part = dot(key_tile(item, 0), queries_turned[head], (1, 0))
-        seen = key_row >= oldest - (item - TILES) * TILE
-        if item == TILES:
-            seen = seen & (key_row <= row)
+        if item:
+            seen = key_row >= oldest - (item - TILES) * TILE
+        else:
+            last = dot(key_tile(TILES, 0), queries_turned[head], (1, 0))
+            part = jnp.where(causal, last, part)
+            seen = key_row >= edge_oldest
         part = jnp.where(seen, part, -jnp.inf)
         tops[head] = jnp.maximum(tops[head], jnp.max(part, axis=0, keepdims=True))
         scores[head][item] = part
@@ -208,6 +214,10 @@
     def weigh(head, item):
         part = jnp.exp2((scores[head][item] - tops[head]) * (SCORE_SCALE * LOG2_E))
         totals[head] = totals[head] + jnp.sum(part, axis=0, keepdims=True)
+        if item == 0:
+            last = jnp.where(causal, part, 0.0)
+            weights[tiles[TILES], columns[head]] = last.astype(jnp.bfloat16)
+            part = jnp.where(causal, 0.0, part)
         weights[tiles[item], columns[head]] = part.astype(jnp.bfloat16)
 
     def put(head, first, part):
@@ -238,14 +248,14 @@
             scaled_parts.append((part.astype(jnp.float32) * down).astype(jnp.bfloat16))
         return jnp.concatenate(scaled_parts, axis=0)
 
-    for item in range(SPAN):
+    for item in range(TILES):
         score(0, item)
-    for item in range(SPAN):
+    for item in range(TILES):
         score(1, item)
         weigh(0, item)
     shares = [1.0 / totals[0]]
     deltas = [attend(0, shares[0])]
-    for item in range(SPAN):
+    for item in range(TILES):
         weigh(1, item)
     shares.append(1.0 / totals[1])
     deltas.append(attend(1, shares[1]))
@@ -290,7 +300,7 @@
             pltpu.VMEM((KEYS, COLUMNS), jnp.bfloat16),
             pltpu.VMEM((KEYS, COLUMNS), jnp.bfloat16),
         ]
-        + [pltpu.VMEM((SPAN, TILE, TILE), jnp.float32)] * 2,
+        + [pltpu.VMEM((TILES, TILE, TILE), jnp.float32)] * 2,
         compiler_params=LIMIT,
         cost_estimate=pl.CostEstimate(
             flops=2 * products, bytes_accessed=WINDOW_LENGTH * width * 30, transcendentals=0

time: 114 us -> 113 us (level)
  no operation moved by 1% of the time
where the time goes in v2:
time: 113 us
  waiting for transfers between devices  48.4 us (43%)
  starting transfers between devices  33.6 us (30%)
  Pallas kernels  21.7 us (19%)
  local copies, waits for them, and re-layouts  5.01 us (4%)
  other arithmetic  3.1 us (3%)
    ppermute x4, waiting for transfers between devices, onward(): return lax.ppermute(block, 'stretch', route)  38.3 us
    pallas_call x1, Pallas kernels, attention(): pl.pallas_call(attention_kernel, grid=(TILES,), in_specs=[SCALARS, rows_b...  17 us
    ppermute x14, starting transfers between devices, swapped(): moved.append(lax.ppermute(piece, 'member', route) if distance else piece)  14.7 us
    ppermute x4, starting transfers between devices, onward(): return lax.ppermute(block, 'stretch', route)  10.5 us
    ppermute x14, waiting for transfers between devices, swapped(): moved.append(lax.ppermute(piece, 'member', route) if distance else piece)  10.1 us
    all_to_all x2, starting transfers between devices, exchanged(): lax.all_to_all(blocks, 'member', split_axis=0, concat_axis=0, tiled=True)  8.4 us
    pallas_call x2, Pallas kernels, pack(): pl.pallas_call(functools.partial(pack_kernel, distances), in_specs=[IN_HB...  3.67 us
  transfers between devices with their start and end apart: 20, of which 11 were waited for; matrix products, arithmetic and copies ran while one was open for 7% of the time, Pallas kernels for 2%

profile of v2, /device:TPU:0, one launch (start us, length us, event | category | flops | bytes accessed | tf_op | source)
XLA Modules:
  0.0 112.7 jit_solution(15052675980039245132)
XLA Ops:
  0.6 1.8 %shard_map.84 = (bf16[128,512]{1,0:T(8,128)(2,1)}, bf16[128,512]{1,0:T(8,128)(2,1)}, bf16[128,512]{1,0:T(8,128)(2,1)}, bf16[128,512]{1,0:T(8,128)(2,1)}) custom-call(bf16[128,2048]{1,0:T(8,128)(2,1)} %left_ref.2, bf16[128,2048]{1,0:T(8,128)(2,1)} %right_ref.2), custom_call_target="tpu_custom_call" | custom-call | bytes 1048576 | tf_op jit(solution)/shard_map/pallas_call | solution.py:85
  2.5 3.4 %collective-permute-start = (bf16[128,512]{1,0:T(8,128)(2,1)}, bf16[128,512]{1,0:T(8,128)(2,1)}, u32[]{:S(2)}, u32[]{:S(2)}) collective-permute-start(bf16[128,512]{1,0:T(8,128)(2,1)} %get-tuple-element.48), channel_id=1, source_target_pairs={{0,7},{1,6},{2,5},{3,4},{4,3},{5,2},{6,1},{7,0},{8,15},{9,14},{10,... | collective-permute-start | bytes 393224 | tf_op jit(solution)/shard_map/ppermute | solution.py:328
  6.5 1.4 %collective-permute-start.2 = (bf16[128,512]{1,0:T(8,128)(2,1)}, bf16[128,512]{1,0:T(8,128)(2,1)}, u32[]{:S(2)}, u32[]{:S(2)}) collective-permute-start(bf16[128,512]{1,0:T(8,128)(2,1)} %get-tuple-element.50), channel_id=1, source_target_pairs={{0,5},{1,4},{2,7},{3,6},{4,1},{5,0},{6,3},{7,2},{8,13},{9,12},{10,... | collective-permute-start | bytes 393224 | tf_op jit(solution)/shard_map/ppermute | solution.py:328
  8.2 1.8 %shard_map.85 = (bf16[128,512]{1,0:T(8,128)(2,1)}, bf16[128,512]{1,0:T(8,128)(2,1)}, bf16[128,512]{1,0:T(8,128)(2,1)}, bf16[128,512]{1,0:T(8,128)(2,1)}) custom-call(bf16[128,2048]{1,0:T(8,128)(2,1)} %left_ref.2, bf16[128,2048]{1,0:T(8,128)(2,1)} %right_ref.2), custom_call_target="tpu_custom_call" | custom-call | bytes 1048576 | tf_op jit(solution)/shard_map/pallas_call | solution.py:85
  10.0 1.2 %collective-permute-start.4 = (bf16[128,512]{1,0:T(8,128)(2,1)}, bf16[128,512]{1,0:T(8,128)(2,1)S(1)}, u32[]{:S(2)}, u32[]{:S(2)}) collective-permute-start(bf16[128,512]{1,0:T(8,128)(2,1)} %get-tuple-element.54), channel_id=1, source_target_pairs={{0,3},{1,2},{2,1},{3,0},{4,7},{5,6},{6,5},{7,4},{8,11},{9,10},{10,... | collective-permute-start | bytes 393224 | tf_op jit(solution)/shard_map/ppermute | solution.py:328
  11.2 1.8 %bitcast_bitcast_fusion = (bf16[8,128,512]{2,1,0:T(8,128)(2,1)S(1)}, bf16[8,128,512]{2,1,0:T(8,128)(2,1)S(1)}) fusion(bf16[16,8,8,512]{3,2,1,0:T(8,128)(2,1)} %bitcast.47, bf16[16,8,8,512]{3,2,1,0:T(8,128)(2,1)} %bitcast.48), kind=kLoop, calls=%fused_computation.1 | loop fusion | bytes 4194304 | tf_op jit(solution)/shard_map/transpose | solution.py:313
  13.9 1.6 %pad_maximum_fusion = bf16[8,128,1024]{2,1,0:T(8,128)(2,1)} fusion(bf16[8,128,512]{2,1,0:T(8,128)(2,1)S(1)} %get-tuple-element.94, bf16[8,128,512]{2,1,0:T(8,128)(2,1)S(1)} %get-tuple-element.95), kind=kLoop, calls=%fused_computation | loop fusion | flops 4194304 | bytes 4194304 | tf_op jit(solution)/shard_map/concatenate | solution.py:346
  15.8 2.8 %collective-permute-done.3 = bf16[128,512]{1,0:T(8,128)(2,1)} collective-permute-done((bf16[128,512]{1,0:T(8,128)(2,1)}, bf16[128,512]{1,0:T(8,128)(2,1)}, u32[]{:S(2)}, u32[]{:S(2)}) %collective-permute-start.3) | collective-permute-done | bytes 131104 | tf_op jit(solution)/shard_map/ppermute | solution.py:328
  19.4 4.5 %all-to-all-start = ((bf16[8,128,1024]{2,1,0:T(8,128)(2,1)}), bf16[8,128,1024]{2,1,0:T(8,128)(2,1)}, u32[]{:S(2)}, u32[]{:S(2)}) async-start(bf16[8,128,1024]{2,1,0:T(8,128)(2,1)} %pad_maximum_fusion), calls=%async_computation | async-start | bytes 4194304 | tf_op jit(solution)/shard_map/all_to_all | solution.py:321
  24.0 3.6 %collective-permute-start.8 = (bf16[4,128,512]{2,1,0:T(8,128)(2,1)S(1)}, bf16[4,128,512]{2,1,0:T(8,128)(2,1)S(1)}, u32[]{:S(2)}, u32[]{:S(2)}) collective-permute-start(bf16[4,128,512]{2,1,0:T(8,128)(2,1)S(1)} %pad_maximum_fusion.2.refs_1_), channel_id=1, source_target_pairs={{0,8},{8,16},{16,24},{1,9},{9,17},{17,25},{2,10},{10,18},{18,26},{... | collective-permute-start | bytes 1572872 | tf_op jit(solution)/shard_map/ppermute | solution.py:335
  27.6 1.2 %pad_maximum_fusion.1.refs_0_ = bf16[4,128,512]{2,1,0:T(8,128)(2,1)S(1)} fusion(bf16[1,128,512]{2,1,0:T(8,128)(2,1)} %bitcast.6, bf16[1,128,512]{2,1,0:T(8,128)(2,1)} %bitcast.5, bf16[1,128,512]{2,1,0:T(8,128)(2,1)} %bitcast.4, bf16[1,128,512]{2,1,0:T(8,128)(2,1)} %bitcast.3), kind=kLoop, calls=%fused_computation.7 | loop fusion | flops 786432 | bytes 1048576 | tf_op jit(solution)/shard_map/stack | solution.py:348
  28.8 4.3 %collective-permute-start.7 = (bf16[4,128,512]{2,1,0:T(8,128)(2,1)S(1)}, bf16[4,128,512]{2,1,0:T(8,128)(2,1)}, u32[]{:S(2)}, u32[]{:S(2)}) collective-permute-start(bf16[4,128,512]{2,1,0:T(8,128)(2,1)S(1)} %pad_maximum_fusion.1.refs_0_), channel_id=1, source_target_pairs={{0,8},{8,16},{16,24},{1,9},{9,17},{17,25},{2,10},{10,18},{18,26},{... | collective-permute-start | bytes 1572872 | tf_op jit(solution)/shard_map/ppermute | solution.py:335
  33.0 6.8 %collective-permute-done.8.refs_3_ = bf16[4,128,512]{2,1,0:T(8,128)(2,1)S(1)} collective-permute-done((bf16[4,128,512]{2,1,0:T(8,128)(2,1)S(1)}, bf16[4,128,512]{2,1,0:T(8,128)(2,1)S(1)}, u32[]{:S(2)}, u32[]{:S(2)}) %collective-permute-start.8) | collective-permute-done | bytes 524320 | tf_op jit(solution)/shard_map/ppermute | solution.py:335
  39.8 10.7 %collective-permute-done.7.refs_2_ = bf16[4,128,512]{2,1,0:T(8,128)(2,1)} collective-permute-done((bf16[4,128,512]{2,1,0:T(8,128)(2,1)S(1)}, bf16[4,128,512]{2,1,0:T(8,128)(2,1)}, u32[]{:S(2)}, u32[]{:S(2)}) %collective-permute-start.7) | collective-permute-done | bytes 524320 | tf_op jit(solution)/shard_map/ppermute | solution.py:335
  50.6 17.0 %shard_map.86 = (bf16[1024,1024]{1,0:T(8,128)(2,1)}, bf16[4,128,512]{2,1,0:T(8,128)(2,1)}, bf16[4,128,512]{2,1,0:T(8,128)(2,1)}, bf16[4,128,512]{2,1,0:T(8,128)(2,1)}, bf16[4,128,512]{2,1,0:T(8,128)(2,1)}) custom-call(s32[8]{0:T(128)} %lengths_ref.1, bf16[1024,1024]{1,0:T(8,128)(2,1)} %bitcast.2.rows_ref, bf16[4,128,512]{2,1,0:T(8,128)(2,1)} %copy-done.3, ...), custom_call_target="tpu_custom_call" | custom-call | flops 16106127360 | bytes 7864320 | tf_op jit(solution)/shard_map/pallas_call | solution.py:290
  67.6 3.9 %all-to-all-start.1 = ((bf16[8,128,1024]{2,1,0:T(8,128)(2,1)}), bf16[8,128,1024]{2,1,0:T(8,128)(2,1)S(1)}, u32[]{:S(2)}, u32[]{:S(2)}) async-start(bf16[8,128,1024]{2,1,0:T(8,128)(2,1)} %bitcast.44), calls=%async_computation.1 | async-start | bytes 4194304 | tf_op jit(solution)/shard_map/all_to_all | solution.py:321
  71.5 1.4 %collective-permute-start.9 = (bf16[4,128,512]{2,1,0:T(8,128)(2,1)S(1)}, bf16[4,128,512]{2,1,0:T(8,128)(2,1)S(1)}, u32[]{:S(2)}, u32[]{:S(2)}) collective-permute-start(bf16[4,128,512]{2,1,0:T(8,128)(2,1)S(1)} %copy-done.6), channel_id=1, source_target_pairs={{8,0},{16,8},{24,16},{9,1},{17,9},{25,17},{10,2},{18,10},{26,18},{... | collective-permute-start | bytes 1572872 | tf_op jit(solution)/shard_map/ppermute | solution.py:335
  72.9 1.3 %collective-permute-start.14 = (bf16[4,128,512]{2,1,0:T(8,128)(2,1)}, bf16[4,128,512]{2,1,0:T(8,128)(2,1)S(1)}, u32[]{:S(2)}, u32[]{:S(2)}) collective-permute-start(bf16[4,128,512]{2,1,0:T(8,128)(2,1)} %get-tuple-element.71), channel_id=1, source_target_pairs={{8,0},{16,8},{24,16},{9,1},{17,9},{25,17},{10,2},{18,10},{26,18},{... | collective-permute-start | bytes 1572872 | tf_op jit(solution)/shard_map/ppermute | solution.py:335
  74.2 14.7 %collective-permute-done.9 = bf16[4,128,512]{2,1,0:T(8,128)(2,1)S(1)} collective-permute-done((bf16[4,128,512]{2,1,0:T(8,128)(2,1)S(1)}, bf16[4,128,512]{2,1,0:T(8,128)(2,1)S(1)}, u32[]{:S(2)}, u32[]{:S(2)}) %collective-permute-start.9) | collective-permute-done | bytes 524320 | tf_op jit(solution)/shard_map/ppermute | solution.py:335
  89.1 2.0 %collective-permute-start.13 = (bf16[128,512]{1,0:T(8,128)(2,1)S(1)}, bf16[128,512]{1,0:T(8,128)(2,1)S(1)}, u32[]{:S(2)}, u32[]{:S(2)}) collective-permute-start(bf16[128,512]{1,0:T(8,128)(2,1)S(1)} %get-tuple-element.90), channel_id=1, source_target_pairs={{0,4},{1,5},{2,6},{3,7},{4,0},{5,1},{6,2},{7,3},{8,12},{9,13},{10,... | collective-permute-start | bytes 393224 | tf_op jit(solution)/shard_map/ppermute | solution.py:328
  91.1 1.5 %collective-permute-start.11 = (bf16[128,512]{1,0:T(8,128)(2,1)S(1)}, bf16[128,512]{1,0:T(8,128)(2,1)S(1)}, u32[]{:S(2)}, u32[]{:S(2)}) collective-permute-start(bf16[128,512]{1,0:T(8,128)(2,1)S(1)} %get-tuple-element.92), channel_id=1, source_target_pairs={{0,6},{1,7},{2,4},{3,5},{4,2},{5,3},{6,0},{7,1},{8,14},{9,15},{10,... | collective-permute-start | bytes 393224 | tf_op jit(solution)/shard_map/ppermute | solution.py:328
  92.6 1.2 %collective-permute-start.10 = (bf16[128,512]{1,0:T(8,128)(2,1)S(1)}, bf16[128,512]{1,0:T(8,128)(2,1)S(1)}, u32[]{:S(2)}, u32[]{:S(2)}) collective-permute-start(bf16[128,512]{1,0:T(8,128)(2,1)S(1)} %get-tuple-element.93), channel_id=1, source_target_pairs={{0,7},{1,6},{2,5},{3,4},{4,3},{5,2},{6,1},{7,0},{8,15},{9,14},{10,... | collective-permute-start | bytes 393224 | tf_op jit(solution)/shard_map/ppermute | solution.py:328
  93.8 6.2 %collective-permute-done.14 = bf16[4,128,512]{2,1,0:T(8,128)(2,1)S(1)} collective-permute-done((bf16[4,128,512]{2,1,0:T(8,128)(2,1)}, bf16[4,128,512]{2,1,0:T(8,128)(2,1)S(1)}, u32[]{:S(2)}, u32[]{:S(2)}) %collective-permute-start.14) | collective-permute-done | bytes 524320 | tf_op jit(solution)/shard_map/ppermute | solution.py:335
  101.8 4.7 %collective-permute-done.13.refs_3_ = bf16[128,512]{1,0:T(8,128)(2,1)S(1)} collective-permute-done((bf16[128,512]{1,0:T(8,128)(2,1)S(1)}, bf16[128,512]{1,0:T(8,128)(2,1)S(1)}, u32[]{:S(2)}, u32[]{:S(2)}) %collective-permute-start.13) | collective-permute-done | bytes 131104 | tf_op jit(solution)/shard_map/ppermute | solution.py:328
  (49 shorter events, 11.3 us)
Async XLA Ops:
  2.5 10.5 %collective-permute-start = (bf16[128,512]{1,0:T(8,128)(2,1)}, bf16[128,512]{1,0:T(8,128)(2,1)}, u32[]{:S(2)}, u32[]{:S(2)}) collective-permute-start(bf16[128,512]{1,0:T(8,128)(2,1)} %get-tuple-element.48), channel_id=1, source_target_pairs={{0,7},{1,6},{2,5},{3,4},{4,3},{5,2},{6,1},{7,0},{8,15},{9,14},{10,... | collective-permute-start | bytes 393224 | tf_op jit(solution)/shard_map/ppermute | solution.py:328
  5.9 7.9 %collective-permute-start.1 = (bf16[128,512]{1,0:T(8,128)(2,1)}, bf16[128,512]{1,0:T(8,128)(2,1)}, u32[]{:S(2)}, u32[]{:S(2)}) collective-permute-start(bf16[128,512]{1,0:T(8,128)(2,1)} %get-tuple-element.49), channel_id=1, source_target_pairs={{0,6},{1,7},{2,4},{3,5},{4,2},{5,3},{6,0},{7,1},{8,14},{9,15},{10,... | collective-permute-start | bytes 393224 | tf_op jit(solution)/shard_map/ppermute | solution.py:328
  6.5 9.3 %collective-permute-start.2 = (bf16[128,512]{1,0:T(8,128)(2,1)}, bf16[128,512]{1,0:T(8,128)(2,1)}, u32[]{:S(2)}, u32[]{:S(2)}) collective-permute-start(bf16[128,512]{1,0:T(8,128)(2,1)} %get-tuple-element.50), channel_id=1, source_target_pairs={{0,5},{1,4},{2,7},{3,6},{4,1},{5,0},{6,3},{7,2},{8,13},{9,12},{10,... | collective-permute-start | bytes 393224 | tf_op jit(solution)/shard_map/ppermute | solution.py:328
  7.9 10.8 %collective-permute-start.3 = (bf16[128,512]{1,0:T(8,128)(2,1)}, bf16[128,512]{1,0:T(8,128)(2,1)}, u32[]{:S(2)}, u32[]{:S(2)}) collective-permute-start(bf16[128,512]{1,0:T(8,128)(2,1)} %get-tuple-element.51), channel_id=1, source_target_pairs={{0,4},{1,5},{2,6},{3,7},{4,0},{5,1},{6,2},{7,3},{8,12},{9,13},{10,... | collective-permute-start | bytes 393224 | tf_op jit(solution)/shard_map/ppermute | solution.py:328
  10.0 8.7 %collective-permute-start.4 = (bf16[128,512]{1,0:T(8,128)(2,1)}, bf16[128,512]{1,0:T(8,128)(2,1)S(1)}, u32[]{:S(2)}, u32[]{:S(2)}) collective-permute-start(bf16[128,512]{1,0:T(8,128)(2,1)} %get-tuple-element.54), channel_id=1, source_target_pairs={{0,3},{1,2},{2,1},{3,0},{4,7},{5,6},{6,5},{7,4},{8,11},{9,10},{10,... | collective-permute-start | bytes 393224 | tf_op jit(solution)/shard_map/ppermute | solution.py:328
  13.0 6.4 %collective-permute-start.5 = (bf16[128,512]{1,0:T(8,128)(2,1)S(1)}, bf16[128,512]{1,0:T(8,128)(2,1)S(1)}, u32[]{:S(2)}, u32[]{:S(2)}) collective-permute-start(bf16[128,512]{1,0:T(8,128)(2,1)S(1)} %copy-done.8), channel_id=1, source_target_pairs={{0,2},{1,3},{2,0},{3,1},{4,6},{5,7},{6,4},{7,5},{8,10},{9,11},{10,... | collective-permute-start | bytes 393224 | tf_op jit(solution)/shard_map/ppermute | solution.py:328
  13.8 5.6 %collective-permute-start.6 = (bf16[128,512]{1,0:T(8,128)(2,1)S(1)}, bf16[128,512]{1,0:T(8,128)(2,1)S(1)}, u32[]{:S(2)}, u32[]{:S(2)}) collective-permute-start(bf16[128,512]{1,0:T(8,128)(2,1)S(1)} %copy-done.7), channel_id=1, source_target_pairs={{0,1},{1,0},{2,3},{3,2},{4,5},{5,4},{6,7},{7,6},{8,9},{9,8},{10,11... | collective-permute-start | bytes 393224 | tf_op jit(solution)/shard_map/ppermute | solution.py:328
  19.4 31.1 %all-to-all-start = ((bf16[8,128,1024]{2,1,0:T(8,128)(2,1)}), bf16[8,128,1024]{2,1,0:T(8,128)(2,1)}, u32[]{:S(2)}, u32[]{:S(2)}) async-start(bf16[8,128,1024]{2,1,0:T(8,128)(2,1)} %pad_maximum_fusion), calls=%async_computation | async-start | bytes 4194304 | tf_op jit(solution)/shard_map/all_to_all | solution.py:321
  24.0 26.6 %copy-start.2 = (bf16[4,128,512]{2,1,0:T(8,128)(2,1)}, bf16[4,128,512]{2,1,0:T(8,128)(2,1)S(1)}, u32[]{:S(2)}) copy-start(bf16[4,128,512]{2,1,0:T(8,128)(2,1)S(1)} %pad_maximum_fusion.2.refs_1_) | copy-start | bytes 1572868
  24.0 15.8 %collective-permute-start.8 = (bf16[4,128,512]{2,1,0:T(8,128)(2,1)S(1)}, bf16[4,128,512]{2,1,0:T(8,128)(2,1)S(1)}, u32[]{:S(2)}, u32[]{:S(2)}) collective-permute-start(bf16[4,128,512]{2,1,0:T(8,128)(2,1)S(1)} %pad_maximum_fusion.2.refs_1_), channel_id=1, source_target_pairs={{0,8},{8,16},{16,24},{1,9},{9,17},{17,25},{2,10},{10,18},{18,26},{... | collective-permute-start | bytes 1572872 | tf_op jit(solution)/shard_map/ppermute | solution.py:335
  28.8 21.8 %copy-start.3 = (bf16[4,128,512]{2,1,0:T(8,128)(2,1)}, bf16[4,128,512]{2,1,0:T(8,128)(2,1)S(1)}, u32[]{:S(2)}) copy-start(bf16[4,128,512]{2,1,0:T(8,128)(2,1)S(1)} %pad_maximum_fusion.1.refs_0_) | copy-start | bytes 1572868
  28.8 21.7 %collective-permute-start.7 = (bf16[4,128,512]{2,1,0:T(8,128)(2,1)S(1)}, bf16[4,128,512]{2,1,0:T(8,128)(2,1)}, u32[]{:S(2)}, u32[]{:S(2)}) collective-permute-start(bf16[4,128,512]{2,1,0:T(8,128)(2,1)S(1)} %pad_maximum_fusion.1.refs_0_), channel_id=1, source_target_pairs={{0,8},{8,16},{16,24},{1,9},{9,17},{17,25},{2,10},{10,18},{18,26},{... | collective-permute-start | bytes 1572872 | tf_op jit(solution)/shard_map/ppermute | solution.py:335
  67.6 21.4 %copy-start.1 = (bf16[4,128,512]{2,1,0:T(8,128)(2,1)S(1)}, bf16[4,128,512]{2,1,0:T(8,128)(2,1)}, u32[]{:S(2)}) copy-start(bf16[4,128,512]{2,1,0:T(8,128)(2,1)} %get-tuple-element.68) | copy-start | bytes 1572868
  67.6 40.7 %all-to-all-start.1 = ((bf16[8,128,1024]{2,1,0:T(8,128)(2,1)}), bf16[8,128,1024]{2,1,0:T(8,128)(2,1)S(1)}, u32[]{:S(2)}, u32[]{:S(2)}) async-start(bf16[8,128,1024]{2,1,0:T(8,128)(2,1)} %bitcast.44), calls=%async_computation.1 | async-start | bytes 4194304 | tf_op jit(solution)/shard_map/all_to_all | solution.py:321
  71.5 28.5 %copy-start = (bf16[4,128,512]{2,1,0:T(8,128)(2,1)S(1)}, bf16[4,128,512]{2,1,0:T(8,128)(2,1)}, u32[]{:S(2)}) copy-start(bf16[4,128,512]{2,1,0:T(8,128)(2,1)} %get-tuple-element.70) | copy-start | bytes 1572868
  71.5 17.4 %collective-permute-start.9 = (bf16[4,128,512]{2,1,0:T(8,128)(2,1)S(1)}, bf16[4,128,512]{2,1,0:T(8,128)(2,1)S(1)}, u32[]{:S(2)}, u32[]{:S(2)}) collective-permute-start(bf16[4,128,512]{2,1,0:T(8,128)(2,1)S(1)} %copy-done.6), channel_id=1, source_target_pairs={{8,0},{16,8},{24,16},{9,1},{17,9},{25,17},{10,2},{18,10},{26,18},{... | collective-permute-start | bytes 1572872 | tf_op jit(solution)/shard_map/ppermute | solution.py:335
  72.9 27.0 %collective-permute-start.14 = (bf16[4,128,512]{2,1,0:T(8,128)(2,1)}, bf16[4,128,512]{2,1,0:T(8,128)(2,1)S(1)}, u32[]{:S(2)}, u32[]{:S(2)}) collective-permute-start(bf16[4,128,512]{2,1,0:T(8,128)(2,1)} %get-tuple-element.71), channel_id=1, source_target_pairs={{8,0},{16,8},{24,16},{9,1},{17,9},{25,17},{10,2},{18,10},{26,18},{... | collective-permute-start | bytes 1572872 | tf_op jit(solution)/shard_map/ppermute | solution.py:335
  89.1 17.4 %collective-permute-start.13 = (bf16[128,512]{1,0:T(8,128)(2,1)S(1)}, bf16[128,512]{1,0:T(8,128)(2,1)S(1)}, u32[]{:S(2)}, u32[]{:S(2)}) collective-permute-start(bf16[128,512]{1,0:T(8,128)(2,1)S(1)} %get-tuple-element.90), channel_id=1, source_target_pairs={{0,4},{1,5},{2,6},{3,7},{4,0},{5,1},{6,2},{7,3},{8,12},{9,13},{10,... | collective-permute-start | bytes 393224 | tf_op jit(solution)/shard_map/ppermute | solution.py:328
  91.1 16.5 %collective-permute-start.12 = (bf16[128,512]{1,0:T(8,128)(2,1)S(1)}, bf16[128,512]{1,0:T(8,128)(2,1)S(1)}, u32[]{:S(2)}, u32[]{:S(2)}) collective-permute-start(bf16[128,512]{1,0:T(8,128)(2,1)S(1)} %get-tuple-element.91), channel_id=1, source_target_pairs={{0,5},{1,4},{2,7},{3,6},{4,1},{5,0},{6,3},{7,2},{8,13},{9,12},{10,... | collective-permute-start | bytes 393224 | tf_op jit(solution)/shard_map/ppermute | solution.py:328
  91.1 19.6 %collective-permute-start.11 = (bf16[128,512]{1,0:T(8,128)(2,1)S(1)}, bf16[128,512]{1,0:T(8,128)(2,1)S(1)}, u32[]{:S(2)}, u32[]{:S(2)}) collective-permute-start(bf16[128,512]{1,0:T(8,128)(2,1)S(1)} %get-tuple-element.92), channel_id=1, source_target_pairs={{0,6},{1,7},{2,4},{3,5},{4,2},{5,3},{6,0},{7,1},{8,14},{9,15},{10,... | collective-permute-start | bytes 393224 | tf_op jit(solution)/shard_map/ppermute | solution.py:328
  92.6 18.1 %collective-permute-start.10 = (bf16[128,512]{1,0:T(8,128)(2,1)S(1)}, bf16[128,512]{1,0:T(8,128)(2,1)S(1)}, u32[]{:S(2)}, u32[]{:S(2)}) collective-permute-start(bf16[128,512]{1,0:T(8,128)(2,1)S(1)} %get-tuple-element.93), channel_id=1, source_target_pairs={{0,7},{1,6},{2,5},{3,4},{4,3},{5,2},{6,1},{7,0},{8,15},{9,14},{10,... | collective-permute-start | bytes 393224 | tf_op jit(solution)/shard_map/ppermute | solution.py:328
  100.8 9.8 %collective-permute-start.17 = (bf16[128,512]{1,0:T(8,128)(2,1)}, bf16[128,512]{1,0:T(8,128)(2,1)S(1)}, u32[]{:S(2)}, u32[]{:S(2)}) collective-permute-start(bf16[128,512]{1,0:T(8,128)(2,1)} %get-tuple-element.86), channel_id=1, source_target_pairs={{0,3},{1,2},{2,1},{3,0},{4,7},{5,6},{6,5},{7,4},{8,11},{9,10},{10,... | collective-permute-start | bytes 393224 | tf_op jit(solution)/shard_map/ppermute | solution.py:328
  106.5 5.2 %collective-permute-start.16 = (bf16[128,512]{1,0:T(8,128)(2,1)}, bf16[128,512]{1,0:T(8,128)(2,1)S(1)}, u32[]{:S(2)}, u32[]{:S(2)}) collective-permute-start(bf16[128,512]{1,0:T(8,128)(2,1)} %get-tuple-element.87), channel_id=1, source_target_pairs={{0,2},{1,3},{2,0},{3,1},{4,6},{5,7},{6,4},{7,5},{8,10},{9,11},{10,... | collective-permute-start | bytes 393224 | tf_op jit(solution)/shard_map/ppermute | solution.py:328
  107.6 4.1 %collective-permute-start.15 = (bf16[128,512]{1,0:T(8,128)(2,1)S(1)}, bf16[128,512]{1,0:T(8,128)(2,1)S(1)}, u32[]{:S(2)}, u32[]{:S(2)}) collective-permute-start(bf16[128,512]{1,0:T(8,128)(2,1)S(1)} %get-tuple-element.88), channel_id=1, source_target_pairs={{0,1},{1,0},{2,3},{3,2},{4,5},{5,4},{6,7},{7,6},{8,9},{9,8},{10,11... | collective-permute-start | bytes 393224 | tf_op jit(solution)/shard_map/ppermute | solution.py:328
  (5 other events, 23.6 us)

commit v3 on v2

--- a/solution.py
+++ b/solution.py
@@ -21,6 +21,7 @@
 KEYS = SPAN * TILE
 ROWS = WINDOW_LENGTH // MEMBERS
 CHUNKS = TILE // ROWS
+ONES = 16
 COLUMNS = 2 * TILE
 SCORE_SCALE = HEAD_WIDTH ** (-0.5)
 LOG2_E = 1.4426950408889634
@@ -144,7 +145,7 @@
 
     def turn(tile):
         part = kv[pl.ds(tile * CHUNKS, CHUNKS)].reshape(TILE, 2 * width)
-        kv_turned[:, pl.ds(pl.multiple_of(tile * TILE, TILE), TILE)] = part.T
+        kv_turned[: 2 * width, pl.ds(pl.multiple_of(tile * TILE, TILE), TILE)] = part.T
 
     @pl.when(step == 0)
     def _():
@@ -153,6 +154,7 @@
             kv[chunk] = earlier_halves[half][part]
             kv[MEMBERS + chunk] = own_halves[half][part]
         sums[:MEMBERS] = jnp.zeros((MEMBERS, ROWS, 2 * width), jnp.float32)
+        kv_turned[2 * width :] = jnp.ones((ONES, 2 * WINDOW_LENGTH), jnp.bfloat16)
         for tile in range(TILES):
             turn(tile)
 
@@ -162,9 +164,9 @@
         tile = pl.ds((step + item) * CHUNKS, CHUNKS)
         return kv[tile, :, first : first + width].reshape(TILE, width)
 
-    def turned_window(first):
+    def turned_window(first, last):
         place = pl.ds(pl.multiple_of(step * TILE, TILE), KEYS)
-        return kv_turned[first : first + width, place]
+        return kv_turned[first:last, place]
 
     def add(item, first, part):
         tile = pl.ds((step + item) * CHUNKS, CHUNKS)
@@ -194,7 +196,6 @@
     key_row = lax.broadcasted_iota(jnp.int32, (TILE, TILE), 0)
 
     tops = [jnp.full((1, TILE), -jnp.inf, jnp.float32)] * 2
-    totals = [jnp.zeros((1, TILE), jnp.float32)] * 2
 
     causal = key_row <= row
     edge_oldest = jnp.where(causal, oldest, oldest + WINDOW_LENGTH)
@@ -213,7 +214,6 @@
 
     def weigh(head, item):
         part = jnp.exp2((scores[head][item] - tops[head]) * (SCORE_SCALE * LOG2_E))
-        totals[head] = totals[head] + jnp.sum(part, axis=0, keepdims=True)
         if item == 0:
             last = jnp.where(causal, part, 0.0)
             weights[tiles[TILES], columns[head]] = last.astype(jnp.bfloat16)
@@ -224,12 +224,14 @@
         place = slice((first + head) * width, (first + head + 1) * width)
         out_ref[:, place] = part.astype(jnp.bfloat16).T
 
-    def attend(head, share):
-        attended = dot(turned_window(width), weights[:, columns[head]], (1, 0))
-        attended = (attended * share).astype(jnp.bfloat16)
+    def attend(head):
+        values = turned_window(width, 2 * width + ONES)
+        attended = dot(values, weights[:, columns[head]], (1, 0))
+        share = 1.0 / attended[width : width + 1]
+        attended = (attended[:width] * share).astype(jnp.bfloat16)
         put(head, 0, attended)
         products = attended.astype(jnp.float32) * cotangents_turned[head].astype(jnp.float32)
-        return jnp.sum(products, axis=0, keepdims=True)
+        return share, jnp.sum(products, axis=0, keepdims=True)
 
     def weigh_grad(head, item, row_delta):
         grad = dot(key_tile(item, width), cotangents_turned[head], (1, 0)) - row_delta
@@ -238,7 +240,7 @@
         grad_weights[tiles[item], columns[head]] = part
 
     def make_query_grad(head, share):
-        query_grad = dot(turned_window(0), grad_weights[:, columns[head]], (1, 0))
+        query_grad = dot(turned_window(0, width), grad_weights[:, columns[head]], (1, 0))
         put(head, 2, query_grad * (share * SCORE_SCALE))
 
     def scaled(parts, shares):
@@ -253,14 +255,13 @@
     for item in range(TILES):
         score(1, item)
         weigh(0, item)
-    shares = [1.0 / totals[0]]
-    deltas = [attend(0, shares[0])]
+    shares, deltas = [None] * 2, [None] * 2
+    shares[0], deltas[0] = attend(0)
     for item in range(TILES):
         weigh(1, item)
-    shares.append(1.0 / totals[1])
-    deltas.append(attend(1, shares[1]))
+    shares[1], deltas[1] = attend(1)
     cotangents_scaled = scaled(cotangents, shares)
-    queries_scaled = scaled(queries, shares)
+    queries_scaled = scaled(queries, [share * SCORE_SCALE for share in shares])
     for item in range(SPAN):
         weigh_grad(0, item, deltas[0])
         weigh_grad(1, item, deltas[1])
@@ -275,10 +276,7 @@
             half, part, chunk = item // HALF, item % HALF, member ^ distance
             for halves, place in ((earlier_grads, chunk), (own_grads, MEMBERS + chunk)):
                 target = halves[half]
-                target[part, :, :width] = (sums[place, :, :width] * SCORE_SCALE).astype(
-                    jnp.bfloat16
-                )
-                target[part, :, width:] = sums[place, :, width:].astype(jnp.bfloat16)
+                target[part] = sums[place].astype(jnp.bfloat16)
 
 
 def attention(doc_lengths, rows, own, earlier):
@@ -295,7 +293,7 @@
         out_shape=[jax.ShapeDtypeStruct(rows.shape, jnp.bfloat16)] + [half] * 4,
         scratch_shapes=[
             pltpu.VMEM((2 * MEMBERS, ROWS, 2 * width), jnp.bfloat16),
-            pltpu.VMEM((2 * width, 2 * WINDOW_LENGTH), jnp.bfloat16),
+            pltpu.VMEM((2 * width + ONES, 2 * WINDOW_LENGTH), jnp.bfloat16),
             pltpu.VMEM((2 * MEMBERS, ROWS, 2 * width), jnp.float32),
             pltpu.VMEM((KEYS, COLUMNS), jnp.bfloat16),
             pltpu.VMEM((KEYS, COLUMNS), jnp.bfloat16),

time: 113 us -> 115 us (1.018)
  Pallas kernels: 21.7 us -> 23.1 us
    pallas_call x1, Pallas kernels: 17 us -> 18.4 us  [attention(): pl.pallas_call(attention_kernel, grid=(TILES,), in_specs=[SCALARS, rows_b...]
where the time goes in v3:
time: 115 us; the launch traced here: 114 us
  waiting for transfers between devices  48.4 us (42%)
  starting transfers between devices  33.6 us (29%)
  Pallas kernels  23.1 us (20%)
  local copies, waits for them, and re-layouts  5.01 us (4%)
  other arithmetic  3.1 us (3%)
    ppermute x4, waiting for transfers between devices, onward(): return lax.ppermute(block, 'stretch', route)  38.3 us
    pallas_call x1, Pallas kernels, attention(): pl.pallas_call(attention_kernel, grid=(TILES,), in_specs=[SCALARS, rows_b...  18.4 us
    ppermute x14, starting transfers between devices, swapped(): moved.append(lax.ppermute(piece, 'member', route) if distance else piece)  14.7 us
    ppermute x4, starting transfers between devices, onward(): return lax.ppermute(block, 'stretch', route)  10.5 us
    ppermute x14, waiting for transfers between devices, swapped(): moved.append(lax.ppermute(piece, 'member', route) if distance else piece)  10.1 us
    all_to_all x2, starting transfers between devices, exchanged(): lax.all_to_all(blocks, 'member', split_axis=0, concat_axis=0, tiled=True)  8.41 us
    pallas_call x2, Pallas kernels, pack(): pl.pallas_call(functools.partial(pack_kernel, distances), in_specs=[IN_HB...  3.67 us
  transfers between devices with their start and end apart: 20, of which 11 were waited for; matrix products, arithmetic and copies ran while one was open for 7% of the time, Pallas kernels for 2%

profile of v3, /device:TPU:0, one launch (start us, length us, event | category | flops | bytes accessed | tf_op | source)
XLA Modules:
  0.0 114.1 jit_solution(14068254328255703747)
XLA Ops:
  0.6 1.8 %shard_map.84 = (bf16[128,512]{1,0:T(8,128)(2,1)}, bf16[128,512]{1,0:T(8,128)(2,1)}, bf16[128,512]{1,0:T(8,128)(2,1)}, bf16[128,512]{1,0:T(8,128)(2,1)}) custom-call(bf16[128,2048]{1,0:T(8,128)(2,1)} %left_ref.2, bf16[128,2048]{1,0:T(8,128)(2,1)} %right_ref.2), custom_call_target="tpu_custom_call" | custom-call | bytes 1048576 | tf_op jit(solution)/shard_map/pallas_call | solution.py:86
  2.5 3.4 %collective-permute-start = (bf16[128,512]{1,0:T(8,128)(2,1)}, bf16[128,512]{1,0:T(8,128)(2,1)}, u32[]{:S(2)}, u32[]{:S(2)}) collective-permute-start(bf16[128,512]{1,0:T(8,128)(2,1)} %get-tuple-element.48), channel_id=1, source_target_pairs={{0,7},{1,6},{2,5},{3,4},{4,3},{5,2},{6,1},{7,0},{8,15},{9,14},{10,... | collective-permute-start | bytes 393224 | tf_op jit(solution)/shard_map/ppermute | solution.py:326
  6.5 1.4 %collective-permute-start.2 = (bf16[128,512]{1,0:T(8,128)(2,1)}, bf16[128,512]{1,0:T(8,128)(2,1)}, u32[]{:S(2)}, u32[]{:S(2)}) collective-permute-start(bf16[128,512]{1,0:T(8,128)(2,1)} %get-tuple-element.50), channel_id=1, source_target_pairs={{0,5},{1,4},{2,7},{3,6},{4,1},{5,0},{6,3},{7,2},{8,13},{9,12},{10,... | collective-permute-start | bytes 393224 | tf_op jit(solution)/shard_map/ppermute | solution.py:326
  8.2 1.8 %shard_map.85 = (bf16[128,512]{1,0:T(8,128)(2,1)}, bf16[128,512]{1,0:T(8,128)(2,1)}, bf16[128,512]{1,0:T(8,128)(2,1)}, bf16[128,512]{1,0:T(8,128)(2,1)}) custom-call(bf16[128,2048]{1,0:T(8,128)(2,1)} %left_ref.2, bf16[128,2048]{1,0:T(8,128)(2,1)} %right_ref.2), custom_call_target="tpu_custom_call" | custom-call | bytes 1048576 | tf_op jit(solution)/shard_map/pallas_call | solution.py:86
  10.0 1.2 %collective-permute-start.4 = (bf16[128,512]{1,0:T(8,128)(2,1)}, bf16[128,512]{1,0:T(8,128)(2,1)S(1)}, u32[]{:S(2)}, u32[]{:S(2)}) collective-permute-start(bf16[128,512]{1,0:T(8,128)(2,1)} %get-tuple-element.54), channel_id=1, source_target_pairs={{0,3},{1,2},{2,1},{3,0},{4,7},{5,6},{6,5},{7,4},{8,11},{9,10},{10,... | collective-permute-start | bytes 393224 | tf_op jit(solution)/shard_map/ppermute | solution.py:326
  11.2 1.8 %bitcast_bitcast_fusion = (bf16[8,128,512]{2,1,0:T(8,128)(2,1)S(1)}, bf16[8,128,512]{2,1,0:T(8,128)(2,1)S(1)}) fusion(bf16[16,8,8,512]{3,2,1,0:T(8,128)(2,1)} %bitcast.47, bf16[16,8,8,512]{3,2,1,0:T(8,128)(2,1)} %bitcast.48), kind=kLoop, calls=%fused_computation.1 | loop fusion | bytes 4194304 | tf_op jit(solution)/shard_map/transpose | solution.py:311
  13.9 1.6 %pad_maximum_fusion = bf16[8,128,1024]{2,1,0:T(8,128)(2,1)} fusion(bf16[8,128,512]{2,1,0:T(8,128)(2,1)S(1)} %get-tuple-element.94, bf16[8,128,512]{2,1,0:T(8,128)(2,1)S(1)} %get-tuple-element.95), kind=kLoop, calls=%fused_computation | loop fusion | flops 4194304 | bytes 4194304 | tf_op jit(solution)/shard_map/concatenate | solution.py:344
  15.8 2.8 %collective-permute-done.3 = bf16[128,512]{1,0:T(8,128)(2,1)} collective-permute-done((bf16[128,512]{1,0:T(8,128)(2,1)}, bf16[128,512]{1,0:T(8,128)(2,1)}, u32[]{:S(2)}, u32[]{:S(2)}) %collective-permute-start.3) | collective-permute-done | bytes 131104 | tf_op jit(solution)/shard_map/ppermute | solution.py:326
  19.4 4.5 %all-to-all-start = ((bf16[8,128,1024]{2,1,0:T(8,128)(2,1)}), bf16[8,128,1024]{2,1,0:T(8,128)(2,1)}, u32[]{:S(2)}, u32[]{:S(2)}) async-start(bf16[8,128,1024]{2,1,0:T(8,128)(2,1)} %pad_maximum_fusion), calls=%async_computation | async-start | bytes 4194304 | tf_op jit(solution)/shard_map/all_to_all | solution.py:319
  24.0 3.6 %collective-permute-start.8 = (bf16[4,128,512]{2,1,0:T(8,128)(2,1)S(1)}, bf16[4,128,512]{2,1,0:T(8,128)(2,1)S(1)}, u32[]{:S(2)}, u32[]{:S(2)}) collective-permute-start(bf16[4,128,512]{2,1,0:T(8,128)(2,1)S(1)} %pad_maximum_fusion.2.refs_1_), channel_id=1, source_target_pairs={{0,8},{8,16},{16,24},{1,9},{9,17},{17,25},{2,10},{10,18},{18,26},{... | collective-permute-start | bytes 1572872 | tf_op jit(solution)/shard_map/ppermute | solution.py:333
  27.6 1.2 %pad_maximum_fusion.1.refs_0_ = bf16[4,128,512]{2,1,0:T(8,128)(2,1)S(1)} fusion(bf16[1,128,512]{2,1,0:T(8,128)(2,1)} %bitcast.6, bf16[1,128,512]{2,1,0:T(8,128)(2,1)} %bitcast.5, bf16[1,128,512]{2,1,0:T(8,128)(2,1)} %bitcast.4, bf16[1,128,512]{2,1,0:T(8,128)(2,1)} %bitcast.3), kind=kLoop, calls=%fused_computation.7 | loop fusion | flops 786432 | bytes 1048576 | tf_op jit(solution)/shard_map/stack | solution.py:346
  28.8 4.3 %collective-permute-start.7 = (bf16[4,128,512]{2,1,0:T(8,128)(2,1)S(1)}, bf16[4,128,512]{2,1,0:T(8,128)(2,1)}, u32[]{:S(2)}, u32[]{:S(2)}) collective-permute-start(bf16[4,128,512]{2,1,0:T(8,128)(2,1)S(1)} %pad_maximum_fusion.1.refs_0_), channel_id=1, source_target_pairs={{0,8},{8,16},{16,24},{1,9},{9,17},{17,25},{2,10},{10,18},{18,26},{... | collective-permute-start | bytes 1572872 | tf_op jit(solution)/shard_map/ppermute | solution.py:333
  33.0 6.8 %collective-permute-done.8.refs_3_ = bf16[4,128,512]{2,1,0:T(8,128)(2,1)S(1)} collective-permute-done((bf16[4,128,512]{2,1,0:T(8,128)(2,1)S(1)}, bf16[4,128,512]{2,1,0:T(8,128)(2,1)S(1)}, u32[]{:S(2)}, u32[]{:S(2)}) %collective-permute-start.8) | collective-permute-done | bytes 524320 | tf_op jit(solution)/shard_map/ppermute | solution.py:333
  39.8 10.7 %collective-permute-done.7.refs_2_ = bf16[4,128,512]{2,1,0:T(8,128)(2,1)} collective-permute-done((bf16[4,128,512]{2,1,0:T(8,128)(2,1)S(1)}, bf16[4,128,512]{2,1,0:T(8,128)(2,1)}, u32[]{:S(2)}, u32[]{:S(2)}) %collective-permute-start.7) | collective-permute-done | bytes 524320 | tf_op jit(solution)/shard_map/ppermute | solution.py:333
  50.6 18.4 %shard_map.86 = (bf16[1024,1024]{1,0:T(8,128)(2,1)}, bf16[4,128,512]{2,1,0:T(8,128)(2,1)}, bf16[4,128,512]{2,1,0:T(8,128)(2,1)}, bf16[4,128,512]{2,1,0:T(8,128)(2,1)}, bf16[4,128,512]{2,1,0:T(8,128)(2,1)}) custom-call(s32[8]{0:T(128)} %lengths_ref.1, bf16[1024,1024]{1,0:T(8,128)(2,1)} %bitcast.2.rows_ref, bf16[4,128,512]{2,1,0:T(8,128)(2,1)} %copy-done.3, ...), custom_call_target="tpu_custom_call" | custom-call | flops 16106127360 | bytes 7864320 | tf_op jit(solution)/shard_map/pallas_call | solution.py:288
  69.0 3.9 %all-to-all-start.1 = ((bf16[8,128,1024]{2,1,0:T(8,128)(2,1)}), bf16[8,128,1024]{2,1,0:T(8,128)(2,1)S(1)}, u32[]{:S(2)}, u32[]{:S(2)}) async-start(bf16[8,128,1024]{2,1,0:T(8,128)(2,1)} %bitcast.44), calls=%async_computation.1 | async-start | bytes 4194304 | tf_op jit(solution)/shard_map/all_to_all | solution.py:319
  72.9 1.4 %collective-permute-start.9 = (bf16[4,128,512]{2,1,0:T(8,128)(2,1)S(1)}, bf16[4,128,512]{2,1,0:T(8,128)(2,1)S(1)}, u32[]{:S(2)}, u32[]{:S(2)}) collective-permute-start(bf16[4,128,512]{2,1,0:T(8,128)(2,1)S(1)} %copy-done.6), channel_id=1, source_target_pairs={{8,0},{16,8},{24,16},{9,1},{17,9},{25,17},{10,2},{18,10},{26,18},{... | collective-permute-start | bytes 1572872 | tf_op jit(solution)/shard_map/ppermute | solution.py:333
  74.3 1.3 %collective-permute-start.14 = (bf16[4,128,512]{2,1,0:T(8,128)(2,1)}, bf16[4,128,512]{2,1,0:T(8,128)(2,1)S(1)}, u32[]{:S(2)}, u32[]{:S(2)}) collective-permute-start(bf16[4,128,512]{2,1,0:T(8,128)(2,1)} %get-tuple-element.71), channel_id=1, source_target_pairs={{8,0},{16,8},{24,16},{9,1},{17,9},{25,17},{10,2},{18,10},{26,18},{... | collective-permute-start | bytes 1572872 | tf_op jit(solution)/shard_map/ppermute | solution.py:333
  75.6 14.7 %collective-permute-done.9 = bf16[4,128,512]{2,1,0:T(8,128)(2,1)S(1)} collective-permute-done((bf16[4,128,512]{2,1,0:T(8,128)(2,1)S(1)}, bf16[4,128,512]{2,1,0:T(8,128)(2,1)S(1)}, u32[]{:S(2)}, u32[]{:S(2)}) %collective-permute-start.9) | collective-permute-done | bytes 524320 | tf_op jit(solution)/shard_map/ppermute | solution.py:333
  90.5 2.0 %collective-permute-start.13 = (bf16[128,512]{1,0:T(8,128)(2,1)S(1)}, bf16[128,512]{1,0:T(8,128)(2,1)S(1)}, u32[]{:S(2)}, u32[]{:S(2)}) collective-permute-start(bf16[128,512]{1,0:T(8,128)(2,1)S(1)} %get-tuple-element.90), channel_id=1, source_target_pairs={{0,4},{1,5},{2,6},{3,7},{4,0},{5,1},{6,2},{7,3},{8,12},{9,13},{10,... | collective-permute-start | bytes 393224 | tf_op jit(solution)/shard_map/ppermute | solution.py:326
  92.5 1.5 %collective-permute-start.11 = (bf16[128,512]{1,0:T(8,128)(2,1)S(1)}, bf16[128,512]{1,0:T(8,128)(2,1)S(1)}, u32[]{:S(2)}, u32[]{:S(2)}) collective-permute-start(bf16[128,512]{1,0:T(8,128)(2,1)S(1)} %get-tuple-element.92), channel_id=1, source_target_pairs={{0,6},{1,7},{2,4},{3,5},{4,2},{5,3},{6,0},{7,1},{8,14},{9,15},{10,... | collective-permute-start | bytes 393224 | tf_op jit(solution)/shard_map/ppermute | solution.py:326
  94.0 1.2 %collective-permute-start.10 = (bf16[128,512]{1,0:T(8,128)(2,1)S(1)}, bf16[128,512]{1,0:T(8,128)(2,1)S(1)}, u32[]{:S(2)}, u32[]{:S(2)}) collective-permute-start(bf16[128,512]{1,0:T(8,128)(2,1)S(1)} %get-tuple-element.93), channel_id=1, source_target_pairs={{0,7},{1,6},{2,5},{3,4},{4,3},{5,2},{6,1},{7,0},{8,15},{9,14},{10,... | collective-permute-start | bytes 393224 | tf_op jit(solution)/shard_map/ppermute | solution.py:326
  95.2 6.2 %collective-permute-done.14 = bf16[4,128,512]{2,1,0:T(8,128)(2,1)S(1)} collective-permute-done((bf16[4,128,512]{2,1,0:T(8,128)(2,1)}, bf16[4,128,512]{2,1,0:T(8,128)(2,1)S(1)}, u32[]{:S(2)}, u32[]{:S(2)}) %collective-permute-start.14) | collective-permute-done | bytes 524320 | tf_op jit(solution)/shard_map/ppermute | solution.py:333
  103.1 4.7 %collective-permute-done.13.refs_3_ = bf16[128,512]{1,0:T(8,128)(2,1)S(1)} collective-permute-done((bf16[128,512]{1,0:T(8,128)(2,1)S(1)}, bf16[128,512]{1,0:T(8,128)(2,1)S(1)}, u32[]{:S(2)}, u32[]{:S(2)}) %collective-permute-start.13) | collective-permute-done | bytes 131104 | tf_op jit(solution)/shard_map/ppermute | solution.py:326
  (49 shorter events, 11.3 us)
Async XLA Ops:
  2.5 10.5 %collective-permute-start = (bf16[128,512]{1,0:T(8,128)(2,1)}, bf16[128,512]{1,0:T(8,128)(2,1)}, u32[]{:S(2)}, u32[]{:S(2)}) collective-permute-start(bf16[128,512]{1,0:T(8,128)(2,1)} %get-tuple-element.48), channel_id=1, source_target_pairs={{0,7},{1,6},{2,5},{3,4},{4,3},{5,2},{6,1},{7,0},{8,15},{9,14},{10,... | collective-permute-start | bytes 393224 | tf_op jit(solution)/shard_map/ppermute | solution.py:326
  5.9 7.9 %collective-permute-start.1 = (bf16[128,512]{1,0:T(8,128)(2,1)}, bf16[128,512]{1,0:T(8,128)(2,1)}, u32[]{:S(2)}, u32[]{:S(2)}) collective-permute-start(bf16[128,512]{1,0:T(8,128)(2,1)} %get-tuple-element.49), channel_id=1, source_target_pairs={{0,6},{1,7},{2,4},{3,5},{4,2},{5,3},{6,0},{7,1},{8,14},{9,15},{10,... | collective-permute-start | bytes 393224 | tf_op jit(solution)/shard_map/ppermute | solution.py:326
  6.5 9.3 %collective-permute-start.2 = (bf16[128,512]{1,0:T(8,128)(2,1)}, bf16[128,512]{1,0:T(8,128)(2,1)}, u32[]{:S(2)}, u32[]{:S(2)}) collective-permute-start(bf16[128,512]{1,0:T(8,128)(2,1)} %get-tuple-element.50), channel_id=1, source_target_pairs={{0,5},{1,4},{2,7},{3,6},{4,1},{5,0},{6,3},{7,2},{8,13},{9,12},{10,... | collective-permute-start | bytes 393224 | tf_op jit(solution)/shard_map/ppermute | solution.py:326
  7.9 10.8 %collective-permute-start.3 = (bf16[128,512]{1,0:T(8,128)(2,1)}, bf16[128,512]{1,0:T(8,128)(2,1)}, u32[]{:S(2)}, u32[]{:S(2)}) collective-permute-start(bf16[128,512]{1,0:T(8,128)(2,1)} %get-tuple-element.51), channel_id=1, source_target_pairs={{0,4},{1,5},{2,6},{3,7},{4,0},{5,1},{6,2},{7,3},{8,12},{9,13},{10,... | collective-permute-start | bytes 393224 | tf_op jit(solution)/shard_map/ppermute | solution.py:326
  10.0 8.7 %collective-permute-start.4 = (bf16[128,512]{1,0:T(8,128)(2,1)}, bf16[128,512]{1,0:T(8,128)(2,1)S(1)}, u32[]{:S(2)}, u32[]{:S(2)}) collective-permute-start(bf16[128,512]{1,0:T(8,128)(2,1)} %get-tuple-element.54), channel_id=1, source_target_pairs={{0,3},{1,2},{2,1},{3,0},{4,7},{5,6},{6,5},{7,4},{8,11},{9,10},{10,... | collective-permute-start | bytes 393224 | tf_op jit(solution)/shard_map/ppermute | solution.py:326
  13.0 6.4 %collective-permute-start.5 = (bf16[128,512]{1,0:T(8,128)(2,1)S(1)}, bf16[128,512]{1,0:T(8,128)(2,1)S(1)}, u32[]{:S(2)}, u32[]{:S(2)}) collective-permute-start(bf16[128,512]{1,0:T(8,128)(2,1)S(1)} %copy-done.8), channel_id=1, source_target_pairs={{0,2},{1,3},{2,0},{3,1},{4,6},{5,7},{6,4},{7,5},{8,10},{9,11},{10,... | collective-permute-start | bytes 393224 | tf_op jit(solution)/shard_map/ppermute | solution.py:326
  13.8 5.6 %collective-permute-start.6 = (bf16[128,512]{1,0:T(8,128)(2,1)S(1)}, bf16[128,512]{1,0:T(8,128)(2,1)S(1)}, u32[]{:S(2)}, u32[]{:S(2)}) collective-permute-start(bf16[128,512]{1,0:T(8,128)(2,1)S(1)} %copy-done.7), channel_id=1, source_target_pairs={{0,1},{1,0},{2,3},{3,2},{4,5},{5,4},{6,7},{7,6},{8,9},{9,8},{10,11... | collective-permute-start | bytes 393224 | tf_op jit(solution)/shard_map/ppermute | solution.py:326
  19.4 31.1 %all-to-all-start = ((bf16[8,128,1024]{2,1,0:T(8,128)(2,1)}), bf16[8,128,1024]{2,1,0:T(8,128)(2,1)}, u32[]{:S(2)}, u32[]{:S(2)}) async-start(bf16[8,128,1024]{2,1,0:T(8,128)(2,1)} %pad_maximum_fusion), calls=%async_computation | async-start | bytes 4194304 | tf_op jit(solution)/shard_map/all_to_all | solution.py:319
  24.0 26.6 %copy-start.2 = (bf16[4,128,512]{2,1,0:T(8,128)(2,1)}, bf16[4,128,512]{2,1,0:T(8,128)(2,1)S(1)}, u32[]{:S(2)}) copy-start(bf16[4,128,512]{2,1,0:T(8,128)(2,1)S(1)} %pad_maximum_fusion.2.refs_1_) | copy-start | bytes 1572868
  24.0 15.8 %collective-permute-start.8 = (bf16[4,128,512]{2,1,0:T(8,128)(2,1)S(1)}, bf16[4,128,512]{2,1,0:T(8,128)(2,1)S(1)}, u32[]{:S(2)}, u32[]{:S(2)}) collective-permute-start(bf16[4,128,512]{2,1,0:T(8,128)(2,1)S(1)} %pad_maximum_fusion.2.refs_1_), channel_id=1, source_target_pairs={{0,8},{8,16},{16,24},{1,9},{9,17},{17,25},{2,10},{10,18},{18,26},{... | collective-permute-start | bytes 1572872 | tf_op jit(solution)/shard_map/ppermute | solution.py:333
  28.8 21.8 %copy-start.3 = (bf16[4,128,512]{2,1,0:T(8,128)(2,1)}, bf16[4,128,512]{2,1,0:T(8,128)(2,1)S(1)}, u32[]{:S(2)}) copy-start(bf16[4,128,512]{2,1,0:T(8,128)(2,1)S(1)} %pad_maximum_fusion.1.refs_0_) | copy-start | bytes 1572868
  28.8 21.7 %collective-permute-start.7 = (bf16[4,128,512]{2,1,0:T(8,128)(2,1)S(1)}, bf16[4,128,512]{2,1,0:T(8,128)(2,1)}, u32[]{:S(2)}, u32[]{:S(2)}) collective-permute-start(bf16[4,128,512]{2,1,0:T(8,128)(2,1)S(1)} %pad_maximum_fusion.1.refs_0_), channel_id=1, source_target_pairs={{0,8},{8,16},{16,24},{1,9},{9,17},{17,25},{2,10},{10,18},{18,26},{... | collective-permute-start | bytes 1572872 | tf_op jit(solution)/shard_map/ppermute | solution.py:333
  68.9 21.4 %copy-start.1 = (bf16[4,128,512]{2,1,0:T(8,128)(2,1)S(1)}, bf16[4,128,512]{2,1,0:T(8,128)(2,1)}, u32[]{:S(2)}) copy-start(bf16[4,128,512]{2,1,0:T(8,128)(2,1)} %get-tuple-element.68) | copy-start | bytes 1572868
  69.0 40.7 %all-to-all-start.1 = ((bf16[8,128,1024]{2,1,0:T(8,128)(2,1)}), bf16[8,128,1024]{2,1,0:T(8,128)(2,1)S(1)}, u32[]{:S(2)}, u32[]{:S(2)}) async-start(bf16[8,128,1024]{2,1,0:T(8,128)(2,1)} %bitcast.44), calls=%async_computation.1 | async-start | bytes 4194304 | tf_op jit(solution)/shard_map/all_to_all | solution.py:319
  72.9 28.5 %copy-start = (bf16[4,128,512]{2,1,0:T(8,128)(2,1)S(1)}, bf16[4,128,512]{2,1,0:T(8,128)(2,1)}, u32[]{:S(2)}) copy-start(bf16[4,128,512]{2,1,0:T(8,128)(2,1)} %get-tuple-element.70) | copy-start | bytes 1572868
  72.9 17.4 %collective-permute-start.9 = (bf16[4,128,512]{2,1,0:T(8,128)(2,1)S(1)}, bf16[4,128,512]{2,1,0:T(8,128)(2,1)S(1)}, u32[]{:S(2)}, u32[]{:S(2)}) collective-permute-start(bf16[4,128,512]{2,1,0:T(8,128)(2,1)S(1)} %copy-done.6), channel_id=1, source_target_pairs={{8,0},{16,8},{24,16},{9,1},{17,9},{25,17},{10,2},{18,10},{26,18},{... | collective-permute-start | bytes 1572872 | tf_op jit(solution)/shard_map/ppermute | solution.py:333
  74.3 27.0 %collective-permute-start.14 = (bf16[4,128,512]{2,1,0:T(8,128)(2,1)}, bf16[4,128,512]{2,1,0:T(8,128)(2,1)S(1)}, u32[]{:S(2)}, u32[]{:S(2)}) collective-permute-start(bf16[4,128,512]{2,1,0:T(8,128)(2,1)} %get-tuple-element.71), channel_id=1, source_target_pairs={{8,0},{16,8},{24,16},{9,1},{17,9},{25,17},{10,2},{18,10},{26,18},{... | collective-permute-start | bytes 1572872 | tf_op jit(solution)/shard_map/ppermute | solution.py:333
  90.5 17.4 %collective-permute-start.13 = (bf16[128,512]{1,0:T(8,128)(2,1)S(1)}, bf16[128,512]{1,0:T(8,128)(2,1)S(1)}, u32[]{:S(2)}, u32[]{:S(2)}) collective-permute-start(bf16[128,512]{1,0:T(8,128)(2,1)S(1)} %get-tuple-element.90), channel_id=1, source_target_pairs={{0,4},{1,5},{2,6},{3,7},{4,0},{5,1},{6,2},{7,3},{8,12},{9,13},{10,... | collective-permute-start | bytes 393224 | tf_op jit(solution)/shard_map/ppermute | solution.py:326
  92.5 16.5 %collective-permute-start.12 = (bf16[128,512]{1,0:T(8,128)(2,1)S(1)}, bf16[128,512]{1,0:T(8,128)(2,1)S(1)}, u32[]{:S(2)}, u32[]{:S(2)}) collective-permute-start(bf16[128,512]{1,0:T(8,128)(2,1)S(1)} %get-tuple-element.91), channel_id=1, source_target_pairs={{0,5},{1,4},{2,7},{3,6},{4,1},{5,0},{6,3},{7,2},{8,13},{9,12},{10,... | collective-permute-start | bytes 393224 | tf_op jit(solution)/shard_map/ppermute | solution.py:326
  92.5 19.6 %collective-permute-start.11 = (bf16[128,512]{1,0:T(8,128)(2,1)S(1)}, bf16[128,512]{1,0:T(8,128)(2,1)S(1)}, u32[]{:S(2)}, u32[]{:S(2)}) collective-permute-start(bf16[128,512]{1,0:T(8,128)(2,1)S(1)} %get-tuple-element.92), channel_id=1, source_target_pairs={{0,6},{1,7},{2,4},{3,5},{4,2},{5,3},{6,0},{7,1},{8,14},{9,15},{10,... | collective-permute-start | bytes 393224 | tf_op jit(solution)/shard_map/ppermute | solution.py:326
  94.0 18.1 %collective-permute-start.10 = (bf16[128,512]{1,0:T(8,128)(2,1)S(1)}, bf16[128,512]{1,0:T(8,128)(2,1)S(1)}, u32[]{:S(2)}, u32[]{:S(2)}) collective-permute-start(bf16[128,512]{1,0:T(8,128)(2,1)S(1)} %get-tuple-element.93), channel_id=1, source_target_pairs={{0,7},{1,6},{2,5},{3,4},{4,3},{5,2},{6,1},{7,0},{8,15},{9,14},{10,... | collective-permute-start | bytes 393224 | tf_op jit(solution)/shard_map/ppermute | solution.py:326
  102.2 9.8 %collective-permute-start.17 = (bf16[128,512]{1,0:T(8,128)(2,1)}, bf16[128,512]{1,0:T(8,128)(2,1)S(1)}, u32[]{:S(2)}, u32[]{:S(2)}) collective-permute-start(bf16[128,512]{1,0:T(8,128)(2,1)} %get-tuple-element.86), channel_id=1, source_target_pairs={{0,3},{1,2},{2,1},{3,0},{4,7},{5,6},{6,5},{7,4},{8,11},{9,10},{10,... | collective-permute-start | bytes 393224 | tf_op jit(solution)/shard_map/ppermute | solution.py:326
  107.9 5.2 %collective-permute-start.16 = (bf16[128,512]{1,0:T(8,128)(2,1)}, bf16[128,512]{1,0:T(8,128)(2,1)S(1)}, u32[]{:S(2)}, u32[]{:S(2)}) collective-permute-start(bf16[128,512]{1,0:T(8,128)(2,1)} %get-tuple-element.87), channel_id=1, source_target_pairs={{0,2},{1,3},{2,0},{3,1},{4,6},{5,7},{6,4},{7,5},{8,10},{9,11},{10,... | collective-permute-start | bytes 393224 | tf_op jit(solution)/shard_map/ppermute | solution.py:326
  109.0 4.1 %collective-permute-start.15 = (bf16[128,512]{1,0:T(8,128)(2,1)S(1)}, bf16[128,512]{1,0:T(8,128)(2,1)S(1)}, u32[]{:S(2)}, u32[]{:S(2)}) collective-permute-start(bf16[128,512]{1,0:T(8,128)(2,1)S(1)} %get-tuple-element.88), channel_id=1, source_target_pairs={{0,1},{1,0},{2,3},{3,2},{4,5},{5,4},{6,7},{7,6},{8,9},{9,8},{10,11... | collective-permute-start | bytes 393224 | tf_op jit(solution)/shard_map/ppermute | solution.py:326
  (5 other events, 23.6 us)

commit v4 on v2

--- a/solution.py
+++ b/solution.py
@@ -262,9 +262,10 @@
     cotangents_scaled = scaled(cotangents, shares)
     queries_scaled = scaled(queries, shares)
     for item in range(SPAN):
+        add(item, width, dot(weights[tiles[item]], cotangents_scaled, (1, 0)))
+    for item in range(SPAN):
         weigh_grad(0, item, deltas[0])
         weigh_grad(1, item, deltas[1])
-        add(item, width, dot(weights[tiles[item]], cotangents_scaled, (1, 0)))
         add(item, 0, dot(grad_weights[tiles[item]], queries_scaled, (1, 0)))
     make_query_grad(0, shares[0])
     make_query_grad(1, shares[1])

time: 113 us -> 114 us (level)
  no operation moved by 1% of the time
where the time goes in v4:
time: 114 us; the launch traced here: 113 us
  waiting for transfers between devices  48.4 us (42%)
  starting transfers between devices  33.6 us (29%)
  Pallas kernels  22.2 us (19%)
  local copies, waits for them, and re-layouts  5.01 us (4%)
  other arithmetic  3.1 us (3%)
    ppermute x4, waiting for transfers between devices, onward(): return lax.ppermute(block, 'stretch', route)  38.3 us
    pallas_call x1, Pallas kernels, attention(): pl.pallas_call(attention_kernel, grid=(TILES,), in_specs=[SCALARS, rows_b...  17.4 us
    ppermute x14, starting transfers between devices, swapped(): moved.append(lax.ppermute(piece, 'member', route) if distance else piece)  14.7 us
    ppermute x4, starting transfers between devices, onward(): return lax.ppermute(block, 'stretch', route)  10.5 us
    ppermute x14, waiting for transfers between devices, swapped(): moved.append(lax.ppermute(piece, 'member', route) if distance else piece)  10.1 us
    all_to_all x2, starting transfers between devices, exchanged(): lax.all_to_all(blocks, 'member', split_axis=0, concat_axis=0, tiled=True)  8.41 us
    pallas_call x2, Pallas kernels, pack(): pl.pallas_call(functools.partial(pack_kernel, distances), in_specs=[IN_HB...  3.67 us
  transfers between devices with their start and end apart: 20, of which 11 were waited for; matrix products, arithmetic and copies ran while one was open for 7% of the time, Pallas kernels for 2%

profile of v4, /device:TPU:0, one launch (start us, length us, event | category | flops | bytes accessed | tf_op | source)
XLA Modules:
  0.0 113.2 jit_solution(1944259671005631777)
XLA Ops:
  0.6 1.8 %shard_map.84 = (bf16[128,512]{1,0:T(8,128)(2,1)}, bf16[128,512]{1,0:T(8,128)(2,1)}, bf16[128,512]{1,0:T(8,128)(2,1)}, bf16[128,512]{1,0:T(8,128)(2,1)}) custom-call(bf16[128,2048]{1,0:T(8,128)(2,1)} %left_ref.2, bf16[128,2048]{1,0:T(8,128)(2,1)} %right_ref.2), custom_call_target="tpu_custom_call" | custom-call | bytes 1048576 | tf_op jit(solution)/shard_map/pallas_call | solution.py:85
  2.5 3.4 %collective-permute-start = (bf16[128,512]{1,0:T(8,128)(2,1)}, bf16[128,512]{1,0:T(8,128)(2,1)}, u32[]{:S(2)}, u32[]{:S(2)}) collective-permute-start(bf16[128,512]{1,0:T(8,128)(2,1)} %get-tuple-element.48), channel_id=1, source_target_pairs={{0,7},{1,6},{2,5},{3,4},{4,3},{5,2},{6,1},{7,0},{8,15},{9,14},{10,... | collective-permute-start | bytes 393224 | tf_op jit(solution)/shard_map/ppermute | solution.py:329
  6.5 1.4 %collective-permute-start.2 = (bf16[128,512]{1,0:T(8,128)(2,1)}, bf16[128,512]{1,0:T(8,128)(2,1)}, u32[]{:S(2)}, u32[]{:S(2)}) collective-permute-start(bf16[128,512]{1,0:T(8,128)(2,1)} %get-tuple-element.50), channel_id=1, source_target_pairs={{0,5},{1,4},{2,7},{3,6},{4,1},{5,0},{6,3},{7,2},{8,13},{9,12},{10,... | collective-permute-start | bytes 393224 | tf_op jit(solution)/shard_map/ppermute | solution.py:329
  8.2 1.8 %shard_map.85 = (bf16[128,512]{1,0:T(8,128)(2,1)}, bf16[128,512]{1,0:T(8,128)(2,1)}, bf16[128,512]{1,0:T(8,128)(2,1)}, bf16[128,512]{1,0:T(8,128)(2,1)}) custom-call(bf16[128,2048]{1,0:T(8,128)(2,1)} %left_ref.2, bf16[128,2048]{1,0:T(8,128)(2,1)} %right_ref.2), custom_call_target="tpu_custom_call" | custom-call | bytes 1048576 | tf_op jit(solution)/shard_map/pallas_call | solution.py:85
  10.0 1.2 %collective-permute-start.4 = (bf16[128,512]{1,0:T(8,128)(2,1)}, bf16[128,512]{1,0:T(8,128)(2,1)S(1)}, u32[]{:S(2)}, u32[]{:S(2)}) collective-permute-start(bf16[128,512]{1,0:T(8,128)(2,1)} %get-tuple-element.54), channel_id=1, source_target_pairs={{0,3},{1,2},{2,1},{3,0},{4,7},{5,6},{6,5},{7,4},{8,11},{9,10},{10,... | collective-permute-start | bytes 393224 | tf_op jit(solution)/shard_map/ppermute | solution.py:329
  11.2 1.8 %bitcast_bitcast_fusion = (bf16[8,128,512]{2,1,0:T(8,128)(2,1)S(1)}, bf16[8,128,512]{2,1,0:T(8,128)(2,1)S(1)}) fusion(bf16[16,8,8,512]{3,2,1,0:T(8,128)(2,1)} %bitcast.47, bf16[16,8,8,512]{3,2,1,0:T(8,128)(2,1)} %bitcast.48), kind=kLoop, calls=%fused_computation.1 | loop fusion | bytes 4194304 | tf_op jit(solution)/shard_map/transpose | solution.py:314
  13.9 1.6 %pad_maximum_fusion = bf16[8,128,1024]{2,1,0:T(8,128)(2,1)} fusion(bf16[8,128,512]{2,1,0:T(8,128)(2,1)S(1)} %get-tuple-element.94, bf16[8,128,512]{2,1,0:T(8,128)(2,1)S(1)} %get-tuple-element.95), kind=kLoop, calls=%fused_computation | loop fusion | flops 4194304 | bytes 4194304 | tf_op jit(solution)/shard_map/concatenate | solution.py:347
  15.8 2.8 %collective-permute-done.3 = bf16[128,512]{1,0:T(8,128)(2,1)} collective-permute-done((bf16[128,512]{1,0:T(8,128)(2,1)}, bf16[128,512]{1,0:T(8,128)(2,1)}, u32[]{:S(2)}, u32[]{:S(2)}) %collective-permute-start.3) | collective-permute-done | bytes 131104 | tf_op jit(solution)/shard_map/ppermute | solution.py:329
  19.4 4.5 %all-to-all-start = ((bf16[8,128,1024]{2,1,0:T(8,128)(2,1)}), bf16[8,128,1024]{2,1,0:T(8,128)(2,1)}, u32[]{:S(2)}, u32[]{:S(2)}) async-start(bf16[8,128,1024]{2,1,0:T(8,128)(2,1)} %pad_maximum_fusion), calls=%async_computation | async-start | bytes 4194304 | tf_op jit(solution)/shard_map/all_to_all | solution.py:322
  24.0 3.6 %collective-permute-start.8 = (bf16[4,128,512]{2,1,0:T(8,128)(2,1)S(1)}, bf16[4,128,512]{2,1,0:T(8,128)(2,1)S(1)}, u32[]{:S(2)}, u32[]{:S(2)}) collective-permute-start(bf16[4,128,512]{2,1,0:T(8,128)(2,1)S(1)} %pad_maximum_fusion.2.refs_1_), channel_id=1, source_target_pairs={{0,8},{8,16},{16,24},{1,9},{9,17},{17,25},{2,10},{10,18},{18,26},{... | collective-permute-start | bytes 1572872 | tf_op jit(solution)/shard_map/ppermute | solution.py:336
  27.6 1.2 %pad_maximum_fusion.1.refs_0_ = bf16[4,128,512]{2,1,0:T(8,128)(2,1)S(1)} fusion(bf16[1,128,512]{2,1,0:T(8,128)(2,1)} %bitcast.6, bf16[1,128,512]{2,1,0:T(8,128)(2,1)} %bitcast.5, bf16[1,128,512]{2,1,0:T(8,128)(2,1)} %bitcast.4, bf16[1,128,512]{2,1,0:T(8,128)(2,1)} %bitcast.3), kind=kLoop, calls=%fused_computation.7 | loop fusion | flops 786432 | bytes 1048576 | tf_op jit(solution)/shard_map/stack | solution.py:349
  28.8 4.3 %collective-permute-start.7 = (bf16[4,128,512]{2,1,0:T(8,128)(2,1)S(1)}, bf16[4,128,512]{2,1,0:T(8,128)(2,1)}, u32[]{:S(2)}, u32[]{:S(2)}) collective-permute-start(bf16[4,128,512]{2,1,0:T(8,128)(2,1)S(1)} %pad_maximum_fusion.1.refs_0_), channel_id=1, source_target_pairs={{0,8},{8,16},{16,24},{1,9},{9,17},{17,25},{2,10},{10,18},{18,26},{... | collective-permute-start | bytes 1572872 | tf_op jit(solution)/shard_map/ppermute | solution.py:336
  33.0 6.8 %collective-permute-done.8.refs_3_ = bf16[4,128,512]{2,1,0:T(8,128)(2,1)S(1)} collective-permute-done((bf16[4,128,512]{2,1,0:T(8,128)(2,1)S(1)}, bf16[4,128,512]{2,1,0:T(8,128)(2,1)S(1)}, u32[]{:S(2)}, u32[]{:S(2)}) %collective-permute-start.8) | collective-permute-done | bytes 524320 | tf_op jit(solution)/shard_map/ppermute | solution.py:336
  39.8 10.7 %collective-permute-done.7.refs_2_ = bf16[4,128,512]{2,1,0:T(8,128)(2,1)} collective-permute-done((bf16[4,128,512]{2,1,0:T(8,128)(2,1)S(1)}, bf16[4,128,512]{2,1,0:T(8,128)(2,1)}, u32[]{:S(2)}, u32[]{:S(2)}) %collective-permute-start.7) | collective-permute-done | bytes 524320 | tf_op jit(solution)/shard_map/ppermute | solution.py:336
  50.6 17.4 %shard_map.86 = (bf16[1024,1024]{1,0:T(8,128)(2,1)}, bf16[4,128,512]{2,1,0:T(8,128)(2,1)}, bf16[4,128,512]{2,1,0:T(8,128)(2,1)}, bf16[4,128,512]{2,1,0:T(8,128)(2,1)}, bf16[4,128,512]{2,1,0:T(8,128)(2,1)}) custom-call(s32[8]{0:T(128)} %lengths_ref.1, bf16[1024,1024]{1,0:T(8,128)(2,1)} %bitcast.2.rows_ref, bf16[4,128,512]{2,1,0:T(8,128)(2,1)} %copy-done.3, ...), custom_call_target="tpu_custom_call" | custom-call | flops 16106127360 | bytes 7864320 | tf_op jit(solution)/shard_map/pallas_call | solution.py:291
  68.0 3.9 %all-to-all-start.1 = ((bf16[8,128,1024]{2,1,0:T(8,128)(2,1)}), bf16[8,128,1024]{2,1,0:T(8,128)(2,1)S(1)}, u32[]{:S(2)}, u32[]{:S(2)}) async-start(bf16[8,128,1024]{2,1,0:T(8,128)(2,1)} %bitcast.44), calls=%async_computation.1 | async-start | bytes 4194304 | tf_op jit(solution)/shard_map/all_to_all | solution.py:322
  71.9 1.4 %collective-permute-start.9 = (bf16[4,128,512]{2,1,0:T(8,128)(2,1)S(1)}, bf16[4,128,512]{2,1,0:T(8,128)(2,1)S(1)}, u32[]{:S(2)}, u32[]{:S(2)}) collective-permute-start(bf16[4,128,512]{2,1,0:T(8,128)(2,1)S(1)} %copy-done.6), channel_id=1, source_target_pairs={{8,0},{16,8},{24,16},{9,1},{17,9},{25,17},{10,2},{18,10},{26,18},{... | collective-permute-start | bytes 1572872 | tf_op jit(solution)/shard_map/ppermute | solution.py:336
  73.4 1.3 %collective-permute-start.14 = (bf16[4,128,512]{2,1,0:T(8,128)(2,1)}, bf16[4,128,512]{2,1,0:T(8,128)(2,1)S(1)}, u32[]{:S(2)}, u32[]{:S(2)}) collective-permute-start(bf16[4,128,512]{2,1,0:T(8,128)(2,1)} %get-tuple-element.71), channel_id=1, source_target_pairs={{8,0},{16,8},{24,16},{9,1},{17,9},{25,17},{10,2},{18,10},{26,18},{... | collective-permute-start | bytes 1572872 | tf_op jit(solution)/shard_map/ppermute | solution.py:336
  74.7 14.7 %collective-permute-done.9 = bf16[4,128,512]{2,1,0:T(8,128)(2,1)S(1)} collective-permute-done((bf16[4,128,512]{2,1,0:T(8,128)(2,1)S(1)}, bf16[4,128,512]{2,1,0:T(8,128)(2,1)S(1)}, u32[]{:S(2)}, u32[]{:S(2)}) %collective-permute-start.9) | collective-permute-done | bytes 524320 | tf_op jit(solution)/shard_map/ppermute | solution.py:336
  89.5 2.0 %collective-permute-start.13 = (bf16[128,512]{1,0:T(8,128)(2,1)S(1)}, bf16[128,512]{1,0:T(8,128)(2,1)S(1)}, u32[]{:S(2)}, u32[]{:S(2)}) collective-permute-start(bf16[128,512]{1,0:T(8,128)(2,1)S(1)} %get-tuple-element.90), channel_id=1, source_target_pairs={{0,4},{1,5},{2,6},{3,7},{4,0},{5,1},{6,2},{7,3},{8,12},{9,13},{10,... | collective-permute-start | bytes 393224 | tf_op jit(solution)/shard_map/ppermute | solution.py:329
  91.5 1.5 %collective-permute-start.11 = (bf16[128,512]{1,0:T(8,128)(2,1)S(1)}, bf16[128,512]{1,0:T(8,128)(2,1)S(1)}, u32[]{:S(2)}, u32[]{:S(2)}) collective-permute-start(bf16[128,512]{1,0:T(8,128)(2,1)S(1)} %get-tuple-element.92), channel_id=1, source_target_pairs={{0,6},{1,7},{2,4},{3,5},{4,2},{5,3},{6,0},{7,1},{8,14},{9,15},{10,... | collective-permute-start | bytes 393224 | tf_op jit(solution)/shard_map/ppermute | solution.py:329
  93.0 1.2 %collective-permute-start.10 = (bf16[128,512]{1,0:T(8,128)(2,1)S(1)}, bf16[128,512]{1,0:T(8,128)(2,1)S(1)}, u32[]{:S(2)}, u32[]{:S(2)}) collective-permute-start(bf16[128,512]{1,0:T(8,128)(2,1)S(1)} %get-tuple-element.93), channel_id=1, source_target_pairs={{0,7},{1,6},{2,5},{3,4},{4,3},{5,2},{6,1},{7,0},{8,15},{9,14},{10,... | collective-permute-start | bytes 393224 | tf_op jit(solution)/shard_map/ppermute | solution.py:329
  94.2 6.2 %collective-permute-done.14 = bf16[4,128,512]{2,1,0:T(8,128)(2,1)S(1)} collective-permute-done((bf16[4,128,512]{2,1,0:T(8,128)(2,1)}, bf16[4,128,512]{2,1,0:T(8,128)(2,1)S(1)}, u32[]{:S(2)}, u32[]{:S(2)}) %collective-permute-start.14) | collective-permute-done | bytes 524320 | tf_op jit(solution)/shard_map/ppermute | solution.py:336
  102.2 4.7 %collective-permute-done.13.refs_3_ = bf16[128,512]{1,0:T(8,128)(2,1)S(1)} collective-permute-done((bf16[128,512]{1,0:T(8,128)(2,1)S(1)}, bf16[128,512]{1,0:T(8,128)(2,1)S(1)}, u32[]{:S(2)}, u32[]{:S(2)}) %collective-permute-start.13) | collective-permute-done | bytes 131104 | tf_op jit(solution)/shard_map/ppermute | solution.py:329
  (49 shorter events, 11.3 us)
Async XLA Ops:
  2.5 10.5 %collective-permute-start = (bf16[128,512]{1,0:T(8,128)(2,1)}, bf16[128,512]{1,0:T(8,128)(2,1)}, u32[]{:S(2)}, u32[]{:S(2)}) collective-permute-start(bf16[128,512]{1,0:T(8,128)(2,1)} %get-tuple-element.48), channel_id=1, source_target_pairs={{0,7},{1,6},{2,5},{3,4},{4,3},{5,2},{6,1},{7,0},{8,15},{9,14},{10,... | collective-permute-start | bytes 393224 | tf_op jit(solution)/shard_map/ppermute | solution.py:329
  5.9 7.9 %collective-permute-start.1 = (bf16[128,512]{1,0:T(8,128)(2,1)}, bf16[128,512]{1,0:T(8,128)(2,1)}, u32[]{:S(2)}, u32[]{:S(2)}) collective-permute-start(bf16[128,512]{1,0:T(8,128)(2,1)} %get-tuple-element.49), channel_id=1, source_target_pairs={{0,6},{1,7},{2,4},{3,5},{4,2},{5,3},{6,0},{7,1},{8,14},{9,15},{10,... | collective-permute-start | bytes 393224 | tf_op jit(solution)/shard_map/ppermute | solution.py:329
  6.5 9.3 %collective-permute-start.2 = (bf16[128,512]{1,0:T(8,128)(2,1)}, bf16[128,512]{1,0:T(8,128)(2,1)}, u32[]{:S(2)}, u32[]{:S(2)}) collective-permute-start(bf16[128,512]{1,0:T(8,128)(2,1)} %get-tuple-element.50), channel_id=1, source_target_pairs={{0,5},{1,4},{2,7},{3,6},{4,1},{5,0},{6,3},{7,2},{8,13},{9,12},{10,... | collective-permute-start | bytes 393224 | tf_op jit(solution)/shard_map/ppermute | solution.py:329
  7.9 10.8 %collective-permute-start.3 = (bf16[128,512]{1,0:T(8,128)(2,1)}, bf16[128,512]{1,0:T(8,128)(2,1)}, u32[]{:S(2)}, u32[]{:S(2)}) collective-permute-start(bf16[128,512]{1,0:T(8,128)(2,1)} %get-tuple-element.51), channel_id=1, source_target_pairs={{0,4},{1,5},{2,6},{3,7},{4,0},{5,1},{6,2},{7,3},{8,12},{9,13},{10,... | collective-permute-start | bytes 393224 | tf_op jit(solution)/shard_map/ppermute | solution.py:329
  10.0 8.7 %collective-permute-start.4 = (bf16[128,512]{1,0:T(8,128)(2,1)}, bf16[128,512]{1,0:T(8,128)(2,1)S(1)}, u32[]{:S(2)}, u32[]{:S(2)}) collective-permute-start(bf16[128,512]{1,0:T(8,128)(2,1)} %get-tuple-element.54), channel_id=1, source_target_pairs={{0,3},{1,2},{2,1},{3,0},{4,7},{5,6},{6,5},{7,4},{8,11},{9,10},{10,... | collective-permute-start | bytes 393224 | tf_op jit(solution)/shard_map/ppermute | solution.py:329
  13.0 6.4 %collective-permute-start.5 = (bf16[128,512]{1,0:T(8,128)(2,1)S(1)}, bf16[128,512]{1,0:T(8,128)(2,1)S(1)}, u32[]{:S(2)}, u32[]{:S(2)}) collective-permute-start(bf16[128,512]{1,0:T(8,128)(2,1)S(1)} %copy-done.8), channel_id=1, source_target_pairs={{0,2},{1,3},{2,0},{3,1},{4,6},{5,7},{6,4},{7,5},{8,10},{9,11},{10,... | collective-permute-start | bytes 393224 | tf_op jit(solution)/shard_map/ppermute | solution.py:329
  13.8 5.6 %collective-permute-start.6 = (bf16[128,512]{1,0:T(8,128)(2,1)S(1)}, bf16[128,512]{1,0:T(8,128)(2,1)S(1)}, u32[]{:S(2)}, u32[]{:S(2)}) collective-permute-start(bf16[128,512]{1,0:T(8,128)(2,1)S(1)} %copy-done.7), channel_id=1, source_target_pairs={{0,1},{1,0},{2,3},{3,2},{4,5},{5,4},{6,7},{7,6},{8,9},{9,8},{10,11... | collective-permute-start | bytes 393224 | tf_op jit(solution)/shard_map/ppermute | solution.py:329
  19.4 31.1 %all-to-all-start = ((bf16[8,128,1024]{2,1,0:T(8,128)(2,1)}), bf16[8,128,1024]{2,1,0:T(8,128)(2,1)}, u32[]{:S(2)}, u32[]{:S(2)}) async-start(bf16[8,128,1024]{2,1,0:T(8,128)(2,1)} %pad_maximum_fusion), calls=%async_computation | async-start | bytes 4194304 | tf_op jit(solution)/shard_map/all_to_all | solution.py:322
  24.0 26.6 %copy-start.2 = (bf16[4,128,512]{2,1,0:T(8,128)(2,1)}, bf16[4,128,512]{2,1,0:T(8,128)(2,1)S(1)}, u32[]{:S(2)}) copy-start(bf16[4,128,512]{2,1,0:T(8,128)(2,1)S(1)} %pad_maximum_fusion.2.refs_1_) | copy-start | bytes 1572868
  24.0 15.8 %collective-permute-start.8 = (bf16[4,128,512]{2,1,0:T(8,128)(2,1)S(1)}, bf16[4,128,512]{2,1,0:T(8,128)(2,1)S(1)}, u32[]{:S(2)}, u32[]{:S(2)}) collective-permute-start(bf16[4,128,512]{2,1,0:T(8,128)(2,1)S(1)} %pad_maximum_fusion.2.refs_1_), channel_id=1, source_target_pairs={{0,8},{8,16},{16,24},{1,9},{9,17},{17,25},{2,10},{10,18},{18,26},{... | collective-permute-start | bytes 1572872 | tf_op jit(solution)/shard_map/ppermute | solution.py:336
  28.8 21.8 %copy-start.3 = (bf16[4,128,512]{2,1,0:T(8,128)(2,1)}, bf16[4,128,512]{2,1,0:T(8,128)(2,1)S(1)}, u32[]{:S(2)}) copy-start(bf16[4,128,512]{2,1,0:T(8,128)(2,1)S(1)} %pad_maximum_fusion.1.refs_0_) | copy-start | bytes 1572868
  28.8 21.7 %collective-permute-start.7 = (bf16[4,128,512]{2,1,0:T(8,128)(2,1)S(1)}, bf16[4,128,512]{2,1,0:T(8,128)(2,1)}, u32[]{:S(2)}, u32[]{:S(2)}) collective-permute-start(bf16[4,128,512]{2,1,0:T(8,128)(2,1)S(1)} %pad_maximum_fusion.1.refs_0_), channel_id=1, source_target_pairs={{0,8},{8,16},{16,24},{1,9},{9,17},{17,25},{2,10},{10,18},{18,26},{... | collective-permute-start | bytes 1572872 | tf_op jit(solution)/shard_map/ppermute | solution.py:336
  68.0 21.4 %copy-start.1 = (bf16[4,128,512]{2,1,0:T(8,128)(2,1)S(1)}, bf16[4,128,512]{2,1,0:T(8,128)(2,1)}, u32[]{:S(2)}) copy-start(bf16[4,128,512]{2,1,0:T(8,128)(2,1)} %get-tuple-element.68) | copy-start | bytes 1572868
  68.0 40.7 %all-to-all-start.1 = ((bf16[8,128,1024]{2,1,0:T(8,128)(2,1)}), bf16[8,128,1024]{2,1,0:T(8,128)(2,1)S(1)}, u32[]{:S(2)}, u32[]{:S(2)}) async-start(bf16[8,128,1024]{2,1,0:T(8,128)(2,1)} %bitcast.44), calls=%async_computation.1 | async-start | bytes 4194304 | tf_op jit(solution)/shard_map/all_to_all | solution.py:322
  71.9 28.5 %copy-start = (bf16[4,128,512]{2,1,0:T(8,128)(2,1)S(1)}, bf16[4,128,512]{2,1,0:T(8,128)(2,1)}, u32[]{:S(2)}) copy-start(bf16[4,128,512]{2,1,0:T(8,128)(2,1)} %get-tuple-element.70) | copy-start | bytes 1572868
  71.9 17.4 %collective-permute-start.9 = (bf16[4,128,512]{2,1,0:T(8,128)(2,1)S(1)}, bf16[4,128,512]{2,1,0:T(8,128)(2,1)S(1)}, u32[]{:S(2)}, u32[]{:S(2)}) collective-permute-start(bf16[4,128,512]{2,1,0:T(8,128)(2,1)S(1)} %copy-done.6), channel_id=1, source_target_pairs={{8,0},{16,8},{24,16},{9,1},{17,9},{25,17},{10,2},{18,10},{26,18},{... | collective-permute-start | bytes 1572872 | tf_op jit(solution)/shard_map/ppermute | solution.py:336
  73.4 27.0 %collective-permute-start.14 = (bf16[4,128,512]{2,1,0:T(8,128)(2,1)}, bf16[4,128,512]{2,1,0:T(8,128)(2,1)S(1)}, u32[]{:S(2)}, u32[]{:S(2)}) collective-permute-start(bf16[4,128,512]{2,1,0:T(8,128)(2,1)} %get-tuple-element.71), channel_id=1, source_target_pairs={{8,0},{16,8},{24,16},{9,1},{17,9},{25,17},{10,2},{18,10},{26,18},{... | collective-permute-start | bytes 1572872 | tf_op jit(solution)/shard_map/ppermute | solution.py:336
  89.5 17.4 %collective-permute-start.13 = (bf16[128,512]{1,0:T(8,128)(2,1)S(1)}, bf16[128,512]{1,0:T(8,128)(2,1)S(1)}, u32[]{:S(2)}, u32[]{:S(2)}) collective-permute-start(bf16[128,512]{1,0:T(8,128)(2,1)S(1)} %get-tuple-element.90), channel_id=1, source_target_pairs={{0,4},{1,5},{2,6},{3,7},{4,0},{5,1},{6,2},{7,3},{8,12},{9,13},{10,... | collective-permute-start | bytes 393224 | tf_op jit(solution)/shard_map/ppermute | solution.py:329
  91.5 16.5 %collective-permute-start.12 = (bf16[128,512]{1,0:T(8,128)(2,1)S(1)}, bf16[128,512]{1,0:T(8,128)(2,1)S(1)}, u32[]{:S(2)}, u32[]{:S(2)}) collective-permute-start(bf16[128,512]{1,0:T(8,128)(2,1)S(1)} %get-tuple-element.91), channel_id=1, source_target_pairs={{0,5},{1,4},{2,7},{3,6},{4,1},{5,0},{6,3},{7,2},{8,13},{9,12},{10,... | collective-permute-start | bytes 393224 | tf_op jit(solution)/shard_map/ppermute | solution.py:329
  91.5 19.6 %collective-permute-start.11 = (bf16[128,512]{1,0:T(8,128)(2,1)S(1)}, bf16[128,512]{1,0:T(8,128)(2,1)S(1)}, u32[]{:S(2)}, u32[]{:S(2)}) collective-permute-start(bf16[128,512]{1,0:T(8,128)(2,1)S(1)} %get-tuple-element.92), channel_id=1, source_target_pairs={{0,6},{1,7},{2,4},{3,5},{4,2},{5,3},{6,0},{7,1},{8,14},{9,15},{10,... | collective-permute-start | bytes 393224 | tf_op jit(solution)/shard_map/ppermute | solution.py:329
  93.0 18.1 %collective-permute-start.10 = (bf16[128,512]{1,0:T(8,128)(2,1)S(1)}, bf16[128,512]{1,0:T(8,128)(2,1)S(1)}, u32[]{:S(2)}, u32[]{:S(2)}) collective-permute-start(bf16[128,512]{1,0:T(8,128)(2,1)S(1)} %get-tuple-element.93), channel_id=1, source_target_pairs={{0,7},{1,6},{2,5},{3,4},{4,3},{5,2},{6,1},{7,0},{8,15},{9,14},{10,... | collective-permute-start | bytes 393224 | tf_op jit(solution)/shard_map/ppermute | solution.py:329
  101.3 9.8 %collective-permute-start.17 = (bf16[128,512]{1,0:T(8,128)(2,1)}, bf16[128,512]{1,0:T(8,128)(2,1)S(1)}, u32[]{:S(2)}, u32[]{:S(2)}) collective-permute-start(bf16[128,512]{1,0:T(8,128)(2,1)} %get-tuple-element.86), channel_id=1, source_target_pairs={{0,3},{1,2},{2,1},{3,0},{4,7},{5,6},{6,5},{7,4},{8,11},{9,10},{10,... | collective-permute-start | bytes 393224 | tf_op jit(solution)/shard_map/ppermute | solution.py:329
  106.9 5.2 %collective-permute-start.16 = (bf16[128,512]{1,0:T(8,128)(2,1)}, bf16[128,512]{1,0:T(8,128)(2,1)S(1)}, u32[]{:S(2)}, u32[]{:S(2)}) collective-permute-start(bf16[128,512]{1,0:T(8,128)(2,1)} %get-tuple-element.87), channel_id=1, source_target_pairs={{0,2},{1,3},{2,0},{3,1},{4,6},{5,7},{6,4},{7,5},{8,10},{9,11},{10,... | collective-permute-start | bytes 393224 | tf_op jit(solution)/shard_map/ppermute | solution.py:329
  108.0 4.1 %collective-permute-start.15 = (bf16[128,512]{1,0:T(8,128)(2,1)S(1)}, bf16[128,512]{1,0:T(8,128)(2,1)S(1)}, u32[]{:S(2)}, u32[]{:S(2)}) collective-permute-start(bf16[128,512]{1,0:T(8,128)(2,1)S(1)} %get-tuple-element.88), channel_id=1, source_target_pairs={{0,1},{1,0},{2,3},{3,2},{4,5},{5,4},{6,7},{7,6},{8,9},{9,8},{10,11... | collective-permute-start | bytes 393224 | tf_op jit(solution)/shard_map/ppermute | solution.py:329
  (5 other events, 23.6 us)

commit v5 on v2

--- a/solution.py
+++ b/solution.py
@@ -260,7 +260,7 @@
     shares.append(1.0 / totals[1])
     deltas.append(attend(1, shares[1]))
     cotangents_scaled = scaled(cotangents, shares)
-    queries_scaled = scaled(queries, shares)
+    queries_scaled = scaled(queries, [share * SCORE_SCALE for share in shares])
     for item in range(SPAN):
         weigh_grad(0, item, deltas[0])
         weigh_grad(1, item, deltas[1])
@@ -275,10 +275,7 @@
             half, part, chunk = item // HALF, item % HALF, member ^ distance
             for halves, place in ((earlier_grads, chunk), (own_grads, MEMBERS + chunk)):
                 target = halves[half]
-                target[part, :, :width] = (sums[place, :, :width] * SCORE_SCALE).astype(
-                    jnp.bfloat16
-                )
-                target[part, :, width:] = sums[place, :, width:].astype(jnp.bfloat16)
+                target[part] = sums[place].astype(jnp.bfloat16)
 
 
 def attention(doc_lengths, rows, own, earlier):

time: 113 us -> 113 us (level)
  no operation moved by 1% of the time
where the time goes in v5:
time: 113 us
  waiting for transfers between devices  48.4 us (43%)
  starting transfers between devices  33.6 us (30%)
  Pallas kernels  21.7 us (19%)
  local copies, waits for them, and re-layouts  5.01 us (4%)
  other arithmetic  3.1 us (3%)
    ppermute x4, waiting for transfers between devices, onward(): return lax.ppermute(block, 'stretch', route)  38.3 us
    pallas_call x1, Pallas kernels, attention(): pl.pallas_call(attention_kernel, grid=(TILES,), in_specs=[SCALARS, rows_b...  17 us
    ppermute x14, starting transfers between devices, swapped(): moved.append(lax.ppermute(piece, 'member', route) if distance else piece)  14.7 us
    ppermute x4, starting transfers between devices, onward(): return lax.ppermute(block, 'stretch', route)  10.5 us
    ppermute x14, waiting for transfers between devices, swapped(): moved.append(lax.ppermute(piece, 'member', route) if distance else piece)  10.1 us
    all_to_all x2, starting transfers between devices, exchanged(): lax.all_to_all(blocks, 'member', split_axis=0, concat_axis=0, tiled=True)  8.4 us
    pallas_call x2, Pallas kernels, pack(): pl.pallas_call(functools.partial(pack_kernel, distances), in_specs=[IN_HB...  3.67 us
  transfers between devices with their start and end apart: 20, of which 11 were waited for; matrix products, arithmetic and copies ran while one was open for 7% of the time, Pallas kernels for 2%

profile of v5, /device:TPU:0, one launch (start us, length us, event | category | flops | bytes accessed | tf_op | source)
XLA Modules:
  0.0 112.7 jit_solution(15810132298826518347)
XLA Ops:
  0.6 1.8 %shard_map.84 = (bf16[128,512]{1,0:T(8,128)(2,1)}, bf16[128,512]{1,0:T(8,128)(2,1)}, bf16[128,512]{1,0:T(8,128)(2,1)}, bf16[128,512]{1,0:T(8,128)(2,1)}) custom-call(bf16[128,2048]{1,0:T(8,128)(2,1)} %left_ref.2, bf16[128,2048]{1,0:T(8,128)(2,1)} %right_ref.2), custom_call_target="tpu_custom_call" | custom-call | bytes 1048576 | tf_op jit(solution)/shard_map/pallas_call | solution.py:85
  2.5 3.4 %collective-permute-start = (bf16[128,512]{1,0:T(8,128)(2,1)}, bf16[128,512]{1,0:T(8,128)(2,1)}, u32[]{:S(2)}, u32[]{:S(2)}) collective-permute-start(bf16[128,512]{1,0:T(8,128)(2,1)} %get-tuple-element.48), channel_id=1, source_target_pairs={{0,7},{1,6},{2,5},{3,4},{4,3},{5,2},{6,1},{7,0},{8,15},{9,14},{10,... | collective-permute-start | bytes 393224 | tf_op jit(solution)/shard_map/ppermute | solution.py:325
  6.5 1.4 %collective-permute-start.2 = (bf16[128,512]{1,0:T(8,128)(2,1)}, bf16[128,512]{1,0:T(8,128)(2,1)}, u32[]{:S(2)}, u32[]{:S(2)}) collective-permute-start(bf16[128,512]{1,0:T(8,128)(2,1)} %get-tuple-element.50), channel_id=1, source_target_pairs={{0,5},{1,4},{2,7},{3,6},{4,1},{5,0},{6,3},{7,2},{8,13},{9,12},{10,... | collective-permute-start | bytes 393224 | tf_op jit(solution)/shard_map/ppermute | solution.py:325
  8.2 1.8 %shard_map.85 = (bf16[128,512]{1,0:T(8,128)(2,1)}, bf16[128,512]{1,0:T(8,128)(2,1)}, bf16[128,512]{1,0:T(8,128)(2,1)}, bf16[128,512]{1,0:T(8,128)(2,1)}) custom-call(bf16[128,2048]{1,0:T(8,128)(2,1)} %left_ref.2, bf16[128,2048]{1,0:T(8,128)(2,1)} %right_ref.2), custom_call_target="tpu_custom_call" | custom-call | bytes 1048576 | tf_op jit(solution)/shard_map/pallas_call | solution.py:85
  10.0 1.2 %collective-permute-start.4 = (bf16[128,512]{1,0:T(8,128)(2,1)}, bf16[128,512]{1,0:T(8,128)(2,1)S(1)}, u32[]{:S(2)}, u32[]{:S(2)}) collective-permute-start(bf16[128,512]{1,0:T(8,128)(2,1)} %get-tuple-element.54), channel_id=1, source_target_pairs={{0,3},{1,2},{2,1},{3,0},{4,7},{5,6},{6,5},{7,4},{8,11},{9,10},{10,... | collective-permute-start | bytes 393224 | tf_op jit(solution)/shard_map/ppermute | solution.py:325
  11.2 1.8 %bitcast_bitcast_fusion = (bf16[8,128,512]{2,1,0:T(8,128)(2,1)S(1)}, bf16[8,128,512]{2,1,0:T(8,128)(2,1)S(1)}) fusion(bf16[16,8,8,512]{3,2,1,0:T(8,128)(2,1)} %bitcast.47, bf16[16,8,8,512]{3,2,1,0:T(8,128)(2,1)} %bitcast.48), kind=kLoop, calls=%fused_computation.1 | loop fusion | bytes 4194304 | tf_op jit(solution)/shard_map/transpose | solution.py:310
  13.9 1.6 %pad_maximum_fusion = bf16[8,128,1024]{2,1,0:T(8,128)(2,1)} fusion(bf16[8,128,512]{2,1,0:T(8,128)(2,1)S(1)} %get-tuple-element.94, bf16[8,128,512]{2,1,0:T(8,128)(2,1)S(1)} %get-tuple-element.95), kind=kLoop, calls=%fused_computation | loop fusion | flops 4194304 | bytes 4194304 | tf_op jit(solution)/shard_map/concatenate | solution.py:343
  15.8 2.8 %collective-permute-done.3 = bf16[128,512]{1,0:T(8,128)(2,1)} collective-permute-done((bf16[128,512]{1,0:T(8,128)(2,1)}, bf16[128,512]{1,0:T(8,128)(2,1)}, u32[]{:S(2)}, u32[]{:S(2)}) %collective-permute-start.3) | collective-permute-done | bytes 131104 | tf_op jit(solution)/shard_map/ppermute | solution.py:325
  19.4 4.5 %all-to-all-start = ((bf16[8,128,1024]{2,1,0:T(8,128)(2,1)}), bf16[8,128,1024]{2,1,0:T(8,128)(2,1)}, u32[]{:S(2)}, u32[]{:S(2)}) async-start(bf16[8,128,1024]{2,1,0:T(8,128)(2,1)} %pad_maximum_fusion), calls=%async_computation | async-start | bytes 4194304 | tf_op jit(solution)/shard_map/all_to_all | solution.py:318
  24.0 3.6 %collective-permute-start.8 = (bf16[4,128,512]{2,1,0:T(8,128)(2,1)S(1)}, bf16[4,128,512]{2,1,0:T(8,128)(2,1)S(1)}, u32[]{:S(2)}, u32[]{:S(2)}) collective-permute-start(bf16[4,128,512]{2,1,0:T(8,128)(2,1)S(1)} %pad_maximum_fusion.2.refs_1_), channel_id=1, source_target_pairs={{0,8},{8,16},{16,24},{1,9},{9,17},{17,25},{2,10},{10,18},{18,26},{... | collective-permute-start | bytes 1572872 | tf_op jit(solution)/shard_map/ppermute | solution.py:332
  27.6 1.2 %pad_maximum_fusion.1.refs_0_ = bf16[4,128,512]{2,1,0:T(8,128)(2,1)S(1)} fusion(bf16[1,128,512]{2,1,0:T(8,128)(2,1)} %bitcast.6, bf16[1,128,512]{2,1,0:T(8,128)(2,1)} %bitcast.5, bf16[1,128,512]{2,1,0:T(8,128)(2,1)} %bitcast.4, bf16[1,128,512]{2,1,0:T(8,128)(2,1)} %bitcast.3), kind=kLoop, calls=%fused_computation.7 | loop fusion | flops 786432 | bytes 1048576 | tf_op jit(solution)/shard_map/stack | solution.py:345
  28.8 4.3 %collective-permute-start.7 = (bf16[4,128,512]{2,1,0:T(8,128)(2,1)S(1)}, bf16[4,128,512]{2,1,0:T(8,128)(2,1)}, u32[]{:S(2)}, u32[]{:S(2)}) collective-permute-start(bf16[4,128,512]{2,1,0:T(8,128)(2,1)S(1)} %pad_maximum_fusion.1.refs_0_), channel_id=1, source_target_pairs={{0,8},{8,16},{16,24},{1,9},{9,17},{17,25},{2,10},{10,18},{18,26},{... | collective-permute-start | bytes 1572872 | tf_op jit(solution)/shard_map/ppermute | solution.py:332
  33.0 6.8 %collective-permute-done.8.refs_3_ = bf16[4,128,512]{2,1,0:T(8,128)(2,1)S(1)} collective-permute-done((bf16[4,128,512]{2,1,0:T(8,128)(2,1)S(1)}, bf16[4,128,512]{2,1,0:T(8,128)(2,1)S(1)}, u32[]{:S(2)}, u32[]{:S(2)}) %collective-permute-start.8) | collective-permute-done | bytes 524320 | tf_op jit(solution)/shard_map/ppermute | solution.py:332
  39.8 10.7 %collective-permute-done.7.refs_2_ = bf16[4,128,512]{2,1,0:T(8,128)(2,1)} collective-permute-done((bf16[4,128,512]{2,1,0:T(8,128)(2,1)S(1)}, bf16[4,128,512]{2,1,0:T(8,128)(2,1)}, u32[]{:S(2)}, u32[]{:S(2)}) %collective-permute-start.7) | collective-permute-done | bytes 524320 | tf_op jit(solution)/shard_map/ppermute | solution.py:332
  50.6 17.0 %shard_map.86 = (bf16[1024,1024]{1,0:T(8,128)(2,1)}, bf16[4,128,512]{2,1,0:T(8,128)(2,1)}, bf16[4,128,512]{2,1,0:T(8,128)(2,1)}, bf16[4,128,512]{2,1,0:T(8,128)(2,1)}, bf16[4,128,512]{2,1,0:T(8,128)(2,1)}) custom-call(s32[8]{0:T(128)} %lengths_ref.1, bf16[1024,1024]{1,0:T(8,128)(2,1)} %bitcast.2.rows_ref, bf16[4,128,512]{2,1,0:T(8,128)(2,1)} %copy-done.3, ...), custom_call_target="tpu_custom_call" | custom-call | flops 16106127360 | bytes 7864320 | tf_op jit(solution)/shard_map/pallas_call | solution.py:287
  67.6 3.9 %all-to-all-start.1 = ((bf16[8,128,1024]{2,1,0:T(8,128)(2,1)}), bf16[8,128,1024]{2,1,0:T(8,128)(2,1)S(1)}, u32[]{:S(2)}, u32[]{:S(2)}) async-start(bf16[8,128,1024]{2,1,0:T(8,128)(2,1)} %bitcast.44), calls=%async_computation.1 | async-start | bytes 4194304 | tf_op jit(solution)/shard_map/all_to_all | solution.py:318
  71.5 1.4 %collective-permute-start.9 = (bf16[4,128,512]{2,1,0:T(8,128)(2,1)S(1)}, bf16[4,128,512]{2,1,0:T(8,128)(2,1)S(1)}, u32[]{:S(2)}, u32[]{:S(2)}) collective-permute-start(bf16[4,128,512]{2,1,0:T(8,128)(2,1)S(1)} %copy-done.6), channel_id=1, source_target_pairs={{8,0},{16,8},{24,16},{9,1},{17,9},{25,17},{10,2},{18,10},{26,18},{... | collective-permute-start | bytes 1572872 | tf_op jit(solution)/shard_map/ppermute | solution.py:332
  72.9 1.3 %collective-permute-start.14 = (bf16[4,128,512]{2,1,0:T(8,128)(2,1)}, bf16[4,128,512]{2,1,0:T(8,128)(2,1)S(1)}, u32[]{:S(2)}, u32[]{:S(2)}) collective-permute-start(bf16[4,128,512]{2,1,0:T(8,128)(2,1)} %get-tuple-element.71), channel_id=1, source_target_pairs={{8,0},{16,8},{24,16},{9,1},{17,9},{25,17},{10,2},{18,10},{26,18},{... | collective-permute-start | bytes 1572872 | tf_op jit(solution)/shard_map/ppermute | solution.py:332
  74.2 14.7 %collective-permute-done.9 = bf16[4,128,512]{2,1,0:T(8,128)(2,1)S(1)} collective-permute-done((bf16[4,128,512]{2,1,0:T(8,128)(2,1)S(1)}, bf16[4,128,512]{2,1,0:T(8,128)(2,1)S(1)}, u32[]{:S(2)}, u32[]{:S(2)}) %collective-permute-start.9) | collective-permute-done | bytes 524320 | tf_op jit(solution)/shard_map/ppermute | solution.py:332
  89.1 2.0 %collective-permute-start.13 = (bf16[128,512]{1,0:T(8,128)(2,1)S(1)}, bf16[128,512]{1,0:T(8,128)(2,1)S(1)}, u32[]{:S(2)}, u32[]{:S(2)}) collective-permute-start(bf16[128,512]{1,0:T(8,128)(2,1)S(1)} %get-tuple-element.90), channel_id=1, source_target_pairs={{0,4},{1,5},{2,6},{3,7},{4,0},{5,1},{6,2},{7,3},{8,12},{9,13},{10,... | collective-permute-start | bytes 393224 | tf_op jit(solution)/shard_map/ppermute | solution.py:325
  91.1 1.5 %collective-permute-start.11 = (bf16[128,512]{1,0:T(8,128)(2,1)S(1)}, bf16[128,512]{1,0:T(8,128)(2,1)S(1)}, u32[]{:S(2)}, u32[]{:S(2)}) collective-permute-start(bf16[128,512]{1,0:T(8,128)(2,1)S(1)} %get-tuple-element.92), channel_id=1, source_target_pairs={{0,6},{1,7},{2,4},{3,5},{4,2},{5,3},{6,0},{7,1},{8,14},{9,15},{10,... | collective-permute-start | bytes 393224 | tf_op jit(solution)/shard_map/ppermute | solution.py:325
  92.6 1.2 %collective-permute-start.10 = (bf16[128,512]{1,0:T(8,128)(2,1)S(1)}, bf16[128,512]{1,0:T(8,128)(2,1)S(1)}, u32[]{:S(2)}, u32[]{:S(2)}) collective-permute-start(bf16[128,512]{1,0:T(8,128)(2,1)S(1)} %get-tuple-element.93), channel_id=1, source_target_pairs={{0,7},{1,6},{2,5},{3,4},{4,3},{5,2},{6,1},{7,0},{8,15},{9,14},{10,... | collective-permute-start | bytes 393224 | tf_op jit(solution)/shard_map/ppermute | solution.py:325
  93.8 6.2 %collective-permute-done.14 = bf16[4,128,512]{2,1,0:T(8,128)(2,1)S(1)} collective-permute-done((bf16[4,128,512]{2,1,0:T(8,128)(2,1)}, bf16[4,128,512]{2,1,0:T(8,128)(2,1)S(1)}, u32[]{:S(2)}, u32[]{:S(2)}) %collective-permute-start.14) | collective-permute-done | bytes 524320 | tf_op jit(solution)/shard_map/ppermute | solution.py:332
  101.7 4.7 %collective-permute-done.13.refs_3_ = bf16[128,512]{1,0:T(8,128)(2,1)S(1)} collective-permute-done((bf16[128,512]{1,0:T(8,128)(2,1)S(1)}, bf16[128,512]{1,0:T(8,128)(2,1)S(1)}, u32[]{:S(2)}, u32[]{:S(2)}) %collective-permute-start.13) | collective-permute-done | bytes 131104 | tf_op jit(solution)/shard_map/ppermute | solution.py:325
  (49 shorter events, 11.3 us)
Async XLA Ops:
  2.5 10.5 %collective-permute-start = (bf16[128,512]{1,0:T(8,128)(2,1)}, bf16[128,512]{1,0:T(8,128)(2,1)}, u32[]{:S(2)}, u32[]{:S(2)}) collective-permute-start(bf16[128,512]{1,0:T(8,128)(2,1)} %get-tuple-element.48), channel_id=1, source_target_pairs={{0,7},{1,6},{2,5},{3,4},{4,3},{5,2},{6,1},{7,0},{8,15},{9,14},{10,... | collective-permute-start | bytes 393224 | tf_op jit(solution)/shard_map/ppermute | solution.py:325
  5.9 7.9 %collective-permute-start.1 = (bf16[128,512]{1,0:T(8,128)(2,1)}, bf16[128,512]{1,0:T(8,128)(2,1)}, u32[]{:S(2)}, u32[]{:S(2)}) collective-permute-start(bf16[128,512]{1,0:T(8,128)(2,1)} %get-tuple-element.49), channel_id=1, source_target_pairs={{0,6},{1,7},{2,4},{3,5},{4,2},{5,3},{6,0},{7,1},{8,14},{9,15},{10,... | collective-permute-start | bytes 393224 | tf_op jit(solution)/shard_map/ppermute | solution.py:325
  6.5 9.3 %collective-permute-start.2 = (bf16[128,512]{1,0:T(8,128)(2,1)}, bf16[128,512]{1,0:T(8,128)(2,1)}, u32[]{:S(2)}, u32[]{:S(2)}) collective-permute-start(bf16[128,512]{1,0:T(8,128)(2,1)} %get-tuple-element.50), channel_id=1, source_target_pairs={{0,5},{1,4},{2,7},{3,6},{4,1},{5,0},{6,3},{7,2},{8,13},{9,12},{10,... | collective-permute-start | bytes 393224 | tf_op jit(solution)/shard_map/ppermute | solution.py:325
  7.9 10.8 %collective-permute-start.3 = (bf16[128,512]{1,0:T(8,128)(2,1)}, bf16[128,512]{1,0:T(8,128)(2,1)}, u32[]{:S(2)}, u32[]{:S(2)}) collective-permute-start(bf16[128,512]{1,0:T(8,128)(2,1)} %get-tuple-element.51), channel_id=1, source_target_pairs={{0,4},{1,5},{2,6},{3,7},{4,0},{5,1},{6,2},{7,3},{8,12},{9,13},{10,... | collective-permute-start | bytes 393224 | tf_op jit(solution)/shard_map/ppermute | solution.py:325
  10.0 8.7 %collective-permute-start.4 = (bf16[128,512]{1,0:T(8,128)(2,1)}, bf16[128,512]{1,0:T(8,128)(2,1)S(1)}, u32[]{:S(2)}, u32[]{:S(2)}) collective-permute-start(bf16[128,512]{1,0:T(8,128)(2,1)} %get-tuple-element.54), channel_id=1, source_target_pairs={{0,3},{1,2},{2,1},{3,0},{4,7},{5,6},{6,5},{7,4},{8,11},{9,10},{10,... | collective-permute-start | bytes 393224 | tf_op jit(solution)/shard_map/ppermute | solution.py:325
  13.0 6.4 %collective-permute-start.5 = (bf16[128,512]{1,0:T(8,128)(2,1)S(1)}, bf16[128,512]{1,0:T(8,128)(2,1)S(1)}, u32[]{:S(2)}, u32[]{:S(2)}) collective-permute-start(bf16[128,512]{1,0:T(8,128)(2,1)S(1)} %copy-done.8), channel_id=1, source_target_pairs={{0,2},{1,3},{2,0},{3,1},{4,6},{5,7},{6,4},{7,5},{8,10},{9,11},{10,... | collective-permute-start | bytes 393224 | tf_op jit(solution)/shard_map/ppermute | solution.py:325
  13.8 5.6 %collective-permute-start.6 = (bf16[128,512]{1,0:T(8,128)(2,1)S(1)}, bf16[128,512]{1,0:T(8,128)(2,1)S(1)}, u32[]{:S(2)}, u32[]{:S(2)}) collective-permute-start(bf16[128,512]{1,0:T(8,128)(2,1)S(1)} %copy-done.7), channel_id=1, source_target_pairs={{0,1},{1,0},{2,3},{3,2},{4,5},{5,4},{6,7},{7,6},{8,9},{9,8},{10,11... | collective-permute-start | bytes 393224 | tf_op jit(solution)/shard_map/ppermute | solution.py:325
  19.4 31.1 %all-to-all-start = ((bf16[8,128,1024]{2,1,0:T(8,128)(2,1)}), bf16[8,128,1024]{2,1,0:T(8,128)(2,1)}, u32[]{:S(2)}, u32[]{:S(2)}) async-start(bf16[8,128,1024]{2,1,0:T(8,128)(2,1)} %pad_maximum_fusion), calls=%async_computation | async-start | bytes 4194304 | tf_op jit(solution)/shard_map/all_to_all | solution.py:318
  24.0 26.6 %copy-start.2 = (bf16[4,128,512]{2,1,0:T(8,128)(2,1)}, bf16[4,128,512]{2,1,0:T(8,128)(2,1)S(1)}, u32[]{:S(2)}) copy-start(bf16[4,128,512]{2,1,0:T(8,128)(2,1)S(1)} %pad_maximum_fusion.2.refs_1_) | copy-start | bytes 1572868
  24.0 15.8 %collective-permute-start.8 = (bf16[4,128,512]{2,1,0:T(8,128)(2,1)S(1)}, bf16[4,128,512]{2,1,0:T(8,128)(2,1)S(1)}, u32[]{:S(2)}, u32[]{:S(2)}) collective-permute-start(bf16[4,128,512]{2,1,0:T(8,128)(2,1)S(1)} %pad_maximum_fusion.2.refs_1_), channel_id=1, source_target_pairs={{0,8},{8,16},{16,24},{1,9},{9,17},{17,25},{2,10},{10,18},{18,26},{... | collective-permute-start | bytes 1572872 | tf_op jit(solution)/shard_map/ppermute | solution.py:332
  28.8 21.8 %copy-start.3 = (bf16[4,128,512]{2,1,0:T(8,128)(2,1)}, bf16[4,128,512]{2,1,0:T(8,128)(2,1)S(1)}, u32[]{:S(2)}) copy-start(bf16[4,128,512]{2,1,0:T(8,128)(2,1)S(1)} %pad_maximum_fusion.1.refs_0_) | copy-start | bytes 1572868
  28.8 21.7 %collective-permute-start.7 = (bf16[4,128,512]{2,1,0:T(8,128)(2,1)S(1)}, bf16[4,128,512]{2,1,0:T(8,128)(2,1)}, u32[]{:S(2)}, u32[]{:S(2)}) collective-permute-start(bf16[4,128,512]{2,1,0:T(8,128)(2,1)S(1)} %pad_maximum_fusion.1.refs_0_), channel_id=1, source_target_pairs={{0,8},{8,16},{16,24},{1,9},{9,17},{17,25},{2,10},{10,18},{18,26},{... | collective-permute-start | bytes 1572872 | tf_op jit(solution)/shard_map/ppermute | solution.py:332
  67.6 21.3 %copy-start.1 = (bf16[4,128,512]{2,1,0:T(8,128)(2,1)S(1)}, bf16[4,128,512]{2,1,0:T(8,128)(2,1)}, u32[]{:S(2)}) copy-start(bf16[4,128,512]{2,1,0:T(8,128)(2,1)} %get-tuple-element.68) | copy-start | bytes 1572868
  67.6 40.7 %all-to-all-start.1 = ((bf16[8,128,1024]{2,1,0:T(8,128)(2,1)}), bf16[8,128,1024]{2,1,0:T(8,128)(2,1)S(1)}, u32[]{:S(2)}, u32[]{:S(2)}) async-start(bf16[8,128,1024]{2,1,0:T(8,128)(2,1)} %bitcast.44), calls=%async_computation.1 | async-start | bytes 4194304 | tf_op jit(solution)/shard_map/all_to_all | solution.py:318
  71.5 28.5 %copy-start = (bf16[4,128,512]{2,1,0:T(8,128)(2,1)S(1)}, bf16[4,128,512]{2,1,0:T(8,128)(2,1)}, u32[]{:S(2)}) copy-start(bf16[4,128,512]{2,1,0:T(8,128)(2,1)} %get-tuple-element.70) | copy-start | bytes 1572868
  71.5 17.4 %collective-permute-start.9 = (bf16[4,128,512]{2,1,0:T(8,128)(2,1)S(1)}, bf16[4,128,512]{2,1,0:T(8,128)(2,1)S(1)}, u32[]{:S(2)}, u32[]{:S(2)}) collective-permute-start(bf16[4,128,512]{2,1,0:T(8,128)(2,1)S(1)} %copy-done.6), channel_id=1, source_target_pairs={{8,0},{16,8},{24,16},{9,1},{17,9},{25,17},{10,2},{18,10},{26,18},{... | collective-permute-start | bytes 1572872 | tf_op jit(solution)/shard_map/ppermute | solution.py:332
  72.9 27.0 %collective-permute-start.14 = (bf16[4,128,512]{2,1,0:T(8,128)(2,1)}, bf16[4,128,512]{2,1,0:T(8,128)(2,1)S(1)}, u32[]{:S(2)}, u32[]{:S(2)}) collective-permute-start(bf16[4,128,512]{2,1,0:T(8,128)(2,1)} %get-tuple-element.71), channel_id=1, source_target_pairs={{8,0},{16,8},{24,16},{9,1},{17,9},{25,17},{10,2},{18,10},{26,18},{... | collective-permute-start | bytes 1572872 | tf_op jit(solution)/shard_map/ppermute | solution.py:332
  89.1 17.4 %collective-permute-start.13 = (bf16[128,512]{1,0:T(8,128)(2,1)S(1)}, bf16[128,512]{1,0:T(8,128)(2,1)S(1)}, u32[]{:S(2)}, u32[]{:S(2)}) collective-permute-start(bf16[128,512]{1,0:T(8,128)(2,1)S(1)} %get-tuple-element.90), channel_id=1, source_target_pairs={{0,4},{1,5},{2,6},{3,7},{4,0},{5,1},{6,2},{7,3},{8,12},{9,13},{10,... | collective-permute-start | bytes 393224 | tf_op jit(solution)/shard_map/ppermute | solution.py:325
  91.1 16.5 %collective-permute-start.12 = (bf16[128,512]{1,0:T(8,128)(2,1)S(1)}, bf16[128,512]{1,0:T(8,128)(2,1)S(1)}, u32[]{:S(2)}, u32[]{:S(2)}) collective-permute-start(bf16[128,512]{1,0:T(8,128)(2,1)S(1)} %get-tuple-element.91), channel_id=1, source_target_pairs={{0,5},{1,4},{2,7},{3,6},{4,1},{5,0},{6,3},{7,2},{8,13},{9,12},{10,... | collective-permute-start | bytes 393224 | tf_op jit(solution)/shard_map/ppermute | solution.py:325
  91.1 19.6 %collective-permute-start.11 = (bf16[128,512]{1,0:T(8,128)(2,1)S(1)}, bf16[128,512]{1,0:T(8,128)(2,1)S(1)}, u32[]{:S(2)}, u32[]{:S(2)}) collective-permute-start(bf16[128,512]{1,0:T(8,128)(2,1)S(1)} %get-tuple-element.92), channel_id=1, source_target_pairs={{0,6},{1,7},{2,4},{3,5},{4,2},{5,3},{6,0},{7,1},{8,14},{9,15},{10,... | collective-permute-start | bytes 393224 | tf_op jit(solution)/shard_map/ppermute | solution.py:325
  92.6 18.1 %collective-permute-start.10 = (bf16[128,512]{1,0:T(8,128)(2,1)S(1)}, bf16[128,512]{1,0:T(8,128)(2,1)S(1)}, u32[]{:S(2)}, u32[]{:S(2)}) collective-permute-start(bf16[128,512]{1,0:T(8,128)(2,1)S(1)} %get-tuple-element.93), channel_id=1, source_target_pairs={{0,7},{1,6},{2,5},{3,4},{4,3},{5,2},{6,1},{7,0},{8,15},{9,14},{10,... | collective-permute-start | bytes 393224 | tf_op jit(solution)/shard_map/ppermute | solution.py:325
  100.8 9.8 %collective-permute-start.17 = (bf16[128,512]{1,0:T(8,128)(2,1)}, bf16[128,512]{1,0:T(8,128)(2,1)S(1)}, u32[]{:S(2)}, u32[]{:S(2)}) collective-permute-start(bf16[128,512]{1,0:T(8,128)(2,1)} %get-tuple-element.86), channel_id=1, source_target_pairs={{0,3},{1,2},{2,1},{3,0},{4,7},{5,6},{6,5},{7,4},{8,11},{9,10},{10,... | collective-permute-start | bytes 393224 | tf_op jit(solution)/shard_map/ppermute | solution.py:325
  106.5 5.2 %collective-permute-start.16 = (bf16[128,512]{1,0:T(8,128)(2,1)}, bf16[128,512]{1,0:T(8,128)(2,1)S(1)}, u32[]{:S(2)}, u32[]{:S(2)}) collective-permute-start(bf16[128,512]{1,0:T(8,128)(2,1)} %get-tuple-element.87), channel_id=1, source_target_pairs={{0,2},{1,3},{2,0},{3,1},{4,6},{5,7},{6,4},{7,5},{8,10},{9,11},{10,... | collective-permute-start | bytes 393224 | tf_op jit(solution)/shard_map/ppermute | solution.py:325
  107.6 4.1 %collective-permute-start.15 = (bf16[128,512]{1,0:T(8,128)(2,1)S(1)}, bf16[128,512]{1,0:T(8,128)(2,1)S(1)}, u32[]{:S(2)}, u32[]{:S(2)}) collective-permute-start(bf16[128,512]{1,0:T(8,128)(2,1)S(1)} %get-tuple-element.88), channel_id=1, source_target_pairs={{0,1},{1,0},{2,3},{3,2},{4,5},{5,4},{6,7},{7,6},{8,9},{9,8},{10,11... | collective-permute-start | bytes 393224 | tf_op jit(solution)/shard_map/ppermute | solution.py:325
  (5 other events, 23.6 us)
